TPU v7x, 128 devices: a whole 4x4x4 slice. The times are simulated.
128 devices in a mesh: slab: 8 (over y, core), row: 16 (over x, z).
Axes of the slice: x: 4, y: 4, z: 4, core: 2. Of those that a mesh axis runs over, the one named last changes fastest.
Arguments:
- state_start: float32 [32, 16, 128, 128], P(None, 'slab', 'row'), may hold values from -6 to 6
- viscosity: float32 [16, 128, 128], P('slab', 'row'), may hold values from 0.5 to 2
- forcing: bfloat16 [8, 32, 16, 128, 128], P(None, None, 'slab', 'row'), may hold values from -6 to 6
- target: int32 [8, 16, 2048, 1], P('slab', 'row'), may hold values from 0 to 15; in each aligned block of 2048 rows (0 to 2047, 2048 to 4095, ..., all dimensions but the last counted through in order) at most 256 rows name the same one
Outputs:
- final_state: float32 [32, 16, 128, 128], P(None, 'slab', 'row')
- r_factor: float32 [256, 256], replicated
- basis: float32 [524288, 256], P(('slab', 'row'))
Inputs may be any that keep to these rules, and one draw needn't show every extreme that they name: `target`: at most 256 cells of one source device have the same row owner, and in every draw some source device gives exactly 256 cells to one owner.
All inputs are finite; a program needn't handle non-finite values.
Results may differ from a plain program's by a relative error of at most 0.0003.
Values sent between devices are 32-bit elements; how exact they have to be, the bound alone decides.
No kernel may reach another device: no remote copies, remote signals or barrier semaphores. Data moves between devices by JAX's collectives and lax.ppermute only.
A program may use at most 128 MiB of HBM per device.

v0:
```python
import jax
import jax.numpy as jnp
from jax import lax
from jax.sharding import PartitionSpec as P

SNAPS = 8
STEPS = 2


step_size = 0.08


def with_halo(block, sides, width):
    for axis, dim in sides:
        count = lax.axis_size(axis)
        forward = [(i, i + 1) for i in range(count - 1)]
        backward = [(target, source) for source, target in forward]
        low = lax.ppermute(
            lax.slice_in_dim(block, block.shape[dim] - width, None, axis=dim), axis, forward
        )
        high = lax.ppermute(lax.slice_in_dim(block, 0, width, axis=dim), axis, backward)
        block = jnp.concatenate([low, block, high], axis=dim)
    return block


def partner(shard, axis, distance):
    return lax.ppermute(shard, axis, [(i, i ^ 1 << distance) for i in range(lax.axis_size(axis))])


def advance(padded, visc_padded):
    center = padded[:, 1:-1, 1:-1]
    visc_mid = visc_padded[1:-1, 1:-1]
    flux_total = 0.5 * (visc_mid + visc_padded[2:, 1:-1]) * (padded[:, 2:, 1:-1] - center)
    flux_total = flux_total + 0.5 * (visc_mid + visc_padded[:-2, 1:-1]) * (
        padded[:, :-2, 1:-1] - center
    )
    flux_total = flux_total + 0.5 * (visc_mid + visc_padded[1:-1, 2:]) * (
        padded[:, 1:-1, 2:] - center
    )
    flux_total = flux_total + 0.5 * (visc_mid + visc_padded[1:-1, :-2]) * (
        padded[:, 1:-1, :-2] - center
    )
    flux_total = flux_total + 0.5 * (visc_mid + jnp.roll(visc_mid, -1, 2)) * (
        jnp.roll(center, -1, 3) - center
    )
    flux_total = flux_total + 0.5 * (visc_mid + jnp.roll(visc_mid, 1, 2)) * (
        jnp.roll(center, 1, 3) - center
    )
    return center + step_size * flux_total


def stepped(fields_now, visc_padded):
    padded = with_halo(fields_now, (("slab", 1), ("row", 2)), 1)
    return advance(padded, visc_padded)


def inner_products(left):
    return lax.dot_general(
        left,
        left,
        (((1,), (1,)), ((), ())),
        precision=lax.Precision.HIGHEST,
        preferred_element_type=jnp.float32,
    )


def factor_upper(gram_matrix):
    order_size = gram_matrix.shape[0]
    positions = jnp.arange(order_size, dtype=jnp.int32)

    def column_step(column_index, carry):
        remainder, upper_part = carry
        factor_row = lax.dynamic_slice_in_dim(remainder, column_index, 1, 0)[0]
        pivot_value = jnp.sqrt(
            lax.dynamic_index_in_dim(factor_row, column_index, 0, keepdims=False)
        )
        factor_row = jnp.where(positions >= column_index, factor_row / pivot_value, 0.0)
        remainder = remainder - factor_row[:, None] * factor_row[None, :]
        upper_part = lax.dynamic_update_slice_in_dim(
            upper_part, factor_row[None, :], column_index, 0
        )
        return (remainder, upper_part)

    start_value = (gram_matrix, jnp.zeros_like(gram_matrix))
    return lax.fori_loop(0, order_size, column_step, start_value)[1]


def invert_upper(upper_part):
    order_size = upper_part.shape[0]
    identity_rows = jnp.eye(order_size, dtype=jnp.float32)

    def back_step(turn_count, inverse_now):
        row_index = order_size - 1 - turn_count
        upper_row = lax.dynamic_slice_in_dim(upper_part, row_index, 1, 0)[0]
        unit_row = lax.dynamic_slice_in_dim(identity_rows, row_index, 1, 0)[0]
        partial_sum = jnp.dot(
            upper_row,
            inverse_now,
            precision=lax.Precision.HIGHEST,
            preferred_element_type=jnp.float32,
        )
        diagonal_value = lax.dynamic_index_in_dim(upper_row, row_index, 0, keepdims=False)
        solved_row = (unit_row - partial_sum) / diagonal_value
        return lax.dynamic_update_slice_in_dim(inverse_now, solved_row[None, :], row_index, 0)

    return lax.fori_loop(0, order_size, back_step, jnp.zeros_like(upper_part))


def on_device(state_start, viscosity, forcing, target):
    row_count = lax.axis_size("row")
    field_count = state_start.shape[0]
    cell_count = viscosity.size
    capacity = 2 * cell_count // row_count
    slot_count = row_count * capacity
    owners = target.reshape(cell_count)
    cell_ids = jnp.arange(cell_count, dtype=jnp.int32)
    ordering = jnp.argsort(owners * cell_count + cell_ids)
    matches = (owners[:, None] == jnp.arange(row_count, dtype=jnp.int32)[None, :]).astype(jnp.int32)
    owner_counts = jnp.sum(matches, axis=0)
    owner_starts = jnp.cumsum(owner_counts) - owner_counts
    slot_rank = jnp.arange(slot_count, dtype=jnp.int32) % capacity
    slot_start = jnp.repeat(owner_starts, capacity)
    slot_valid = slot_rank < jnp.repeat(owner_counts, capacity)
    position = jnp.minimum(slot_start + slot_rank, cell_count - 1)
    source_cell = jnp.take(ordering, position, axis=0)
    visc_padded = with_halo(viscosity, (("slab", 0), ("row", 1)), 1)
    fields_now = state_start
    columns = []
    for snapshot in range(SNAPS):
        fields_now = fields_now + forcing[snapshot].astype(jnp.float32)
        for substep in range(STEPS):
            fields_now = stepped(fields_now, visc_padded)
        values = fields_now.reshape(field_count, cell_count)
        columns.append(values)
    stacked = jnp.concatenate(columns, 0)
    outgoing = jnp.where(slot_valid[None, :], jnp.take(stacked, source_cell, axis=1), 0.0)
    panel_t = lax.all_to_all(outgoing, "row", split_axis=1, concat_axis=1, tiled=True)
    gram_local = inner_products(panel_t)
    summed = gram_local
    for level_bit in range(lax.axis_size("row").bit_length() - 1):
        summed = summed + partner(summed, "row", level_bit)
    for level_bit in range(lax.axis_size("slab").bit_length() - 1):
        summed = summed + partner(summed, "slab", level_bit)
    r_factor = factor_upper(summed)
    inverse_factor = invert_upper(r_factor)
    basis = lax.dot_general(
        panel_t,
        inverse_factor,
        (((0,), (0,)), ((), ())),
        precision=lax.Precision.HIGHEST,
        preferred_element_type=jnp.float32,
    )
    return (fields_now, r_factor, basis)


def solution(mesh):
    placed = (
        P(None, "slab", "row", None),
        P("slab", "row", None),
        P(None, None, "slab", "row", None),
        P("slab", "row", None, None),
    )
    return jax.shard_map(
        on_device,
        mesh=mesh,
        in_specs=placed,
        out_specs=(P(None, "slab", "row", None), P(), P(("slab", "row"), None)),
        check_vma=False,
    )
```

profile of v0, /device:TPU:64, one launch (start us, length us, event | category | flops | bytes accessed | tf_op | source)
XLA Modules:
  0.0 1284.5 jit_solution(16189157874308771270)
XLA Ops:
  19.9 23.0 %gather_fusion = s32[4096]{0:T(1024)S(1)} fusion(s32[2048]{0:T(1024)S(1)} %get-tuple-element.255, s32[4096]{0:T(1024)S(1)} %broadcast_clamp_fusion.1), kind=kCustom, calls=%fused_computation | custom fusion | bytes 49152 | tf_op jit(solution)/shard_map/jit(_take)/gather | solution.py:125
  66.7 6.2 collective-permute-start.11
  84.3 6.5 collective-permute-start.15
  103.2 6.4 collective-permute-start.19
  123.0 6.4 collective-permute-start.23
  133.0 6.1 collective-permute-start.25
  142.1 6.4 collective-permute-start.27
  161.7 6.4 collective-permute-start.31
  171.6 6.1 collective-permute-start.33
  180.7 6.4 collective-permute-start.35
  200.4 6.4 collective-permute-start.39
  210.3 6.1 collective-permute-start.41
  219.4 6.6 collective-permute-start.43
  239.0 6.4 collective-permute-start.47
  249.0 6.1 collective-permute-start.49
  258.1 6.4 collective-permute-start.51
  277.7 6.4 collective-permute-start.55
  287.6 6.2 collective-permute-start.57
  296.8 6.4 collective-permute-start.59
  316.4 6.4 collective-permute-start.63
  326.3 6.1 collective-permute-start.65
  335.4 6.4 collective-permute-start.67
  351.5 16.1 %gather_fusion.1 = f32[4096,256]{1,0:T(8,128)} fusion(f32[256,2048]{0,1:T(8,128)S(1)} %concatenate.530, s32[4096]{0:T(1024)S(1)} %broadcast_clamp_fusion), kind=kCustom, calls=%fused_computation.1 | custom fusion | bytes 8404992 | tf_op jit(solution)/shard_map/jit(_take)/gather | solution.py:136
  375.8 58.2 %all_to_all.9 = f32[256,16,256]{2,0,1:T(8,128)S(1)} all-to-all(f32[256,16,256]{2,0,1:T(8,128)S(1)} %select_select_fusion), channel_id=1, replica_groups=mesh['slab'=8,'row'=16] {'row'}, dimensions={1} | all-to-all | bytes 8388608 | tf_op jit(solution)/shard_map/all_to_all | solution.py:137
  439.0 6.7 collective-permute-done.68
  447.0 9.3 collective-permute-done.69
  456.8 8.0 collective-permute-done.70
  466.6 7.4 collective-permute-done.71
  477.0 7.0 collective-permute-done.73
  493.3 387.9 %while.36 = (s32[]{:T(128)}, f32[256,256]{1,0:T(8,128)S(1)}, f32[256,256]{1,0:T(8,128)S(1)}, s32[]{:T(128)}, s32[]{:T(128)}, /*index=5*/s32[]{:T(128)}) while((s32[]{:T(128)}, f32[256,256]{1,0:T(8,128)S(1)}, f32[256,256]{1,0:T(8,128)S(1)}, s32[]{:T(128)}, s32[]{:T(128)}, /*index=5*/s32[]{:T(128)}) %tuple.164), condition=%wide.region_4.5_spmd.clone, body=%wide.region_3.4_spmd.clone.sunk | while | flops 132355 | bytes 534141 | solution.py:85
  881.2 395.6 %while.35 = (s32[]{:T(128)}, f32[256,256]{1,0:T(8,128)S(1)}, f32[256,256]{1,0:T(8,128)S(1)}, f32[256,256]{1,0:T(8,128)S(1)}, s32[]{:T(128)}, /*index=5*/s32[]{:T(128)}, s32[]{:T(128)}, s32[]{:T(128)}) while((s32[]{:T(128)}, f32[256,256]{1,0:T(8,128)S(1)}, f32[256,256]{1,0:T(8,128)S(1)}, f32[256,256]{1,0:T(8,128)S(1)}, s32[]{:T(128)}, ...), condition=%wide.region_6.7_spmd, body=%wide.region_5.6_spmd.sunk | while | flops 786951 | bytes 271535 | solution.py:106
  1276.8 7.7 fusion.353
  (3076 shorter events, 806.3 us)
Async XLA Ops:
  1.3 41.8 %collective-permute-start.2 = (f32[1,8,128]{2,1,0:T(8,128)S(1)}, f32[1,8,128]{2,1,0:T(8,128)S(1)}, u32[]{:S(2)}, u32[]{:S(2)}) collective-permute-start(f32[1,8,128]{2,1,0:T(8,128)S(1)} %get-tuple-element.433), channel_id=1, source_target_pairs={{0,16},{16,32},{32,48},{48,64},{64,80},{80,96},{96,112},{1,17},{17... | collective-permute-start | bytes 12296 | tf_op jit(solution)/shard_map/ppermute | solution.py:18
  3.1 40.1 %collective-permute-start = (f32[1,8,128]{2,1,0:T(8,128)S(1)}, f32[1,8,128]{2,1,0:T(8,128)S(1)}, u32[]{:S(2)}, u32[]{:S(2)}) collective-permute-start(f32[1,8,128]{2,1,0:T(8,128)S(1)} %get-tuple-element.432), channel_id=1, source_target_pairs={{16,0},{32,16},{48,32},{64,48},{80,64},{96,80},{112,96},{17,1},{33... | collective-permute-start | bytes 12296 | tf_op jit(solution)/shard_map/ppermute | solution.py:21
  5.4 43.7 %collective-permute-start.1 = (f32[32,1,8,128]{3,2,1,0:T(8,128)S(1)}, f32[32,1,8,128]{3,2,1,0:T(8,128)S(1)}, u32[]{:S(2)}, u32[]{:S(2)}) collective-permute-start(f32[32,1,8,128]{3,2,1,0:T(8,128)S(1)} %get-tuple-element.423), channel_id=1, source_target_pairs={{16,0},{32,16},{48,32},{64,48},{80,64},{96,80},{112,96},{17,1},{33... | collective-permute-start | bytes 393224 | tf_op jit(solution)/shard_map/ppermute | solution.py:21
  6.7 42.4 %collective-permute-start.3 = (f32[32,1,8,128]{3,2,1,0:T(8,128)S(1)}, f32[32,1,8,128]{3,2,1,0:T(8,128)S(1)}, u32[]{:S(2)}, u32[]{:S(2)}) collective-permute-start(f32[32,1,8,128]{3,2,1,0:T(8,128)S(1)} %get-tuple-element.422), channel_id=1, source_target_pairs={{0,16},{16,32},{32,48},{48,64},{64,80},{80,96},{96,112},{1,17},{17... | collective-permute-start | bytes 393224 | tf_op jit(solution)/shard_map/ppermute | solution.py:18
  43.2 13.6 %collective-permute-start.4 = (f32[4,1,128]{2,1,0:T(1,128)S(1)}, f32[4,1,128]{2,1,0:T(1,128)S(1)}, u32[]{:S(2)}, u32[]{:S(2)}) collective-permute-start(f32[4,1,128]{2,1,0:T(1,128)S(1)} %get-tuple-element.426), channel_id=1, source_target_pairs={{1,0},{2,1},{3,2},{4,3},{5,4},{6,5},{7,6},{8,7},{9,8},{10,9},{11,1... | collective-permute-start | bytes 6152 | tf_op jit(solution)/shard_map/ppermute | solution.py:21
  45.2 11.5 collective-permute-start.6
  64.8 8.4 collective-permute-start.10
  82.3 8.9 collective-permute-start.14
  84.3 8.4 collective-permute-start.15
  101.3 8.6 collective-permute-start.18
  103.2 8.3 collective-permute-start.19
  121.1 9.8 collective-permute-start.22
  123.0 8.3 collective-permute-start.23
  140.1 8.6 collective-permute-start.26
  159.8 9.8 collective-permute-start.30
  178.8 8.6 collective-permute-start.34
  180.7 8.3 collective-permute-start.35
  198.4 9.8 collective-permute-start.38
  217.5 8.6 collective-permute-start.42
  237.1 9.8 collective-permute-start.46
  239.0 8.3 collective-permute-start.47
  256.1 8.6 collective-permute-start.50
  258.1 8.3 collective-permute-start.51
  275.8 9.8 collective-permute-start.54
  294.8 8.6 collective-permute-start.58
  314.4 9.8 collective-permute-start.62
  333.5 8.6 collective-permute-start.66
  445.7 10.7 collective-permute-start.69
  456.4 8.4 collective-permute-start.70
  464.9 9.1 collective-permute-start.71
  475.6 8.4 collective-permute-start.73
  484.1 9.1 collective-permute-start.74
  (47 other events, 347.0 us)
where the time goes:
time: 1300 us; the launch traced here: 1280 us
  local copies, waits for them, and re-layouts  407 us (31%)
  starting transfers between devices  260 us (20%)
  other arithmetic  225 us (17%)
  loops' own time  200 us (15%)
  waiting for transfers between devices  72.9 us (6%)
  matrix products  58.5 us (4%)
  blocking collectives  58.2 us (4%)
    ppermute x34, starting transfers between devices, with_halo(): lax.ppermute(lax.slice_in_dim(block, block.shape[dim] - width, None, axis...  196 us
    another operation x1, loops' own time, factor_upper(): return lax.fori_loop(0, order_size, column_step, start_value)[1]  191 us
    div x256, other arithmetic, back_step(): solved_row = (unit_row - partial_sum) / diagonal_value  166 us
    dynamic_slice x256, local copies, waits for them, and re-layouts, back_step(): lax.dynamic_index_in_dim(upper_row, row_index, 0, keepdims=False)  161 us
    dynamic_slice x256, local copies, waits for them, and re-layouts, column_step(): lax.dynamic_index_in_dim(factor_row, column_index, 0, keepdims=False)  151 us
    all_to_all x1, blocking collectives, on_device(): lax.all_to_all(outgoing, 'row', split_axis=1, concat_axis=1, tiled=True)  58.2 us
    ppermute x34, starting transfers between devices, with_halo(): lax.ppermute(lax.slice_in_dim(block, 0, width, axis=dim), axis, backward)  54.8 us
    dot_general x256, matrix products, back_step(): jnp.dot(upper_row, inverse_now, precision=lax.Precision.HIGHEST, preferre...  47.3 us
  transfers between devices with their start and end apart: 75, of which 46 were waited for; matrix products, arithmetic and copies ran while one was open for 4% of the time, Pallas kernels for 0%

commit v1 on v0

v1 whole, which is shorter than its diff:
```python
import functools

import jax
import jax.numpy as jnp
from jax import lax
from jax.experimental import pallas as pl
from jax.experimental.pallas import tpu as pltpu
from jax.sharding import Mesh, PartitionSpec as P

SNAPS = 8
STEPS = 2
HALF = SNAPS // 2
DEEP = HALF * STEPS
step_size = 0.08
F32 = jnp.float32
BF16 = jnp.bfloat16
NT = (((1,), (1,)), ((), ()))
NN = (((1,), (0,)), ((), ()))
TN = (((0,), (0,)), ((), ()))


def split(value):
    high = value.astype(BF16)
    return high, (value - high.astype(F32)).astype(BF16)


def exact_dot(left, right, dims):
    return lax.dot_general(
        left, right, dims, precision=lax.Precision.HIGHEST, preferred_element_type=F32
    )


def bf_dot(left, right, dims):
    return lax.dot_general(left, right, dims, preferred_element_type=F32)


def lane_next(value):
    return pltpu.roll(value, value.shape[-1] - 1, value.ndim - 1)


def lane_prev(value):
    return pltpu.roll(value, 1, value.ndim - 1)


def make_coefs(visc, coefs, rows):
    half = 0.5 * step_size
    slab = lax.broadcasted_iota(jnp.int32, (8, 128), 0)

    def row_body(y, carry):
        v0, v1 = visc[y, 0], visc[y, 1]
        pair = half * (v0 + v1)
        up = jnp.where(slab < 7, pltpu.roll(v0, 7, 0), 0.0)
        cross_up = half * (v1 + up)
        down = jnp.where(slab > 0, pltpu.roll(v1, 1, 0), 0.0)
        cross_down = half * (v0 + down)
        for i, v, cross in ((0, v0, cross_down), (1, v1, cross_up)):
            nxt, prv = visc[y + 1, i], visc[y - 1, i]
            z_next = half * (v + lane_next(v))
            z_prev = lane_prev(z_next)
            to_next = half * (v + nxt)
            to_prev = half * (v + prv)
            total = to_next + to_prev + pair + cross + z_next + z_prev
            inside = v > 0.0
            coefs[0, y, i] = jnp.where(inside, 1.0 - total, 0.0)
            coefs[1, y, i] = jnp.where(inside & (nxt > 0.0), to_next, 0.0)
            coefs[2, y, i] = jnp.where(inside, pair, 0.0)
            wall = (slab == 0) if i == 0 else (slab == 7)
            coefs[3, y, i] = jnp.where(inside & ~wall, cross, 0.0)
            coefs[4, y, i] = jnp.where(inside, z_next, 0.0)
            coefs[5, y, i] = jnp.where(inside, z_prev, 0.0)
        return carry

    v0, v1 = visc[0, 0], visc[0, 1]
    for i, v in ((0, v0), (1, v1)):
        nxt = visc[1, i]
        coefs[1, 0, i] = jnp.where((v > 0.0) & (nxt > 0.0), half * (v + nxt), 0.0)
    lax.fori_loop(1, rows - 1, row_body, 0)


def diffuse(source, dest, coefs, low, high):
    def row_body(y, carry):
        u0, u1 = source[y, 0], source[y, 1]
        for i, mine, other in ((0, u0, u1), (1, u1, u0)):
            cross = pltpu.roll(other, 1 if i == 0 else 7, 0)
            total = coefs[0, y, i] * mine + coefs[2, y, i] * other
            total = total + coefs[3, y, i] * cross
            total = total + coefs[1, y, i] * source[y + 1, i]
            total = total + coefs[1, y - 1, i] * source[y - 1, i]
            total = total + coefs[4, y, i] * lane_next(mine)
            total = total + coefs[5, y, i] * lane_prev(mine)
            dest[y, i] = total
        return carry

    lax.fori_loop(low, high, row_body, 0, unroll=2)


def run_steps(fields, forcing, coefs, pieces, own, snaps, records, last):
    rows = own + 2 * snaps * STEPS
    side = snaps * STEPS
    done = 0
    for k in range(snaps):
        first = fields[0]
        if k:

            def add_body(y, carry):
                first[y, 0] = first[y, 0] + forcing[k - 1, y, 0]
                first[y, 1] = first[y, 1] + forcing[k - 1, y, 1]
                return carry

            lax.fori_loop(done, rows - done, add_body, 0, unroll=2)
        for step in range(STEPS):
            done += 1
            diffuse(fields[step % 2], fields[(step + 1) % 2], coefs, done, rows - done)
        for y in range(own):
            z, j = divmod(y, 8)
            for i in range(2):
                value = first[side + y, i]
                records[pl.ds((z * snaps + k) * 16 + i * 8 + j, 8, stride=pieces * snaps * 16), :] = value
                if k == snaps - 1:
                    last[y, i] = value


def collect(main, low, high, blocks, pieces, block, store):
    for i in range(2):
        for j in range(8):
            at = block * 16 + i * 8 + j
            store(j, i, low[pl.ds(at, 8, stride=blocks * 16), :])
            store(8 + 8 * pieces + j, i, high[pl.ds(at, 8, stride=blocks * 16), :])
            for z in range(pieces):
                start = (z * blocks + block) * 16 + i * 8 + j
                store(8 + 8 * z + j, i, main[pl.ds(start, 8, stride=pieces * blocks * 16), :])


def first_kernel(pieces, snaps, edge, main, low, high, records, last, visc_out, buf0, buf1, forcing, coefs):
    own = 8 * pieces
    rows = own + 2 * snaps * STEPS
    blocks = snaps + 1
    has_low = jnp.where(edge[0] > 0, 1.0, 0.0)
    has_high = jnp.where(edge[1] > 0, 1.0, 0.0)

    def put_visc(y, i, value):
        if y < 8:
            value = value * has_low
        elif y >= 8 + own:
            value = value * has_high
        visc_out[y, i] = value

    collect(main, low, high, blocks, pieces, 0, put_visc)

    def put_start(y, i, value):
        buf0[y, i] = value

    collect(main, low, high, blocks, pieces, 1, put_start)
    for k in range(1, snaps):

        def put_force(y, i, value, k=k):
            forcing[k - 1, y, i] = value

        collect(main, low, high, blocks, pieces, k + 1, put_force)
    make_coefs(visc_out, coefs, rows)
    run_steps((buf0, buf1), forcing, coefs, pieces, own, snaps, records, last)


def second_kernel(pieces, snaps, main, low, high, start, start_low, start_high, visc, records, last, buf0, buf1, forcing, coefs):
    own = 8 * pieces
    rows = own + 2 * snaps * STEPS
    blocks = snaps

    def put_start(y, i, value):
        if y < 8:
            buf0[y, i] = value + start_low[y, i]
        elif y >= 8 + own:
            buf0[y, i] = value + start_high[y - 8 - own, i]
        else:
            buf0[y, i] = value + start[y - 8, i]

    collect(main, low, high, blocks, pieces, 0, put_start)
    for k in range(1, snaps):

        def put_force(y, i, value, k=k):
            forcing[k - 1, y, i] = value

        collect(main, low, high, blocks, pieces, k, put_force)
    make_coefs(visc, coefs, rows)
    run_steps((buf0, buf1), forcing, coefs, pieces, own, snaps, records, last)


VMEM = pl.BlockSpec(memory_space=pltpu.VMEM)
SMEM = pl.BlockSpec(memory_space=pltpu.SMEM)


def params(size=48):
    return pltpu.CompilerParams(vmem_limit_bytes=size * 1024 * 1024)


def step_scratch(rows, snaps):
    return [
        pltpu.VMEM((rows, 2, 8, 128), F32),
        pltpu.VMEM((rows, 2, 8, 128), F32),
        pltpu.VMEM((snaps - 1, rows, 2, 8, 128), F32),
        pltpu.VMEM((6, rows, 2, 8, 128), F32),
    ]


def first_half(edge, main, low, high, pieces, snaps):
    rows = 8 * pieces + 2 * snaps * STEPS
    return pl.pallas_call(
        functools.partial(first_kernel, pieces, snaps),
        out_shape=(
            jax.ShapeDtypeStruct((8 * pieces * snaps * 16, 128), F32),
            jax.ShapeDtypeStruct((8 * pieces, 2, 8, 128), F32),
            jax.ShapeDtypeStruct((rows, 2, 8, 128), F32),
        ),
        in_specs=[SMEM, VMEM, VMEM, VMEM],
        out_specs=(VMEM, VMEM, VMEM),
        scratch_shapes=step_scratch(rows, snaps),
        compiler_params=params(),
        name="diffuse_first",
    )(edge, main, low, high)


def second_half(main, low, high, start, start_low, start_high, visc, pieces, snaps):
    rows = 8 * pieces + 2 * snaps * STEPS
    return pl.pallas_call(
        functools.partial(second_kernel, pieces, snaps),
        out_shape=(
            jax.ShapeDtypeStruct((8 * pieces * snaps * 16, 128), F32),
            jax.ShapeDtypeStruct((8 * pieces, 2, 8, 128), F32),
        ),
        in_specs=[VMEM] * 7,
        out_specs=(VMEM, VMEM),
        scratch_shapes=step_scratch(rows, snaps),
        compiler_params=params(),
        name="diffuse_second",
    )(main, low, high, start, start_low, start_high, visc)


def prep_kernel(fields, snaps, count, *refs):
    rec = refs[0]
    before = refs[1 : 1 + 2 * count]
    high_out, low_out = refs[1 + 2 * count : 3 + 2 * count]
    gram = refs[3 + 2 * count]
    for cell_row in range(16):
        for s in range(snaps):
            for f in range(0, fields, 16):
                parts = [
                    rec[pl.ds(((f + g) * snaps + s) * 16 + cell_row, 8, stride=snaps * 16), :]
                    for g in (0, 8)
                ]
                high, low = split(jnp.concatenate(parts, 0))
                at = (slice(s * fields + f, s * fields + f + 16), slice(cell_row * 128, cell_row * 128 + 128))
                high_out[at] = high
                low_out[at] = low
    high, low = high_out[...], low_out[...]
    width = fields * snaps
    pairs = [(before[2 * c], before[2 * c + 1]) for c in range(count)] + [(high_out, low_out)]
    for c, (other_high, other_low) in enumerate(pairs):
        oh, ol = other_high[...], other_low[...]
        block = bf_dot(high, oh, NT) + (bf_dot(high, ol, NT) + bf_dot(low, oh, NT))
        gram[:, c * width : (c + 1) * width] = block


def prep(rec, before, fields, snaps):
    width = fields * snaps
    cells = 2048
    return pl.pallas_call(
        functools.partial(prep_kernel, fields, snaps, len(before) // 2),
        out_shape=(
            jax.ShapeDtypeStruct((width, cells), BF16),
            jax.ShapeDtypeStruct((width, cells), BF16),
            jax.ShapeDtypeStruct((width, width * (len(before) // 2 + 1)), F32),
        ),
        in_specs=[VMEM] * (1 + len(before)),
        out_specs=(VMEM,) * 3,
        compiler_params=params(),
        name="gram_blocks",
    )(rec, *before)


def rank_kernel(owner_count, owners, hot):
    own = owners[...]
    rows = own.shape[0]
    total = owner_count * rows
    stacked = jnp.concatenate(
        [jnp.where(own == o, 1.0, 0.0).astype(F32) for o in range(owner_count)], 0
    )
    ones = stacked.astype(BF16)
    before = lax.broadcasted_iota(jnp.int32, (128, 128), 0) < lax.broadcasted_iota(jnp.int32, (128, 128), 1)
    inner = bf_dot(ones, jnp.where(before, 1.0, 0.0).astype(BF16), NN)
    sums = bf_dot(ones, jnp.ones((128, 128), BF16), NN).astype(BF16)
    at = lax.broadcasted_iota(jnp.int32, (total, total), 0)
    of = lax.broadcasted_iota(jnp.int32, (total, total), 1)
    lower = (of < at) & (of // rows == at // rows)
    offset = bf_dot(jnp.where(lower, 1.0, 0.0).astype(BF16), sums, NN)
    picked = stacked * (inner + offset)
    rank = picked[0:rows]
    for o in range(1, owner_count):
        rank = rank + picked[o * rows : (o + 1) * rows]
    rank = rank.astype(jnp.int32)
    slot = lax.broadcasted_iota(jnp.int32, (hot.shape[0], 128), 0)
    for r in range(rows):
        hot[:, r * 128 : (r + 1) * 128] = jnp.where(slot == rank[r : r + 1, :], 1.0, 0.0).astype(BF16)


def rank_hot(owners, owner_count, capacity):
    return pl.pallas_call(
        functools.partial(rank_kernel, owner_count),
        out_shape=jax.ShapeDtypeStruct((capacity, owners.size), BF16),
        in_specs=[VMEM],
        out_specs=VMEM,
        compiler_params=params(),
        name="slot_ranks",
    )(owners)


GROUP = 4


def pack_kernel(owners, hot, high, low, out, picked):
    width = high.shape[0]
    base = pl.program_id(0) * GROUP
    own = owners[...]
    rows = own.shape[0]
    for part, source in enumerate((high, low)):
        for g in range(GROUP):
            mask = jnp.where(own == base + g, 1.0, 0.0)
            for r in range(rows):
                cols = slice(r * 128, (r + 1) * 128)
                keep = jnp.broadcast_to(mask[r : r + 1, :], (width, 128)).astype(BF16)
                picked[part, g * width : (g + 1) * width, cols] = source[:, cols] * keep
    sums = bf_dot(picked[0], hot[...], NT) + bf_dot(picked[1], hot[...], NT)
    for g in range(GROUP):
        out[g] = sums[g * width : (g + 1) * width]


def pack(owners, hot, high, low, owner_count):
    width, cells = high.shape
    capacity = hot.shape[0]
    return pl.pallas_call(
        pack_kernel,
        grid=(owner_count // GROUP,),
        out_shape=jax.ShapeDtypeStruct((owner_count, width, capacity), F32),
        in_specs=[VMEM] * 4,
        out_specs=pl.BlockSpec((GROUP, width, capacity), lambda g: (g, 0, 0)),
        scratch_shapes=[pltpu.VMEM((2, GROUP * width, cells), BF16)],
        compiler_params=params(),
        name="pack_slots",
    )(owners, hot, high, low)


BLOCK = 32


def factor_kernel(gram, r_out, inv_out, work):
    order = gram.shape[0]
    work[:, 0:order] = gram[...]
    eye = lax.broadcasted_iota(jnp.int32, (order, order), 0) == lax.broadcasted_iota(jnp.int32, (order, order), 1)
    work[:, order:] = jnp.where(eye, 1.0, 0.0)
    row_at = lax.broadcasted_iota(jnp.int32, (BLOCK, 128), 0)
    lane_at = lax.broadcasted_iota(jnp.int32, (BLOCK, 128), 1)
    for first in range(0, order, BLOCK):
        tile, inner = divmod(first, 128)
        tile *= 128
        on_diag = lane_at == row_at + inner
        part = work[first : first + BLOCK, tile : tile + 128]
        unit = jnp.where(on_diag, 1.0, 0.0)
        for k in range(BLOCK):
            column = part[:, inner + k : inner + k + 1]
            factor = jnp.where(row_at > k, column / part[k : k + 1, inner + k : inner + k + 1], 0.0)
            unit = unit - factor * unit[k : k + 1, :]
            part = part - factor * part[k : k + 1, :]
        pivots = jnp.sum(jnp.where(on_diag, part, 0.0), axis=1, keepdims=True)
        unit = unit / jnp.sqrt(pivots)
        solved = exact_dot(unit, work[tile : tile + 128, :], NN)
        work[first : first + BLOCK, :] = solved
        if first + BLOCK < order:
            change = exact_dot(solved[:, 0:order], solved, TN)
            work[first + BLOCK :, :] = work[first + BLOCK :, :] - change[first + BLOCK :, :]
    keep = lax.broadcasted_iota(jnp.int32, (order, order), 0) <= lax.broadcasted_iota(jnp.int32, (order, order), 1)
    r_out[...] = jnp.where(keep, work[:, 0:order], 0.0)
    inv_out[...] = work[:, order:]


def factor(gram):
    order = gram.shape[0]
    return pl.pallas_call(
        factor_kernel,
        out_shape=(jax.ShapeDtypeStruct((order, order), F32),) * 2,
        in_specs=[VMEM],
        out_specs=(VMEM,) * 2,
        scratch_shapes=[pltpu.VMEM((order, 2 * order), F32)],
        compiler_params=params(),
        name="factor_upper",
    )(gram)


def basis_kernel(inverse, *refs):
    out = refs[-1]
    panel = jnp.concatenate([ref[0] for ref in refs[:-1]], 0).T
    high, low = split(panel)
    inv_high, inv_low = split(inverse[...])
    out[...] = bf_dot(high, inv_high, NT) + (bf_dot(high, inv_low, NT) + bf_dot(low, inv_high, NT))


def basis_of(inverse, panels):
    sources, width, capacity = panels[0].shape
    order = inverse.shape[0]
    return pl.pallas_call(
        basis_kernel,
        grid=(sources,),
        out_shape=jax.ShapeDtypeStruct((sources * capacity, order), F32),
        in_specs=[pl.BlockSpec((order, order), lambda b: (0, 0))]
        + [pl.BlockSpec((1, width, capacity), lambda b: (b, 0, 0)) for _ in panels],
        out_specs=pl.BlockSpec((capacity, order), lambda b: (b, 0)),
        compiler_params=params(),
        name="basis_rows",
    )(inverse, *panels)


def ring(size, shift):
    return [(i, (i + shift) % size) for i in range(size)]


def reduced(value):
    for axis in ("slab", "z", "x"):
        size = lax.axis_size(axis)
        for level in range(size.bit_length() - 1):
            value = value + lax.ppermute(value, axis, [(i, i ^ 1 << level) for i in range(size)])
    return value


def on_device(state_start, viscosity, forcing, target):
    fields, wide, deep, lanes = state_start.shape
    x_size, pieces = lax.axis_size("x"), lax.axis_size("z")
    owner_count = x_size * pieces
    plane = ("slab", "z")
    capacity = 2 * viscosity.size // owner_count
    owners = target.reshape(wide * deep, lanes)

    def swap(value):
        return lax.all_to_all(value, plane, split_axis=0, concat_axis=0, tiled=True)

    start = state_start + forcing[0].astype(F32)
    visc_blocks = jnp.broadcast_to(viscosity[None, None], (fields, 1, wide, deep, lanes))
    later = jnp.transpose(forcing, (1, 0, 2, 3, 4))
    one = swap(jnp.concatenate([visc_blocks, start[:, None], later[:, 1:HALF].astype(F32)], 1))
    two = swap(later[:, HALF:].astype(F32))
    slabs = fields // pieces

    def edges(value):
        by_row = value.reshape((slabs, pieces) + value.shape[1:])
        low = lax.ppermute(by_row[:, pieces - 1], "x", ring(x_size, 1))
        high = lax.ppermute(by_row[:, 0], "x", ring(x_size, -1))
        return low.reshape(-1, lanes), high.reshape(-1, lanes)

    x_at = lax.axis_index("x")
    edge = jnp.stack([x_at > 0, x_at < x_size - 1]).astype(jnp.int32)
    low_one, high_one = edges(one)
    records_one, middle, visc = first_half(edge, one.reshape(-1, lanes), low_one, high_one, pieces, HALF)
    low_two, high_two = edges(two)
    middle_low = lax.ppermute(middle[-deep:], "x", ring(x_size, 1))
    middle_high = lax.ppermute(middle[:deep], "x", ring(x_size, -1))
    records_two, _ = second_half(
        two.reshape(-1, lanes), low_two, high_two, middle, middle_low, middle_high, visc, pieces, HALF
    )
    block = (fields, HALF, wide, deep, lanes)
    home_one = swap(records_one.reshape(block))
    home_two = swap(records_two.reshape(block))
    hot = rank_hot(owners, owner_count, capacity)
    high_a, low_a, gram_a = prep(home_one.reshape(-1, lanes), (), fields, HALF)
    high_b, low_b, gram_b = prep(home_two.reshape(-1, lanes), (high_a, low_a), fields, HALF)
    panels = [
        lax.all_to_all(pack(owners, hot, high, low, owner_count), ("x", "z"), split_axis=0, concat_axis=0, tiled=True)
        for high, low in ((high_a, low_a), (high_b, low_b))
    ]
    width = fields * HALF
    gram = jnp.concatenate([jnp.concatenate([gram_a, gram_b[:, :width].T], 1), gram_b], 0)
    r_factor, inverse = factor(reduced(gram))
    basis = basis_of(inverse, panels)
    return home_two[:, HALF - 1], r_factor, basis


def solution(mesh):
    slab_size, row_size = mesh.shape["slab"], mesh.shape["row"]
    z_size = 4
    cut = Mesh(mesh.devices.reshape(slab_size, row_size // z_size, z_size), ("slab", "x", "z"))
    row = ("x", "z")
    placed = (
        P(None, "slab", row, None),
        P("slab", row, None),
        P(None, None, "slab", row, None),
        P("slab", row, None, None),
    )
    return jax.shard_map(
        on_device,
        mesh=cut,
        in_specs=placed,
        out_specs=(P(None, "slab", row, None), P(), P(("slab",) + row, None)),
        check_vma=False,
    )
```

time: 1300 us -> 276 us (0.21); the launches traced: 1280 us -> 274 us
  local copies, waits for them, and re-layouts: 407 us -> 15.5 us
  other arithmetic: 225 us -> 5.27 us
  starting transfers between devices: 260 us -> 54.7 us
  loops' own time: 200 us -> 0 us
  Pallas kernels: 0 us -> 101 us
  matrix products: 58.5 us -> 0 us
  blocking collectives: 58.2 us -> 0 us
  waiting for transfers between devices: 72.9 us -> 96 us
    dynamic_slice x768 -> x0, local copies, waits for them, and re-layouts: 313 us -> none  [the longest x256 161 us: back_step(): lax.dynamic_index_in_dim(upper_row, row_index, 0, keepdims=False)]
    ppermute x75 -> x13, starting transfers between devices: 260 us -> 13.7 us  [the longest x7 6.7 us: reduced(): lax.ppermute(value, axis, [(i, i ^ 1 << level) for i in range(size)])]
    another operation x2 -> x0, loops' own time: 200 us -> none  [the longest x1 191 us: factor_upper(): return lax.fori_loop(0, order_size, column_step, start_value)[1]]
    div x256 -> x0, other arithmetic: 166 us -> none  [back_step(): solved_row = (unit_row - partial_sum) / diagonal_value]
    pallas_call x0 -> x9, Pallas kernels: none -> 101 us  [the longest x1 27.6 us: factor(): pl.pallas_call(factor_kernel, out_shape=(jax.ShapeDtypeStruct((order, ord...]
    dot_general x258 -> x0, matrix products: 58.5 us -> none  [the longest x256 47.3 us: back_step(): jnp.dot(upper_row, inverse_now, precision=lax.Precision.HIGHEST, preferre...]
    all_to_all x1 -> x0, blocking collectives: 58.2 us -> none  [on_device(): lax.all_to_all(outgoing, 'row', split_axis=1, concat_axis=1, tiled=True)]
    gather x4 -> x0, local copies, waits for them, and re-layouts: 44.6 us -> none  [the longest x2 23 us: on_device(): source_cell = jnp.take(ordering, position, axis=0)]
  transfers between devices with their start and end apart: 75 -> 19, of which waited for: 46 -> 14; matrix products, arithmetic and copies ran while one was open for 4% -> 2% of each run, Pallas kernels for 0% -> 33%
where the time goes in v1:
time: 276 us; the launch traced here: 274 us
  Pallas kernels  101 us (37%)
  waiting for transfers between devices  96 us (35%)
  starting transfers between devices  54.7 us (20%)
  local copies, waits for them, and re-layouts  15.5 us (6%)
  other arithmetic  5.27 us (2%)
    ppermute x7, waiting for transfers between devices, reduced(): lax.ppermute(value, axis, [(i, i ^ 1 << level) for i in range(size)])  45.9 us
    all_to_all x4, starting transfers between devices, swap(): return lax.all_to_all(value, plane, split_axis=0, concat_axis=0, tiled=True)  28.3 us
    pallas_call x1, Pallas kernels, factor(): pl.pallas_call(factor_kernel, out_shape=(jax.ShapeDtypeStruct((order, ord...  27.6 us
    pallas_call x1, Pallas kernels, first_half(): pl.pallas_call(functools.partial(first_kernel, pieces, snaps), out_shape=...  22.3 us
    pallas_call x1, Pallas kernels, second_half(): pl.pallas_call(functools.partial(second_kernel, pieces, snaps), out_shape...  21.8 us
    all_to_all x4, waiting for transfers between devices, swap(): return lax.all_to_all(value, plane, split_axis=0, concat_axis=0, tiled=True)  21.6 us
    pallas_call x2, Pallas kernels, pack(): pl.pallas_call(pack_kernel, grid=(owner_count // GROUP,), out_shape=jax.S...  14.2 us
    unnamed x31, local copies, waits for them, and re-layouts  12.9 us
  transfers between devices with their start and end apart: 19, of which 14 were waited for; matrix products, arithmetic and copies ran while one was open for 2% of the time, Pallas kernels for 33%

profile of v1, /device:TPU:64, one launch (start us, length us, event | category | flops | bytes accessed | tf_op | source)
XLA Modules:
  0.0 273.7 jit_solution(6939319425586981649)
XLA Ops:
  0.6 1.6 copy.27
  4.4 7.8 %all-to-all-start.1 = ((f32[32,5,2,8,128]{4,3,2,1,0:T(8,128)}), f32[32,5,2,8,128]{4,3,2,1,0:T(8,128)S(1)}, u32[]{:S(2)}, u32[]{:S(2)}) async-start(f32[32,5,2,8,128]{4,3,2,1,0:T(8,128)} %pad_maximum_fusion), calls=%async_computation.1 | async-start | bytes 2621440 | tf_op jit(solution)/shard_map/all_to_all | solution.py:441
  13.3 17.0 %all-to-all-done.1 = f32[32,5,2,8,128]{4,3,2,1,0:T(8,128)S(1)} async-done(((f32[32,5,2,8,128]{4,3,2,1,0:T(8,128)}), f32[32,5,2,8,128]{4,3,2,1,0:T(8,128)S(1)}, u32[]{:S(2)}, u32[]{:S(2)}) %all-to-all-start.1) | async-done | bytes 1310752 | tf_op jit(solution)/shard_map/all_to_all | solution.py:441
  30.3 5.6 %all-to-all-start = ((f32[32,4,2,8,128]{4,3,2,1,0:T(8,128)}), f32[32,4,2,8,128]{4,3,2,1,0:T(8,128)S(1)}, u32[]{:S(2)}, u32[]{:S(2)}) async-start(f32[32,4,2,8,128]{4,3,2,1,0:T(8,128)} %slice_convert_fusion), calls=%async_computation | async-start | bytes 2097152 | tf_op jit(solution)/shard_map/all_to_all | solution.py:441
  36.7 2.8 %collective-permute-start.3 = (f32[8,5,2,8,128]{4,3,2,1,0:T(8,128)}, f32[8,5,2,8,128]{4,3,2,1,0:T(8,128)S(1)}, u32[]{:S(2)}, u32[]{:S(2)}) collective-permute-start(f32[8,5,2,8,128]{4,3,2,1,0:T(8,128)} %get-tuple-element.27), channel_id=1, source_target_pairs={{0,12},{4,0},{8,4},{12,8},{1,13},{5,1},{9,5},{13,9},{2,14},{6,2},{... | collective-permute-start | bytes 983048 | tf_op jit(solution)/shard_map/ppermute | solution.py:453
  39.5 7.5 %collective-permute-done.3 = f32[8,5,2,8,128]{4,3,2,1,0:T(8,128)S(1)} collective-permute-done((f32[8,5,2,8,128]{4,3,2,1,0:T(8,128)}, f32[8,5,2,8,128]{4,3,2,1,0:T(8,128)S(1)}, u32[]{:S(2)}, u32[]{:S(2)}) %collective-permute-start.3) | collective-permute-done | bytes 327712 | tf_op jit(solution)/shard_map/ppermute | solution.py:453
  47.1 3.1 %collective-permute-done.2 = f32[8,5,2,8,128]{4,3,2,1,0:T(8,128)S(1)} collective-permute-done((f32[8,5,2,8,128]{4,3,2,1,0:T(8,128)S(1)}, f32[8,5,2,8,128]{4,3,2,1,0:T(8,128)S(1)}, u32[]{:S(2)}, u32[]{:S(2)}) %collective-permute-start.2) | collective-permute-done | bytes 327712 | tf_op jit(solution)/shard_map/ppermute | solution.py:452
  51.9 22.3 %diffuse_first.1 = (f32[2048,128]{1,0:T(8,128)}, f32[32,2,8,128]{3,2,1,0:T(8,128)S(1)}, f32[48,2,8,128]{3,2,1,0:T(8,128)S(1)}) custom-call(s32[2]{0:T(128)S(1)} %add_convert_fusion.edge, f32[2560,128]{1,0:T(8,128)S(1)} %bitcast.44, f32[640,128]{1,0:T(8,128)S(1)} %bitcast.50, f32[640,128]{1,0:T(8,128)S(1)} %bitcast.49), custom_call_target="tpu_custom_call" | custom-call | tf_op jit(solution)/shard_map/diffuse_first/pallas_call | solution.py:207
  74.2 7.5 %all-to-all-start.3 = ((f32[32,4,2,8,128]{4,3,2,1,0:T(8,128)}), f32[32,4,2,8,128]{4,3,2,1,0:T(8,128)S(1)}, u32[]{:S(2)}, u32[]{:S(2)}) async-start(f32[32,4,2,8,128]{4,3,2,1,0:T(8,128)} %bitcast.19), calls=%async_computation.3 | async-start | bytes 2097152 | tf_op jit(solution)/shard_map/all_to_all | solution.py:441
  82.3 1.5 collective-permute-start
  83.8 1.8 collective-permute-start.5
  85.9 4.9 %collective-permute-done.1 = f32[8,4,2,8,128]{4,3,2,1,0:T(8,128)S(1)} collective-permute-done((f32[8,4,2,8,128]{4,3,2,1,0:T(8,128)S(1)}, f32[8,4,2,8,128]{4,3,2,1,0:T(8,128)S(1)}, u32[]{:S(2)}, u32[]{:S(2)}) %collective-permute-start.1) | collective-permute-done | bytes 262176 | tf_op jit(solution)/shard_map/ppermute | solution.py:453
  92.9 21.8 %diffuse_second.1 = (f32[2048,128]{1,0:T(8,128)}, f32[32,2,8,128]{3,2,1,0:T(8,128)}) custom-call(f32[2048,128]{1,0:T(8,128)S(1)} %bitcast.46, f32[512,128]{1,0:T(8,128)S(1)} %bitcast.52, f32[512,128]{1,0:T(8,128)S(1)} %bitcast.51, f32[32,2,8,128]{3,2,1,0:T(8,128)S(1)} %get-tuple-element.15.start, f32[8,2,8,128]{3,2,1,0:T(8,128)S(1)} %collective-permute-done.4.start_low, ...), custom_call_target="tpu_custom_call" | custom-call | tf_op jit(solution)/shard_map/diffuse_second/pallas_call | solution.py:224
  114.8 7.5 %all-to-all-start.2 = ((f32[32,4,2,8,128]{4,3,2,1,0:T(8,128)}), f32[32,4,2,8,128]{4,3,2,1,0:T(8,128)S(1)}, u32[]{:S(2)}, u32[]{:S(2)}) async-start(f32[32,4,2,8,128]{4,3,2,1,0:T(8,128)} %bitcast.17), calls=%async_computation.2 | async-start | bytes 2097152 | tf_op jit(solution)/shard_map/all_to_all | solution.py:441
  124.3 7.1 %pack_slots.2 = f32[16,128,256]{2,1,0:T(8,128)} custom-call(s32[16,128]{1,0:T(8,128)S(1)} %bitcast.54, bf16[256,2048]{1,0:T(8,128)(2,1)S(1)} %slot_ranks.1.hot, bf16[128,2048]{1,0:T(8,128)(2,1)S(1)} %get-tuple-element.20.refs_1_.high, bf16[128,2048]{1,0:T(8,128)(2,1)S(1)} %get-tuple-element.21.refs_2_.low), custom_call_target="tpu_custom_call" | custom-call | tf_op jit(solution)/shard_map/pack_slots/pallas_call | solution.py:339
  133.1 4.6 %all-to-all-done.2 = f32[32,4,2,8,128]{4,3,2,1,0:T(8,128)S(1)} async-done(((f32[32,4,2,8,128]{4,3,2,1,0:T(8,128)}), f32[32,4,2,8,128]{4,3,2,1,0:T(8,128)S(1)}, u32[]{:S(2)}, u32[]{:S(2)}) %all-to-all-start.2) | async-done | bytes 1048608 | tf_op jit(solution)/shard_map/all_to_all | solution.py:441
  138.6 5.5 %all-to-all-start.4 = ((f32[16,128,256]{2,1,0:T(8,128)}), f32[16,128,256]{2,1,0:T(8,128)S(1)}, u32[]{:S(2)}, u32[]{:S(2)}) async-start(f32[16,128,256]{2,1,0:T(8,128)} %pack_slots.2), calls=%async_computation.4 | async-start | bytes 4194304 | tf_op jit(solution)/shard_map/all_to_all | solution.py:473
  147.5 1.5 gram_blocks.3
  153.6 7.1 %pack_slots.3 = f32[16,128,256]{2,1,0:T(8,128)} custom-call(s32[16,128]{1,0:T(8,128)S(1)} %bitcast.55, bf16[256,2048]{1,0:T(8,128)(2,1)S(1)} %slot_ranks.1.hot, bf16[128,2048]{1,0:T(8,128)(2,1)S(1)} %copy-done.7, bf16[128,2048]{1,0:T(8,128)(2,1)S(1)} %copy-done.9), custom_call_target="tpu_custom_call" | custom-call | tf_op jit(solution)/shard_map/pack_slots/pallas_call | solution.py:339
  160.6 10.9 %all-to-all-done.4.refs_0_ = f32[16,128,256]{2,1,0:T(8,128)S(1)} async-done(((f32[16,128,256]{2,1,0:T(8,128)}), f32[16,128,256]{2,1,0:T(8,128)S(1)}, u32[]{:S(2)}, u32[]{:S(2)}) %all-to-all-start.4) | async-done | bytes 2097184 | tf_op jit(solution)/shard_map/all_to_all | solution.py:473
  171.5 7.2 %all-to-all-start.5 = ((f32[16,128,256]{2,1,0:T(8,128)}), f32[16,128,256]{2,1,0:T(8,128)}, u32[]{:S(2)}, u32[]{:S(2)}) async-start(f32[16,128,256]{2,1,0:T(8,128)} %pack_slots.3), calls=%async_computation.5 | async-start | bytes 4194304 | tf_op jit(solution)/shard_map/all_to_all | solution.py:473
  179.7 1.5 collective-permute-start.7
  181.2 5.0 %collective-permute-done.7 = f32[256,256]{1,0:T(8,128)S(1)} collective-permute-done((f32[256,256]{1,0:T(8,128)S(1)}, f32[256,256]{1,0:T(8,128)S(1)}, u32[]{:S(2)}, u32[]{:S(2)}) %collective-permute-start.7) | collective-permute-done | bytes 262176 | tf_op jit(solution)/shard_map/ppermute | solution.py:428
  186.2 2.9 %collective-permute-start.8 = (f32[256,256]{1,0:T(8,128)S(1)}, f32[256,256]{1,0:T(8,128)S(1)}, u32[]{:S(2)}, u32[]{:S(2)}) collective-permute-start(f32[256,256]{1,0:T(8,128)S(1)} %add.26), channel_id=1, source_target_pairs={{0,64},{16,80},{32,96},{48,112},{64,0},{80,16},{96,32},{112,48},{1... | collective-permute-start | bytes 786440 | tf_op jit(solution)/shard_map/ppermute | solution.py:428
  189.1 5.1 %collective-permute-done.8 = f32[256,256]{1,0:T(8,128)S(1)} collective-permute-done((f32[256,256]{1,0:T(8,128)S(1)}, f32[256,256]{1,0:T(8,128)S(1)}, u32[]{:S(2)}, u32[]{:S(2)}) %collective-permute-start.8) | collective-permute-done | bytes 262176 | tf_op jit(solution)/shard_map/ppermute | solution.py:428
  195.5 13.2 %collective-permute-done.9 = f32[256,256]{1,0:T(8,128)S(1)} collective-permute-done((f32[256,256]{1,0:T(8,128)S(1)}, f32[256,256]{1,0:T(8,128)S(1)}, u32[]{:S(2)}, u32[]{:S(2)}) %collective-permute-start.9) | collective-permute-done | bytes 262176 | tf_op jit(solution)/shard_map/ppermute | solution.py:428
  208.8 9.7 %collective-permute-done.10 = f32[256,256]{1,0:T(8,128)S(1)} collective-permute-done((f32[256,256]{1,0:T(8,128)S(1)}, f32[256,256]{1,0:T(8,128)S(1)}, u32[]{:S(2)}, u32[]{:S(2)}) %collective-permute-start.10) | collective-permute-done | bytes 262176 | tf_op jit(solution)/shard_map/ppermute | solution.py:428
  218.7 7.4 %collective-permute-done.11 = f32[256,256]{1,0:T(8,128)S(1)} collective-permute-done((f32[256,256]{1,0:T(8,128)S(1)}, f32[256,256]{1,0:T(8,128)S(1)}, u32[]{:S(2)}, u32[]{:S(2)}) %collective-permute-start.11) | collective-permute-done | bytes 262176 | tf_op jit(solution)/shard_map/ppermute | solution.py:428
  226.9 1.7 slice_bitcast_fusion.2
  228.6 5.5 %collective-permute-done.12 = f32[256,256]{1,0:T(8,128)S(1)} collective-permute-done((f32[256,256]{1,0:T(8,128)S(1)}, f32[256,256]{1,0:T(8,128)S(1)}, u32[]{:S(2)}, u32[]{:S(2)}) %collective-permute-start.12) | collective-permute-done | bytes 262176 | tf_op jit(solution)/shard_map/ppermute | solution.py:428
  234.2 27.6 %factor_upper.1 = (f32[256,256]{1,0:T(8,128)}, f32[256,256]{1,0:T(8,128)S(1)}) custom-call(f32[256,256]{1,0:T(8,128)S(1)} %add.31.gram), custom_call_target="tpu_custom_call" | custom-call | tf_op jit(solution)/shard_map/factor_upper/pallas_call | solution.py:386
  261.7 11.9 %basis_rows.1 = f32[4096,256]{1,0:T(8,128)} custom-call(f32[256,256]{1,0:T(8,128)S(1)} %get-tuple-element.24.inverse, f32[16,128,256]{2,1,0:T(8,128)S(1)} %all-to-all-done.4.refs_0_, f32[16,128,256]{2,1,0:T(8,128)} %all-to-all-done.5.refs_1_), custom_call_target="tpu_custom_call" | custom-call | tf_op jit(solution)/shard_map/basis_rows/pallas_call | solution.py:408
  (66 shorter events, 24.9 us)
Async XLA Ops:
  0.6 1.6 copy-start.13
  2.2 1.0 copy-start.14
  4.4 25.9 %all-to-all-start.1 = ((f32[32,5,2,8,128]{4,3,2,1,0:T(8,128)}), f32[32,5,2,8,128]{4,3,2,1,0:T(8,128)S(1)}, u32[]{:S(2)}, u32[]{:S(2)}) async-start(f32[32,5,2,8,128]{4,3,2,1,0:T(8,128)} %pad_maximum_fusion), calls=%async_computation.1 | async-start | bytes 2621440 | tf_op jit(solution)/shard_map/all_to_all | solution.py:441
  30.3 43.8 %all-to-all-start = ((f32[32,4,2,8,128]{4,3,2,1,0:T(8,128)}), f32[32,4,2,8,128]{4,3,2,1,0:T(8,128)S(1)}, u32[]{:S(2)}, u32[]{:S(2)}) async-start(f32[32,4,2,8,128]{4,3,2,1,0:T(8,128)} %slice_convert_fusion), calls=%async_computation | async-start | bytes 2097152 | tf_op jit(solution)/shard_map/all_to_all | solution.py:441
  36.7 10.4 %collective-permute-start.3 = (f32[8,5,2,8,128]{4,3,2,1,0:T(8,128)}, f32[8,5,2,8,128]{4,3,2,1,0:T(8,128)S(1)}, u32[]{:S(2)}, u32[]{:S(2)}) collective-permute-start(f32[8,5,2,8,128]{4,3,2,1,0:T(8,128)} %get-tuple-element.27), channel_id=1, source_target_pairs={{0,12},{4,0},{8,4},{12,8},{1,13},{5,1},{9,5},{13,9},{2,14},{6,2},{... | collective-permute-start | bytes 983048 | tf_op jit(solution)/shard_map/ppermute | solution.py:453
  39.5 10.7 %collective-permute-start.2 = (f32[8,5,2,8,128]{4,3,2,1,0:T(8,128)S(1)}, f32[8,5,2,8,128]{4,3,2,1,0:T(8,128)S(1)}, u32[]{:S(2)}, u32[]{:S(2)}) collective-permute-start(f32[8,5,2,8,128]{4,3,2,1,0:T(8,128)S(1)} %get-tuple-element.28), channel_id=1, source_target_pairs={{0,4},{4,8},{8,12},{12,0},{1,5},{5,9},{9,13},{13,1},{2,6},{6,10},{... | collective-permute-start | bytes 983048 | tf_op jit(solution)/shard_map/ppermute | solution.py:452
  50.9 1.0 copy-start.11
  74.2 40.6 %all-to-all-start.3 = ((f32[32,4,2,8,128]{4,3,2,1,0:T(8,128)}), f32[32,4,2,8,128]{4,3,2,1,0:T(8,128)S(1)}, u32[]{:S(2)}, u32[]{:S(2)}) async-start(f32[32,4,2,8,128]{4,3,2,1,0:T(8,128)} %bitcast.19), calls=%async_computation.3 | async-start | bytes 2097152 | tf_op jit(solution)/shard_map/all_to_all | solution.py:441
  81.7 9.1 %collective-permute-start.1 = (f32[8,4,2,8,128]{4,3,2,1,0:T(8,128)S(1)}, f32[8,4,2,8,128]{4,3,2,1,0:T(8,128)S(1)}, u32[]{:S(2)}, u32[]{:S(2)}) collective-permute-start(f32[8,4,2,8,128]{4,3,2,1,0:T(8,128)S(1)} %get-tuple-element.29), channel_id=1, source_target_pairs={{0,12},{4,0},{8,4},{12,8},{1,13},{5,1},{9,5},{13,9},{2,14},{6,2},{... | collective-permute-start | bytes 786440 | tf_op jit(solution)/shard_map/ppermute | solution.py:453
  82.3 10.0 %collective-permute-start = (f32[8,4,2,8,128]{4,3,2,1,0:T(8,128)S(1)}, f32[8,4,2,8,128]{4,3,2,1,0:T(8,128)S(1)}, u32[]{:S(2)}, u32[]{:S(2)}) collective-permute-start(f32[8,4,2,8,128]{4,3,2,1,0:T(8,128)S(1)} %get-tuple-element.30), channel_id=1, source_target_pairs={{0,4},{4,8},{8,12},{12,0},{1,5},{5,9},{9,13},{13,1},{2,6},{6,10},{... | collective-permute-start | bytes 786440 | tf_op jit(solution)/shard_map/ppermute | solution.py:452
  83.8 8.5 %collective-permute-start.5 = (f32[8,2,8,128]{3,2,1,0:T(8,128)S(1)}, f32[8,2,8,128]{3,2,1,0:T(8,128)S(1)}, u32[]{:S(2)}, u32[]{:S(2)}) collective-permute-start(f32[8,2,8,128]{3,2,1,0:T(8,128)S(1)} %get-tuple-element.31), channel_id=1, source_target_pairs={{0,12},{4,0},{8,4},{12,8},{1,13},{5,1},{9,5},{13,9},{2,14},{6,2},{... | collective-permute-start | bytes 196616 | tf_op jit(solution)/shard_map/ppermute | solution.py:462
  85.6 7.4 %collective-permute-start.4 = (f32[8,2,8,128]{3,2,1,0:T(8,128)S(1)}, f32[8,2,8,128]{3,2,1,0:T(8,128)S(1)}, u32[]{:S(2)}, u32[]{:S(2)}) collective-permute-start(f32[8,2,8,128]{3,2,1,0:T(8,128)S(1)} %get-tuple-element.32), channel_id=1, source_target_pairs={{0,4},{4,8},{8,12},{12,0},{1,5},{5,9},{9,13},{13,1},{2,6},{6,10},{... | collective-permute-start | bytes 196616 | tf_op jit(solution)/shard_map/ppermute | solution.py:461
  114.8 7.5 %copy-start.12 = (s32[1,1,2048,1]{2,3,1,0:T(1,128)S(1)}, s32[1,1,2048,1]{2,3,1,0:T(1,128)}, u32[]{:S(2)}) copy-start(s32[1,1,2048,1]{2,3,1,0:T(1,128)} %param.7) | copy-start | bytes 24580
  114.8 22.9 %all-to-all-start.2 = ((f32[32,4,2,8,128]{4,3,2,1,0:T(8,128)}), f32[32,4,2,8,128]{4,3,2,1,0:T(8,128)S(1)}, u32[]{:S(2)}, u32[]{:S(2)}) async-start(f32[32,4,2,8,128]{4,3,2,1,0:T(8,128)} %bitcast.17), calls=%async_computation.2 | async-start | bytes 2097152 | tf_op jit(solution)/shard_map/all_to_all | solution.py:441
  131.4 0.8 copy-start.2
  132.2 0.8 copy-start.4
  137.6 1.0 copy-start
  138.6 32.9 %all-to-all-start.4 = ((f32[16,128,256]{2,1,0:T(8,128)}), f32[16,128,256]{2,1,0:T(8,128)S(1)}, u32[]{:S(2)}, u32[]{:S(2)}) async-start(f32[16,128,256]{2,1,0:T(8,128)} %pack_slots.2), calls=%async_computation.4 | async-start | bytes 4194304 | tf_op jit(solution)/shard_map/all_to_all | solution.py:473
  144.2 1.2 copy-start.1
  145.4 1.0 copy-start.3
  146.4 1.0 copy-start.5
  149.8 0.8 copy-start.8
  151.5 27.2 %collective-permute-start.6 = (f32[256,256]{1,0:T(8,128)}, f32[256,256]{1,0:T(8,128)}, u32[]{:S(2)}, u32[]{:S(2)}) collective-permute-start(f32[256,256]{1,0:T(8,128)} %pad_maximum_fusion.1), channel_id=1, source_target_pairs={{0,16},{16,0},{32,48},{48,32},{64,80},{80,64},{96,112},{112,96},{1... | collective-permute-start | bytes 786440 | tf_op jit(solution)/shard_map/ppermute | solution.py:428
  151.5 1.0 copy-start.7
  152.5 1.0 copy-start.9
  171.5 90.2 %all-to-all-start.5 = ((f32[16,128,256]{2,1,0:T(8,128)}), f32[16,128,256]{2,1,0:T(8,128)}, u32[]{:S(2)}, u32[]{:S(2)}) async-start(f32[16,128,256]{2,1,0:T(8,128)} %pack_slots.3), calls=%async_computation.5 | async-start | bytes 4194304 | tf_op jit(solution)/shard_map/all_to_all | solution.py:473
  179.7 6.5 %collective-permute-start.7 = (f32[256,256]{1,0:T(8,128)S(1)}, f32[256,256]{1,0:T(8,128)S(1)}, u32[]{:S(2)}, u32[]{:S(2)}) collective-permute-start(f32[256,256]{1,0:T(8,128)S(1)} %fusion.1), channel_id=1, source_target_pairs={{0,32},{16,48},{32,0},{48,16},{64,96},{80,112},{96,64},{112,80},{1... | collective-permute-start | bytes 786440 | tf_op jit(solution)/shard_map/ppermute | solution.py:428
  186.2 8.0 %collective-permute-start.8 = (f32[256,256]{1,0:T(8,128)S(1)}, f32[256,256]{1,0:T(8,128)S(1)}, u32[]{:S(2)}, u32[]{:S(2)}) collective-permute-start(f32[256,256]{1,0:T(8,128)S(1)} %add.26), channel_id=1, source_target_pairs={{0,64},{16,80},{32,96},{48,112},{64,0},{80,16},{96,32},{112,48},{1... | collective-permute-start | bytes 786440 | tf_op jit(solution)/shard_map/ppermute | solution.py:428
  194.3 14.4 %collective-permute-start.9 = (f32[256,256]{1,0:T(8,128)S(1)}, f32[256,256]{1,0:T(8,128)S(1)}, u32[]{:S(2)}, u32[]{:S(2)}) collective-permute-start(f32[256,256]{1,0:T(8,128)S(1)} %add.27), channel_id=1, source_target_pairs={{0,1},{1,0},{2,3},{3,2},{4,5},{5,4},{6,7},{7,6},{8,9},{9,8},{10,11... | collective-permute-start | bytes 786440 | tf_op jit(solution)/shard_map/ppermute | solution.py:428
  208.7 9.8 %collective-permute-start.10 = (f32[256,256]{1,0:T(8,128)S(1)}, f32[256,256]{1,0:T(8,128)S(1)}, u32[]{:S(2)}, u32[]{:S(2)}) collective-permute-start(f32[256,256]{1,0:T(8,128)S(1)} %add.28), channel_id=1, source_target_pairs={{0,2},{1,3},{2,0},{3,1},{4,6},{5,7},{6,4},{7,5},{8,10},{9,11},{10,... | collective-permute-start | bytes 786440 | tf_op jit(solution)/shard_map/ppermute | solution.py:428
  218.6 7.5 %collective-permute-start.11 = (f32[256,256]{1,0:T(8,128)S(1)}, f32[256,256]{1,0:T(8,128)S(1)}, u32[]{:S(2)}, u32[]{:S(2)}) collective-permute-start(f32[256,256]{1,0:T(8,128)S(1)} %add.29), channel_id=1, source_target_pairs={{0,4},{4,0},{8,12},{12,8},{1,5},{5,1},{9,13},{13,9},{2,6},{6,2},{1... | collective-permute-start | bytes 786440 | tf_op jit(solution)/shard_map/ppermute | solution.py:428
  226.1 8.0 %collective-permute-start.12 = (f32[256,256]{1,0:T(8,128)S(1)}, f32[256,256]{1,0:T(8,128)S(1)}, u32[]{:S(2)}, u32[]{:S(2)}) collective-permute-start(f32[256,256]{1,0:T(8,128)S(1)} %add.30), channel_id=1, source_target_pairs={{0,8},{4,12},{8,0},{12,4},{1,9},{5,13},{9,1},{13,5},{2,10},{6,14},... | collective-permute-start | bytes 786440 | tf_op jit(solution)/shard_map/ppermute | solution.py:428
  (2 other events, 1.5 us)

commit v2 on v1

--- a/solution.py
+++ b/solution.py
@@ -11,6 +11,7 @@
 STEPS = 2
 HALF = SNAPS // 2
 DEEP = HALF * STEPS
+ROWS = 8
 step_size = 0.08
 F32 = jnp.float32
 BF16 = jnp.bfloat16
@@ -74,24 +75,30 @@
     for i, v in ((0, v0), (1, v1)):
         nxt = visc[1, i]
         coefs[1, 0, i] = jnp.where((v > 0.0) & (nxt > 0.0), half * (v + nxt), 0.0)
-    lax.fori_loop(1, rows - 1, row_body, 0)
-
-
-def diffuse(source, dest, coefs, low, high):
-    def row_body(y, carry):
-        u0, u1 = source[y, 0], source[y, 1]
-        for i, mine, other in ((0, u0, u1), (1, u1, u0)):
-            cross = pltpu.roll(other, 1 if i == 0 else 7, 0)
-            total = coefs[0, y, i] * mine + coefs[2, y, i] * other
-            total = total + coefs[3, y, i] * cross
-            total = total + coefs[1, y, i] * source[y + 1, i]
-            total = total + coefs[1, y - 1, i] * source[y - 1, i]
-            total = total + coefs[4, y, i] * lane_next(mine)
-            total = total + coefs[5, y, i] * lane_prev(mine)
-            dest[y, i] = total
+    lax.fori_loop(1, rows - 1, row_body, 0, unroll=6)
+
+
+def diffuse(source, dest, coefs, low, high, plus=None):
+    def block_body(block, carry):
+        base = low + block * ROWS
+        u = [[source[base - 1 + r, i] for i in range(2)] for r in range(ROWS + 2)]
+        face = [[coefs[1, base - 1 + r, i] for i in range(2)] for r in range(ROWS + 1)]
+        for r in range(1, ROWS + 1):
+            y = base - 1 + r
+            for i in range(2):
+                mine, other = u[r][i], u[r][1 - i]
+                cross = pltpu.roll(other, 1 if i == 0 else 7, 0)
+                total = (coefs[0, y, i] * mine + coefs[2, y, i] * other) + (
+                    face[r][i] * u[r + 1][i] + face[r - 1][i] * u[r - 1][i]
+                )
+                total = total + (
+                    (coefs[4, y, i] * lane_next(mine) + coefs[5, y, i] * lane_prev(mine))
+                    + coefs[3, y, i] * cross
+                )
+                dest[y, i] = total
         return carry
 
-    lax.fori_loop(low, high, row_body, 0, unroll=2)
+    lax.fori_loop(0, (high - low + ROWS - 1) // ROWS, block_body, 0, unroll=True)
 
 
 def run_steps(fields, forcing, coefs, pieces, own, snaps, records, last):
@@ -107,7 +114,7 @@
                 first[y, 1] = first[y, 1] + forcing[k - 1, y, 1]
                 return carry
 
-            lax.fori_loop(done, rows - done, add_body, 0, unroll=2)
+            lax.fori_loop(done, rows - done, add_body, 0, unroll=4)
         for step in range(STEPS):
             done += 1
             diffuse(fields[step % 2], fields[(step + 1) % 2], coefs, done, rows - done)
@@ -194,11 +201,12 @@
 
 
 def step_scratch(rows, snaps):
+    padded = rows + ROWS
     return [
-        pltpu.VMEM((rows, 2, 8, 128), F32),
-        pltpu.VMEM((rows, 2, 8, 128), F32),
+        pltpu.VMEM((padded, 2, 8, 128), F32),
+        pltpu.VMEM((padded, 2, 8, 128), F32),
         pltpu.VMEM((snaps - 1, rows, 2, 8, 128), F32),
-        pltpu.VMEM((6, rows, 2, 8, 128), F32),
+        pltpu.VMEM((6, padded, 2, 8, 128), F32),
     ]
 
 
@@ -328,9 +336,9 @@
                 cols = slice(r * 128, (r + 1) * 128)
                 keep = jnp.broadcast_to(mask[r : r + 1, :], (width, 128)).astype(BF16)
                 picked[part, g * width : (g + 1) * width, cols] = source[:, cols] * keep
-    sums = bf_dot(picked[0], hot[...], NT) + bf_dot(picked[1], hot[...], NT)
+    sums = bf_dot(hot[...], picked[0], NT) + bf_dot(hot[...], picked[1], NT)
     for g in range(GROUP):
-        out[g] = sums[g * width : (g + 1) * width]
+        out[g] = sums[:, g * width : (g + 1) * width]
 
 
 def pack(owners, hot, high, low, owner_count):
@@ -339,9 +347,9 @@
     return pl.pallas_call(
         pack_kernel,
         grid=(owner_count // GROUP,),
-        out_shape=jax.ShapeDtypeStruct((owner_count, width, capacity), F32),
+        out_shape=jax.ShapeDtypeStruct((owner_count, capacity, width), F32),
         in_specs=[VMEM] * 4,
-        out_specs=pl.BlockSpec((GROUP, width, capacity), lambda g: (g, 0, 0)),
+        out_specs=pl.BlockSpec((GROUP, capacity, width), lambda g: (g, 0, 0)),
         scratch_shapes=[pltpu.VMEM((2, GROUP * width, cells), BF16)],
         compiler_params=params(),
         name="pack_slots",
@@ -351,11 +359,7 @@
 BLOCK = 32
 
 
-def factor_kernel(gram, r_out, inv_out, work):
-    order = gram.shape[0]
-    work[:, 0:order] = gram[...]
-    eye = lax.broadcasted_iota(jnp.int32, (order, order), 0) == lax.broadcasted_iota(jnp.int32, (order, order), 1)
-    work[:, order:] = jnp.where(eye, 1.0, 0.0)
+def eliminate(work, order):
     row_at = lax.broadcasted_iota(jnp.int32, (BLOCK, 128), 0)
     lane_at = lax.broadcasted_iota(jnp.int32, (BLOCK, 128), 1)
     for first in range(0, order, BLOCK):
@@ -366,7 +370,7 @@
         unit = jnp.where(on_diag, 1.0, 0.0)
         for k in range(BLOCK):
             column = part[:, inner + k : inner + k + 1]
-            factor = jnp.where(row_at > k, column / part[k : k + 1, inner + k : inner + k + 1], 0.0)
+            factor = jnp.where(row_at > k, column * (1.0 / part[k : k + 1, inner + k : inner + k + 1]), 0.0)
             unit = unit - factor * unit[k : k + 1, :]
             part = part - factor * part[k : k + 1, :]
         pivots = jnp.sum(jnp.where(on_diag, part, 0.0), axis=1, keepdims=True)
@@ -376,42 +380,96 @@
         if first + BLOCK < order:
             change = exact_dot(solved[:, 0:order], solved, TN)
             work[first + BLOCK :, :] = work[first + BLOCK :, :] - change[first + BLOCK :, :]
-    keep = lax.broadcasted_iota(jnp.int32, (order, order), 0) <= lax.broadcasted_iota(jnp.int32, (order, order), 1)
-    r_out[...] = jnp.where(keep, work[:, 0:order], 0.0)
+
+
+def identity(order):
+    at = lax.broadcasted_iota(jnp.int32, (order, order), 0)
+    return jnp.where(at == lax.broadcasted_iota(jnp.int32, (order, order), 1), 1.0, 0.0)
+
+
+def upper(value):
+    at = lax.broadcasted_iota(jnp.int32, value.shape, 0)
+    return jnp.where(at <= lax.broadcasted_iota(jnp.int32, value.shape, 1), value, 0.0)
+
+
+def lead_kernel(gram, r_out, inv_out, work):
+    order = gram.shape[0]
+    work[:, 0:order] = gram[...]
+    work[:, order:] = identity(order)
+    eliminate(work, order)
+    r_out[...] = upper(work[:, 0:order])
     inv_out[...] = work[:, order:]
 
 
-def factor(gram):
+def trail_kernel(gram, lead, lead_inv, r_out, inv_out, work):
+    order = lead.shape[0]
+    inverse = lead_inv[...]
+    cross = exact_dot(inverse, gram[:, 0:order], NT)
+    work[:, 0:order] = gram[:, order:] - exact_dot(cross, cross, TN)
+    work[:, order:] = identity(order)
+    eliminate(work, order)
+    zeros = jnp.zeros((order, order), F32)
+    own = work[:, order:]
+    r_out[0:order, 0:order] = lead[...]
+    r_out[0:order, order:] = cross
+    r_out[order:, 0:order] = zeros
+    r_out[order:, order:] = upper(work[:, 0:order])
+    inv_out[0:order, 0:order] = inverse
+    inv_out[0:order, order:] = zeros
+    inv_out[order:, 0:order] = -exact_dot(own, exact_dot(cross, inverse, TN), NN)
+    inv_out[order:, order:] = own
+
+
+def factor_lead(gram):
     order = gram.shape[0]
     return pl.pallas_call(
-        factor_kernel,
+        lead_kernel,
         out_shape=(jax.ShapeDtypeStruct((order, order), F32),) * 2,
         in_specs=[VMEM],
         out_specs=(VMEM,) * 2,
         scratch_shapes=[pltpu.VMEM((order, 2 * order), F32)],
         compiler_params=params(),
-        name="factor_upper",
+        name="factor_lead",
     )(gram)
+
+
+def factor_trail(gram, lead, lead_inv):
+    order = lead.shape[0]
+    return pl.pallas_call(
+        trail_kernel,
+        out_shape=(jax.ShapeDtypeStruct((2 * order, 2 * order), F32),) * 2,
+        in_specs=[VMEM] * 3,
+        out_specs=(VMEM,) * 2,
+        scratch_shapes=[pltpu.VMEM((order, 2 * order), F32)],
+        compiler_params=params(),
+        name="factor_trail",
+    )(gram, lead, lead_inv)
+
+
+SOURCES = 2
 
 
 def basis_kernel(inverse, *refs):
     out = refs[-1]
-    panel = jnp.concatenate([ref[0] for ref in refs[:-1]], 0).T
-    high, low = split(panel)
     inv_high, inv_low = split(inverse[...])
-    out[...] = bf_dot(high, inv_high, NT) + (bf_dot(high, inv_low, NT) + bf_dot(low, inv_high, NT))
+    for b in range(SOURCES):
+        high, low = split(jnp.concatenate([ref[b] for ref in refs[:-1]], 1))
+        rows = high.shape[0]
+        out[b * rows : (b + 1) * rows, :] = bf_dot(high, inv_high, NT) + (
+            bf_dot(high, inv_low, NT) + bf_dot(low, inv_high, NT)
+        )
 
 
 def basis_of(inverse, panels):
-    sources, width, capacity = panels[0].shape
+    sources, capacity, width = panels[0].shape
     order = inverse.shape[0]
     return pl.pallas_call(
         basis_kernel,
-        grid=(sources,),
+        grid=(sources // SOURCES,),
         out_shape=jax.ShapeDtypeStruct((sources * capacity, order), F32),
         in_specs=[pl.BlockSpec((order, order), lambda b: (0, 0))]
-        + [pl.BlockSpec((1, width, capacity), lambda b: (b, 0, 0)) for _ in panels],
-        out_specs=pl.BlockSpec((capacity, order), lambda b: (b, 0)),
+        + [pl.BlockSpec((SOURCES, capacity, width), lambda b: (b, 0, 0)) for _ in panels],
+        out_specs=pl.BlockSpec((SOURCES * capacity, order), lambda b: (b, 0)),
         compiler_params=params(),
         name="basis_rows",
     )(inverse, *panels)
@@ -473,9 +531,8 @@
         lax.all_to_all(pack(owners, hot, high, low, owner_count), ("x", "z"), split_axis=0, concat_axis=0, tiled=True)
         for high, low in ((high_a, low_a), (high_b, low_b))
     ]
-    width = fields * HALF
-    gram = jnp.concatenate([jnp.concatenate([gram_a, gram_b[:, :width].T], 1), gram_b], 0)
-    r_factor, inverse = factor(reduced(gram))
+    lead, lead_inv = factor_lead(reduced(gram_a))
+    r_factor, inverse = factor_trail(reduced(gram_b), lead, lead_inv)
     basis = basis_of(inverse, panels)
     return home_two[:, HALF - 1], r_factor, basis
 

time: 276 us -> 234 us (0.85)
  Pallas kernels: 101 us -> 62.1 us
  starting transfers between devices: 54.7 us -> 64.4 us
  waiting for transfers between devices: 96 us -> 87.6 us
  local copies, waits for them, and re-layouts: 15.5 us -> 11.7 us
    pallas_call x1, Pallas kernels: 22.3 us -> 6.3 us  [first_half(): pl.pallas_call(functools.partial(first_kernel, pieces, snaps), out_shape=...]
    pallas_call x1, Pallas kernels: 21.8 us -> 5.82 us  [second_half(): pl.pallas_call(functools.partial(second_kernel, pieces, snaps), out_shape...]
    ppermute x7 -> x14, waiting for transfers between devices: 45.9 us -> 31.3 us  [reduced(): lax.ppermute(value, axis, [(i, i ^ 1 << level) for i in range(size)])]
    ppermute x7 -> x14, starting transfers between devices: 6.7 us -> 16.4 us  [reduced(): lax.ppermute(value, axis, [(i, i ^ 1 << level) for i in range(size)])]
    pallas_call x2 -> x3, Pallas kernels: 39.5 us -> 33.8 us  [the longest x1 14 us: factor_trail(): pl.pallas_call(trail_kernel, out_shape=(jax.ShapeDtypeStruct((2 * order,...]
    all_to_all x2, waiting for transfers between devices: 10.9 us -> 16.2 us  [on_device(): lax.all_to_all(pack(owners, hot, high, low, owner_count), ('x', 'z'), spl...]
    unnamed x31 -> x23, local copies, waits for them, and re-layouts: 12.9 us -> 9.2 us
  transfers between devices with their start and end apart: 19 -> 26, of which waited for: 14 -> 17; matrix products, arithmetic and copies ran while one was open for 2% -> 2% of each run, Pallas kernels for 33% -> 24%
where the time goes in v2:
time: 234 us; the launch traced here: 230 us
  waiting for transfers between devices  87.6 us (37%)
  starting transfers between devices  64.4 us (28%)
  Pallas kernels  62.1 us (27%)
  local copies, waits for them, and re-layouts  11.7 us (5%)
  other arithmetic  3.52 us (2%)
    ppermute x14, waiting for transfers between devices, reduced(): lax.ppermute(value, axis, [(i, i ^ 1 << level) for i in range(size)])  31.3 us
    all_to_all x4, starting transfers between devices, swap(): return lax.all_to_all(value, plane, split_axis=0, concat_axis=0, tiled=True)  28.3 us
    all_to_all x4, waiting for transfers between devices, swap(): return lax.all_to_all(value, plane, split_axis=0, concat_axis=0, tiled=True)  22.4 us
    ppermute x14, starting transfers between devices, reduced(): lax.ppermute(value, axis, [(i, i ^ 1 << level) for i in range(size)])  16.4 us
    all_to_all x2, waiting for transfers between devices, on_device(): lax.all_to_all(pack(owners, hot, high, low, owner_count), ('x', 'z'), spl...  16.2 us
    pallas_call x1, Pallas kernels, factor_trail(): pl.pallas_call(trail_kernel, out_shape=(jax.ShapeDtypeStruct((2 * order,...  14 us
    all_to_all x2, starting transfers between devices, on_device(): lax.all_to_all(pack(owners, hot, high, low, owner_count), ('x', 'z'), spl...  12.7 us
    pallas_call x2, Pallas kernels, pack(): pl.pallas_call(pack_kernel, grid=(owner_count // GROUP,), out_shape=jax.S...  12.6 us
  transfers between devices with their start and end apart: 26, of which 17 were waited for; matrix products, arithmetic and copies ran while one was open for 2% of the time, Pallas kernels for 24%

profile of v2, /device:TPU:64, one launch (start us, length us, event | category | flops | bytes accessed | tf_op | source)
XLA Modules:
  0.0 230.3 jit_solution(4675121352054007516)
XLA Ops:
  4.4 7.8 %all-to-all-start.1 = ((f32[32,5,2,8,128]{4,3,2,1,0:T(8,128)}), f32[32,5,2,8,128]{4,3,2,1,0:T(8,128)S(1)}, u32[]{:S(2)}, u32[]{:S(2)}) async-start(f32[32,5,2,8,128]{4,3,2,1,0:T(8,128)} %pad_maximum_fusion), calls=%async_computation.1 | async-start | bytes 2621440 | tf_op jit(solution)/shard_map/all_to_all | solution.py:499
  13.3 17.0 %all-to-all-done.1 = f32[32,5,2,8,128]{4,3,2,1,0:T(8,128)S(1)} async-done(((f32[32,5,2,8,128]{4,3,2,1,0:T(8,128)}), f32[32,5,2,8,128]{4,3,2,1,0:T(8,128)S(1)}, u32[]{:S(2)}, u32[]{:S(2)}) %all-to-all-start.1) | async-done | bytes 1310752 | tf_op jit(solution)/shard_map/all_to_all | solution.py:499
  30.3 5.6 %all-to-all-start = ((f32[32,4,2,8,128]{4,3,2,1,0:T(8,128)}), f32[32,4,2,8,128]{4,3,2,1,0:T(8,128)S(1)}, u32[]{:S(2)}, u32[]{:S(2)}) async-start(f32[32,4,2,8,128]{4,3,2,1,0:T(8,128)} %slice_convert_fusion), calls=%async_computation | async-start | bytes 2097152 | tf_op jit(solution)/shard_map/all_to_all | solution.py:499
  36.7 2.8 %collective-permute-start.3 = (f32[8,5,2,8,128]{4,3,2,1,0:T(8,128)}, f32[8,5,2,8,128]{4,3,2,1,0:T(8,128)S(1)}, u32[]{:S(2)}, u32[]{:S(2)}) collective-permute-start(f32[8,5,2,8,128]{4,3,2,1,0:T(8,128)} %get-tuple-element.31), channel_id=1, source_target_pairs={{0,12},{4,0},{8,4},{12,8},{1,13},{5,1},{9,5},{13,9},{2,14},{6,2},{... | collective-permute-start | bytes 983048 | tf_op jit(solution)/shard_map/ppermute | solution.py:511
  39.5 7.5 %collective-permute-done.3 = f32[8,5,2,8,128]{4,3,2,1,0:T(8,128)S(1)} collective-permute-done((f32[8,5,2,8,128]{4,3,2,1,0:T(8,128)}, f32[8,5,2,8,128]{4,3,2,1,0:T(8,128)S(1)}, u32[]{:S(2)}, u32[]{:S(2)}) %collective-permute-start.3) | collective-permute-done | bytes 327712 | tf_op jit(solution)/shard_map/ppermute | solution.py:511
  47.1 3.1 %collective-permute-done.2 = f32[8,5,2,8,128]{4,3,2,1,0:T(8,128)S(1)} collective-permute-done((f32[8,5,2,8,128]{4,3,2,1,0:T(8,128)S(1)}, f32[8,5,2,8,128]{4,3,2,1,0:T(8,128)S(1)}, u32[]{:S(2)}, u32[]{:S(2)}) %collective-permute-start.2) | collective-permute-done | bytes 327712 | tf_op jit(solution)/shard_map/ppermute | solution.py:510
  51.9 6.3 %diffuse_first.1 = (f32[2048,128]{1,0:T(8,128)}, f32[32,2,8,128]{3,2,1,0:T(8,128)S(1)}, f32[48,2,8,128]{3,2,1,0:T(8,128)S(1)}) custom-call(s32[2]{0:T(128)S(1)} %add_convert_fusion.edge, f32[2560,128]{1,0:T(8,128)S(1)} %bitcast.42, f32[640,128]{1,0:T(8,128)S(1)} %bitcast.48, f32[640,128]{1,0:T(8,128)S(1)} %bitcast.47), custom_call_target="tpu_custom_call" | custom-call | tf_op jit(solution)/shard_map/diffuse_first/pallas_call | solution.py:215
  58.2 7.5 %all-to-all-start.3 = ((f32[32,4,2,8,128]{4,3,2,1,0:T(8,128)}), f32[32,4,2,8,128]{4,3,2,1,0:T(8,128)S(1)}, u32[]{:S(2)}, u32[]{:S(2)}) async-start(f32[32,4,2,8,128]{4,3,2,1,0:T(8,128)} %bitcast.20), calls=%async_computation.3 | async-start | bytes 2097152 | tf_op jit(solution)/shard_map/all_to_all | solution.py:499
  67.8 1.8 collective-permute-start.5
  69.9 4.9 %collective-permute-done.1 = f32[8,4,2,8,128]{4,3,2,1,0:T(8,128)S(1)} collective-permute-done((f32[8,4,2,8,128]{4,3,2,1,0:T(8,128)S(1)}, f32[8,4,2,8,128]{4,3,2,1,0:T(8,128)S(1)}, u32[]{:S(2)}, u32[]{:S(2)}) %collective-permute-start.1) | collective-permute-done | bytes 262176 | tf_op jit(solution)/shard_map/ppermute | solution.py:511
  77.0 5.8 %diffuse_second.1 = (f32[2048,128]{1,0:T(8,128)}, f32[32,2,8,128]{3,2,1,0:T(8,128)}) custom-call(f32[2048,128]{1,0:T(8,128)S(1)} %bitcast.44, f32[512,128]{1,0:T(8,128)S(1)} %bitcast.50, f32[512,128]{1,0:T(8,128)S(1)} %bitcast.49, f32[32,2,8,128]{3,2,1,0:T(8,128)S(1)} %get-tuple-element.17.start, f32[8,2,8,128]{3,2,1,0:T(8,128)S(1)} %collective-permute-done.4.start_low, ...), custom_call_target="tpu_custom_call" | custom-call | tf_op jit(solution)/shard_map/diffuse_second/pallas_call | solution.py:232
  82.8 7.5 %all-to-all-start.2 = ((f32[32,4,2,8,128]{4,3,2,1,0:T(8,128)}), f32[32,4,2,8,128]{4,3,2,1,0:T(8,128)S(1)}, u32[]{:S(2)}, u32[]{:S(2)}) async-start(f32[32,4,2,8,128]{4,3,2,1,0:T(8,128)} %bitcast.17), calls=%async_computation.2 | async-start | bytes 2097152 | tf_op jit(solution)/shard_map/all_to_all | solution.py:499
  92.4 6.3 %pack_slots.2 = f32[16,256,128]{2,1,0:T(8,128)} custom-call(s32[16,128]{1,0:T(8,128)S(1)} %bitcast.52, bf16[256,2048]{1,0:T(8,128)(2,1)S(1)} %slot_ranks.1.hot, bf16[128,2048]{1,0:T(8,128)(2,1)S(1)} %get-tuple-element.21.refs_1_.high, bf16[128,2048]{1,0:T(8,128)(2,1)S(1)} %get-tuple-element.22.refs_2_.low), custom_call_target="tpu_custom_call" | custom-call | tf_op jit(solution)/shard_map/pack_slots/pallas_call | solution.py:347
  100.3 5.4 %all-to-all-done.2 = f32[32,4,2,8,128]{4,3,2,1,0:T(8,128)S(1)} async-done(((f32[32,4,2,8,128]{4,3,2,1,0:T(8,128)}), f32[32,4,2,8,128]{4,3,2,1,0:T(8,128)S(1)}, u32[]{:S(2)}, u32[]{:S(2)}) %all-to-all-start.2) | async-done | bytes 1048608 | tf_op jit(solution)/shard_map/all_to_all | solution.py:499
  106.7 5.5 %all-to-all-start.4 = ((f32[16,256,128]{2,1,0:T(8,128)}), f32[16,256,128]{2,1,0:T(8,128)S(1)}, u32[]{:S(2)}, u32[]{:S(2)}) async-start(f32[16,256,128]{2,1,0:T(8,128)} %pack_slots.2), calls=%async_computation.4 | async-start | bytes 4194304 | tf_op jit(solution)/shard_map/all_to_all | solution.py:531
  117.0 6.3 %pack_slots.3 = f32[16,256,128]{2,1,0:T(8,128)} custom-call(s32[16,128]{1,0:T(8,128)S(1)} %bitcast.53, bf16[256,2048]{1,0:T(8,128)(2,1)S(1)} %slot_ranks.1.hot, bf16[128,2048]{1,0:T(8,128)(2,1)S(1)} %get-tuple-element.29.high, bf16[128,2048]{1,0:T(8,128)(2,1)S(1)} %get-tuple-element.30.low), custom_call_target="tpu_custom_call" | custom-call | tf_op jit(solution)/shard_map/pack_slots/pallas_call | solution.py:347
  123.3 16.2 %all-to-all-done.4.refs_0_ = f32[16,256,128]{2,1,0:T(8,128)S(1)} async-done(((f32[16,256,128]{2,1,0:T(8,128)}), f32[16,256,128]{2,1,0:T(8,128)S(1)}, u32[]{:S(2)}, u32[]{:S(2)}) %all-to-all-start.4) | async-done | bytes 2097184 | tf_op jit(solution)/shard_map/all_to_all | solution.py:531
  139.5 7.2 %all-to-all-start.5 = ((f32[16,256,128]{2,1,0:T(8,128)}), f32[16,256,128]{2,1,0:T(8,128)}, u32[]{:S(2)}, u32[]{:S(2)}) async-start(f32[16,256,128]{2,1,0:T(8,128)} %pack_slots.3), calls=%async_computation.5 | async-start | bytes 4194304 | tf_op jit(solution)/shard_map/all_to_all | solution.py:531
  149.6 4.1 %collective-permute-done.7 = f32[128,256]{1,0:T(8,128)S(1)} collective-permute-done((f32[128,256]{1,0:T(8,128)S(1)}, f32[128,256]{1,0:T(8,128)S(1)}, u32[]{:S(2)}, u32[]{:S(2)}) %collective-permute-start.7) | collective-permute-done | bytes 131104 | tf_op jit(solution)/shard_map/ppermute | solution.py:486
  153.7 2.2 collective-permute-start.8
  155.9 4.4 %collective-permute-done.8 = f32[128,256]{1,0:T(8,128)S(1)} collective-permute-done((f32[128,256]{1,0:T(8,128)S(1)}, f32[128,256]{1,0:T(8,128)S(1)}, u32[]{:S(2)}, u32[]{:S(2)}) %collective-permute-start.8) | collective-permute-done | bytes 131104 | tf_op jit(solution)/shard_map/ppermute | solution.py:486
  163.0 2.9 %collective-permute-done.14 = f32[128,128]{1,0:T(8,128)S(1)} collective-permute-done((f32[128,128]{1,0:T(8,128)S(1)}, f32[128,128]{1,0:T(8,128)S(1)}, u32[]{:S(2)}, u32[]{:S(2)}) %collective-permute-start.14) | collective-permute-done | bytes 65568 | tf_op jit(solution)/shard_map/ppermute | solution.py:486
  165.9 2.2 collective-permute-start.15
  168.1 5.7 %collective-permute-done.9 = f32[128,256]{1,0:T(8,128)S(1)} collective-permute-done((f32[128,256]{1,0:T(8,128)S(1)}, f32[128,256]{1,0:T(8,128)S(1)}, u32[]{:S(2)}, u32[]{:S(2)}) %collective-permute-start.9) | collective-permute-done | bytes 131104 | tf_op jit(solution)/shard_map/ppermute | solution.py:486
  174.9 5.0 %collective-permute-done.16 = f32[128,128]{1,0:T(8,128)S(1)} collective-permute-done((f32[128,128]{1,0:T(8,128)S(1)}, f32[128,128]{1,0:T(8,128)S(1)}, u32[]{:S(2)}, u32[]{:S(2)}) %collective-permute-start.16) | collective-permute-done | bytes 65568 | tf_op jit(solution)/shard_map/ppermute | solution.py:486
  179.9 2.7 %collective-permute-start.17 = (f32[128,128]{1,0:T(8,128)S(1)}, f32[128,128]{1,0:T(8,128)S(1)}, u32[]{:S(2)}, u32[]{:S(2)}) collective-permute-start(f32[128,128]{1,0:T(8,128)S(1)} %add.56), channel_id=1, source_target_pairs={{0,2},{1,3},{2,0},{3,1},{4,6},{5,7},{6,4},{7,5},{8,10},{9,11},{10,... | collective-permute-start | bytes 196616 | tf_op jit(solution)/shard_map/ppermute | solution.py:486
  182.7 3.0 %collective-permute-done.17 = f32[128,128]{1,0:T(8,128)S(1)} collective-permute-done((f32[128,128]{1,0:T(8,128)S(1)}, f32[128,128]{1,0:T(8,128)S(1)}, u32[]{:S(2)}, u32[]{:S(2)}) %collective-permute-start.17) | collective-permute-done | bytes 65568 | tf_op jit(solution)/shard_map/ppermute | solution.py:486
  185.8 4.7 %collective-permute-done.18 = f32[128,128]{1,0:T(8,128)S(1)} collective-permute-done((f32[128,128]{1,0:T(8,128)S(1)}, f32[128,128]{1,0:T(8,128)S(1)}, u32[]{:S(2)}, u32[]{:S(2)}) %collective-permute-start.18) | collective-permute-done | bytes 65568 | tf_op jit(solution)/shard_map/ppermute | solution.py:486
  191.5 3.0 %collective-permute-start.12 = (f32[128,256]{1,0:T(8,128)S(1)}, f32[128,256]{1,0:T(8,128)S(1)}, u32[]{:S(2)}, u32[]{:S(2)}) collective-permute-start(f32[128,256]{1,0:T(8,128)S(1)} %add.51), channel_id=1, source_target_pairs={{0,8},{4,12},{8,0},{12,4},{1,9},{5,13},{9,1},{13,5},{2,10},{6,14},... | collective-permute-start | bytes 393224 | tf_op jit(solution)/shard_map/ppermute | solution.py:486
  196.4 12.4 %factor_lead.1 = (f32[128,128]{1,0:T(8,128)S(1)}, f32[128,128]{1,0:T(8,128)S(1)}) custom-call(f32[128,128]{1,0:T(8,128)S(1)} %add.59.gram), custom_call_target="tpu_custom_call" | custom-call | tf_op jit(solution)/shard_map/factor_lead/pallas_call | solution.py:425
  208.8 14.0 %factor_trail.1 = (f32[256,256]{1,0:T(8,128)}, f32[256,256]{1,0:T(8,128)S(1)}) custom-call(f32[128,256]{1,0:T(8,128)S(1)} %add.52.gram, f32[128,128]{1,0:T(8,128)S(1)} %get-tuple-element.25.lead, f32[128,128]{1,0:T(8,128)S(1)} %get-tuple-element.26.lead_inv), custom_call_target="tpu_custom_call" | custom-call | tf_op jit(solution)/shard_map/factor_trail/pallas_call | solution.py:438
  222.8 7.5 %basis_rows.1 = f32[4096,256]{1,0:T(8,128)} custom-call(f32[256,256]{1,0:T(8,128)S(1)} %get-tuple-element.28.inverse, f32[16,256,128]{2,1,0:T(8,128)S(1)} %all-to-all-done.4.refs_0_, f32[16,256,128]{2,1,0:T(8,128)} %all-to-all-done.5.refs_1_), custom_call_target="tpu_custom_call" | custom-call | tf_op jit(solution)/shard_map/basis_rows/pallas_call | solution.py:466
  (77 shorter events, 31.4 us)
Async XLA Ops:
  0.6 1.6 copy-start.9
  2.2 1.0 copy-start.10
  4.4 25.9 %all-to-all-start.1 = ((f32[32,5,2,8,128]{4,3,2,1,0:T(8,128)}), f32[32,5,2,8,128]{4,3,2,1,0:T(8,128)S(1)}, u32[]{:S(2)}, u32[]{:S(2)}) async-start(f32[32,5,2,8,128]{4,3,2,1,0:T(8,128)} %pad_maximum_fusion), calls=%async_computation.1 | async-start | bytes 2621440 | tf_op jit(solution)/shard_map/all_to_all | solution.py:499
  30.3 27.8 %all-to-all-start = ((f32[32,4,2,8,128]{4,3,2,1,0:T(8,128)}), f32[32,4,2,8,128]{4,3,2,1,0:T(8,128)S(1)}, u32[]{:S(2)}, u32[]{:S(2)}) async-start(f32[32,4,2,8,128]{4,3,2,1,0:T(8,128)} %slice_convert_fusion), calls=%async_computation | async-start | bytes 2097152 | tf_op jit(solution)/shard_map/all_to_all | solution.py:499
  36.7 10.4 %collective-permute-start.3 = (f32[8,5,2,8,128]{4,3,2,1,0:T(8,128)}, f32[8,5,2,8,128]{4,3,2,1,0:T(8,128)S(1)}, u32[]{:S(2)}, u32[]{:S(2)}) collective-permute-start(f32[8,5,2,8,128]{4,3,2,1,0:T(8,128)} %get-tuple-element.31), channel_id=1, source_target_pairs={{0,12},{4,0},{8,4},{12,8},{1,13},{5,1},{9,5},{13,9},{2,14},{6,2},{... | collective-permute-start | bytes 983048 | tf_op jit(solution)/shard_map/ppermute | solution.py:511
  39.5 10.7 %collective-permute-start.2 = (f32[8,5,2,8,128]{4,3,2,1,0:T(8,128)S(1)}, f32[8,5,2,8,128]{4,3,2,1,0:T(8,128)S(1)}, u32[]{:S(2)}, u32[]{:S(2)}) collective-permute-start(f32[8,5,2,8,128]{4,3,2,1,0:T(8,128)S(1)} %get-tuple-element.32), channel_id=1, source_target_pairs={{0,4},{4,8},{8,12},{12,0},{1,5},{5,9},{9,13},{13,1},{2,6},{6,10},{... | collective-permute-start | bytes 983048 | tf_op jit(solution)/shard_map/ppermute | solution.py:510
  58.2 24.6 %all-to-all-start.3 = ((f32[32,4,2,8,128]{4,3,2,1,0:T(8,128)}), f32[32,4,2,8,128]{4,3,2,1,0:T(8,128)S(1)}, u32[]{:S(2)}, u32[]{:S(2)}) async-start(f32[32,4,2,8,128]{4,3,2,1,0:T(8,128)} %bitcast.20), calls=%async_computation.3 | async-start | bytes 2097152 | tf_op jit(solution)/shard_map/all_to_all | solution.py:499
  65.7 9.1 %collective-permute-start.1 = (f32[8,4,2,8,128]{4,3,2,1,0:T(8,128)S(1)}, f32[8,4,2,8,128]{4,3,2,1,0:T(8,128)S(1)}, u32[]{:S(2)}, u32[]{:S(2)}) collective-permute-start(f32[8,4,2,8,128]{4,3,2,1,0:T(8,128)S(1)} %get-tuple-element.33), channel_id=1, source_target_pairs={{0,12},{4,0},{8,4},{12,8},{1,13},{5,1},{9,5},{13,9},{2,14},{6,2},{... | collective-permute-start | bytes 786440 | tf_op jit(solution)/shard_map/ppermute | solution.py:511
  66.3 10.0 %collective-permute-start = (f32[8,4,2,8,128]{4,3,2,1,0:T(8,128)S(1)}, f32[8,4,2,8,128]{4,3,2,1,0:T(8,128)S(1)}, u32[]{:S(2)}, u32[]{:S(2)}) collective-permute-start(f32[8,4,2,8,128]{4,3,2,1,0:T(8,128)S(1)} %get-tuple-element.34), channel_id=1, source_target_pairs={{0,4},{4,8},{8,12},{12,0},{1,5},{5,9},{9,13},{13,1},{2,6},{6,10},{... | collective-permute-start | bytes 786440 | tf_op jit(solution)/shard_map/ppermute | solution.py:510
  67.8 8.5 %collective-permute-start.5 = (f32[8,2,8,128]{3,2,1,0:T(8,128)S(1)}, f32[8,2,8,128]{3,2,1,0:T(8,128)S(1)}, u32[]{:S(2)}, u32[]{:S(2)}) collective-permute-start(f32[8,2,8,128]{3,2,1,0:T(8,128)S(1)} %get-tuple-element.35), channel_id=1, source_target_pairs={{0,12},{4,0},{8,4},{12,8},{1,13},{5,1},{9,5},{13,9},{2,14},{6,2},{... | collective-permute-start | bytes 196616 | tf_op jit(solution)/shard_map/ppermute | solution.py:520
  69.6 7.4 %collective-permute-start.4 = (f32[8,2,8,128]{3,2,1,0:T(8,128)S(1)}, f32[8,2,8,128]{3,2,1,0:T(8,128)S(1)}, u32[]{:S(2)}, u32[]{:S(2)}) collective-permute-start(f32[8,2,8,128]{3,2,1,0:T(8,128)S(1)} %get-tuple-element.36), channel_id=1, source_target_pairs={{0,4},{4,8},{8,12},{12,0},{1,5},{5,9},{9,13},{13,1},{2,6},{6,10},{... | collective-permute-start | bytes 196616 | tf_op jit(solution)/shard_map/ppermute | solution.py:519
  82.8 7.5 %copy-start.8 = (s32[1,1,2048,1]{2,3,1,0:T(1,128)S(1)}, s32[1,1,2048,1]{2,3,1,0:T(1,128)}, u32[]{:S(2)}) copy-start(s32[1,1,2048,1]{2,3,1,0:T(1,128)} %param.7) | copy-start | bytes 24580
  82.8 22.9 %all-to-all-start.2 = ((f32[32,4,2,8,128]{4,3,2,1,0:T(8,128)}), f32[32,4,2,8,128]{4,3,2,1,0:T(8,128)S(1)}, u32[]{:S(2)}, u32[]{:S(2)}) async-start(f32[32,4,2,8,128]{4,3,2,1,0:T(8,128)} %bitcast.17), calls=%async_computation.2 | async-start | bytes 2097152 | tf_op jit(solution)/shard_map/all_to_all | solution.py:499
  106.7 32.9 %all-to-all-start.4 = ((f32[16,256,128]{2,1,0:T(8,128)}), f32[16,256,128]{2,1,0:T(8,128)S(1)}, u32[]{:S(2)}, u32[]{:S(2)}) async-start(f32[16,256,128]{2,1,0:T(8,128)} %pack_slots.2), calls=%async_computation.4 | async-start | bytes 4194304 | tf_op jit(solution)/shard_map/all_to_all | solution.py:531
  112.2 1.2 copy-start.1
  113.4 1.0 copy-start.3
  114.4 1.0 copy-start.5
  139.5 83.3 %all-to-all-start.5 = ((f32[16,256,128]{2,1,0:T(8,128)}), f32[16,256,128]{2,1,0:T(8,128)}, u32[]{:S(2)}, u32[]{:S(2)}) async-start(f32[16,256,128]{2,1,0:T(8,128)} %pack_slots.3), calls=%async_computation.5 | async-start | bytes 4194304 | tf_op jit(solution)/shard_map/all_to_all | solution.py:531
  146.7 1.3 collective-permute-start.6
  148.1 5.6 %collective-permute-start.7 = (f32[128,256]{1,0:T(8,128)S(1)}, f32[128,256]{1,0:T(8,128)S(1)}, u32[]{:S(2)}, u32[]{:S(2)}) collective-permute-start(f32[128,256]{1,0:T(8,128)S(1)} %add.46), channel_id=1, source_target_pairs={{0,32},{16,48},{32,0},{48,16},{64,96},{80,112},{96,64},{112,80},{1... | collective-permute-start | bytes 393224 | tf_op jit(solution)/shard_map/ppermute | solution.py:486
  153.7 6.6 %collective-permute-start.8 = (f32[128,256]{1,0:T(8,128)S(1)}, f32[128,256]{1,0:T(8,128)S(1)}, u32[]{:S(2)}, u32[]{:S(2)}) collective-permute-start(f32[128,256]{1,0:T(8,128)S(1)} %add.47), channel_id=1, source_target_pairs={{0,64},{16,80},{32,96},{48,112},{64,0},{80,16},{96,32},{112,48},{1... | collective-permute-start | bytes 393224 | tf_op jit(solution)/shard_map/ppermute | solution.py:486
  155.9 5.7 %collective-permute-start.13 = (f32[128,128]{1,0:T(8,128)S(1)}, f32[128,128]{1,0:T(8,128)S(1)}, u32[]{:S(2)}, u32[]{:S(2)}) collective-permute-start(f32[128,128]{1,0:T(8,128)S(1)} %get-tuple-element.24), channel_id=1, source_target_pairs={{0,16},{16,0},{32,48},{48,32},{64,80},{80,64},{96,112},{112,96},{1... | collective-permute-start | bytes 196616 | tf_op jit(solution)/shard_map/ppermute | solution.py:486
  160.3 13.5 %collective-permute-start.9 = (f32[128,256]{1,0:T(8,128)S(1)}, f32[128,256]{1,0:T(8,128)S(1)}, u32[]{:S(2)}, u32[]{:S(2)}) collective-permute-start(f32[128,256]{1,0:T(8,128)S(1)} %add.48), channel_id=1, source_target_pairs={{0,1},{1,0},{2,3},{3,2},{4,5},{5,4},{6,7},{7,6},{8,9},{9,8},{10,11... | collective-permute-start | bytes 393224 | tf_op jit(solution)/shard_map/ppermute | solution.py:486
  161.6 4.3 %collective-permute-start.14 = (f32[128,128]{1,0:T(8,128)S(1)}, f32[128,128]{1,0:T(8,128)S(1)}, u32[]{:S(2)}, u32[]{:S(2)}) collective-permute-start(f32[128,128]{1,0:T(8,128)S(1)} %add.53), channel_id=1, source_target_pairs={{0,32},{16,48},{32,0},{48,16},{64,96},{80,112},{96,64},{112,80},{1... | collective-permute-start | bytes 196616 | tf_op jit(solution)/shard_map/ppermute | solution.py:486
  165.9 7.9 %collective-permute-start.15 = (f32[128,128]{1,0:T(8,128)S(1)}, f32[128,128]{1,0:T(8,128)S(1)}, u32[]{:S(2)}, u32[]{:S(2)}) collective-permute-start(f32[128,128]{1,0:T(8,128)S(1)} %add.54), channel_id=1, source_target_pairs={{0,64},{16,80},{32,96},{48,112},{64,0},{80,16},{96,32},{112,48},{1... | collective-permute-start | bytes 196616 | tf_op jit(solution)/shard_map/ppermute | solution.py:486
  173.8 8.8 %collective-permute-start.10 = (f32[128,256]{1,0:T(8,128)S(1)}, f32[128,256]{1,0:T(8,128)S(1)}, u32[]{:S(2)}, u32[]{:S(2)}) collective-permute-start(f32[128,256]{1,0:T(8,128)S(1)} %add.49), channel_id=1, source_target_pairs={{0,2},{1,3},{2,0},{3,1},{4,6},{5,7},{6,4},{7,5},{8,10},{9,11},{10,... | collective-permute-start | bytes 393224 | tf_op jit(solution)/shard_map/ppermute | solution.py:486
  173.9 6.0 %collective-permute-start.16 = (f32[128,128]{1,0:T(8,128)S(1)}, f32[128,128]{1,0:T(8,128)S(1)}, u32[]{:S(2)}, u32[]{:S(2)}) collective-permute-start(f32[128,128]{1,0:T(8,128)S(1)} %add.55), channel_id=1, source_target_pairs={{0,1},{1,0},{2,3},{3,2},{4,5},{5,4},{6,7},{7,6},{8,9},{9,8},{10,11... | collective-permute-start | bytes 196616 | tf_op jit(solution)/shard_map/ppermute | solution.py:486
  179.9 5.8 %collective-permute-start.17 = (f32[128,128]{1,0:T(8,128)S(1)}, f32[128,128]{1,0:T(8,128)S(1)}, u32[]{:S(2)}, u32[]{:S(2)}) collective-permute-start(f32[128,128]{1,0:T(8,128)S(1)} %add.56), channel_id=1, source_target_pairs={{0,2},{1,3},{2,0},{3,1},{4,6},{5,7},{6,4},{7,5},{8,10},{9,11},{10,... | collective-permute-start | bytes 196616 | tf_op jit(solution)/shard_map/ppermute | solution.py:486
  182.6 8.8 %collective-permute-start.11 = (f32[128,256]{1,0:T(8,128)S(1)}, f32[128,256]{1,0:T(8,128)S(1)}, u32[]{:S(2)}, u32[]{:S(2)}) collective-permute-start(f32[128,256]{1,0:T(8,128)S(1)} %add.50), channel_id=1, source_target_pairs={{0,4},{4,0},{8,12},{12,8},{1,5},{5,1},{9,13},{13,9},{2,6},{6,2},{1... | collective-permute-start | bytes 393224 | tf_op jit(solution)/shard_map/ppermute | solution.py:486
  185.7 4.8 %collective-permute-start.18 = (f32[128,128]{1,0:T(8,128)S(1)}, f32[128,128]{1,0:T(8,128)S(1)}, u32[]{:S(2)}, u32[]{:S(2)}) collective-permute-start(f32[128,128]{1,0:T(8,128)S(1)} %add.57), channel_id=1, source_target_pairs={{0,4},{4,0},{8,12},{12,8},{1,5},{5,1},{9,13},{13,9},{2,6},{6,2},{1... | collective-permute-start | bytes 196616 | tf_op jit(solution)/shard_map/ppermute | solution.py:486
  190.5 5.8 %collective-permute-start.19 = (f32[128,128]{1,0:T(8,128)S(1)}, f32[128,128]{1,0:T(8,128)S(1)}, u32[]{:S(2)}, u32[]{:S(2)}) collective-permute-start(f32[128,128]{1,0:T(8,128)S(1)} %add.58), channel_id=1, source_target_pairs={{0,8},{4,12},{8,0},{12,4},{1,9},{5,13},{9,1},{13,5},{2,10},{6,14},... | collective-permute-start | bytes 196616 | tf_op jit(solution)/shard_map/ppermute | solution.py:486
  191.5 17.3 %collective-permute-start.12 = (f32[128,256]{1,0:T(8,128)S(1)}, f32[128,256]{1,0:T(8,128)S(1)}, u32[]{:S(2)}, u32[]{:S(2)}) collective-permute-start(f32[128,256]{1,0:T(8,128)S(1)} %add.51), channel_id=1, source_target_pairs={{0,8},{4,12},{8,0},{12,4},{1,9},{5,13},{9,1},{13,5},{2,10},{6,14},... | collective-permute-start | bytes 393224 | tf_op jit(solution)/shard_map/ppermute | solution.py:486
  (5 other events, 4.3 us)

commit v3 on v2

--- a/solution.py
+++ b/solution.py
@@ -246,8 +246,7 @@
 def prep_kernel(fields, snaps, count, *refs):
     rec = refs[0]
     before = refs[1 : 1 + 2 * count]
-    high_out, low_out = refs[1 + 2 * count : 3 + 2 * count]
-    gram = refs[3 + 2 * count]
+    high_out, low_out, gram = refs[-3:]
     for cell_row in range(16):
         for s in range(snaps):
             for f in range(0, fields, 16):
@@ -268,7 +267,7 @@
         gram[:, c * width : (c + 1) * width] = block
 
 
-def prep(rec, before, fields, snaps):
+def prep(rec, before, fields, snaps, after=()):
     width = fields * snaps
     cells = 2048
     return pl.pallas_call(
@@ -278,11 +277,11 @@
             jax.ShapeDtypeStruct((width, cells), BF16),
             jax.ShapeDtypeStruct((width, width * (len(before) // 2 + 1)), F32),
         ),
-        in_specs=[VMEM] * (1 + len(before)),
+        in_specs=[VMEM] * (1 + len(before)) + [pl.BlockSpec(memory_space=pl.ANY)] * len(after),
         out_specs=(VMEM,) * 3,
         compiler_params=params(),
         name="gram_blocks",
-    )(rec, *before)
+    )(rec, *before, *after)
 
 
 def rank_kernel(owner_count, owners, hot):
@@ -324,7 +323,8 @@
 GROUP = 4
 
 
-def pack_kernel(owners, hot, high, low, out, picked):
+def pack_kernel(owners, hot, high, low, *refs):
+    out, picked = refs[-2:]
     width = high.shape[0]
     base = pl.program_id(0) * GROUP
     own = owners[...]
@@ -341,19 +341,24 @@
         out[g] = sums[:, g * width : (g + 1) * width]
 
 
-def pack(owners, hot, high, low, owner_count):
+def pack(owners, hot, high, low, owner_count, half, slots=None):
     width, cells = high.shape
     capacity = hot.shape[0]
+    more = (slots,) if half else ()
     return pl.pallas_call(
         pack_kernel,
         grid=(owner_count // GROUP,),
-        out_shape=jax.ShapeDtypeStruct((owner_count, capacity, width), F32),
-        in_specs=[VMEM] * 4,
-        out_specs=pl.BlockSpec((GROUP, capacity, width), lambda g: (g, 0, 0)),
+        out_shape=jax.ShapeDtypeStruct((owner_count, capacity, 2 * width), F32),
+        in_specs=[VMEM] * 4 + [pl.BlockSpec(memory_space=pl.ANY)] * len(more),
+        out_specs=pl.BlockSpec((GROUP, capacity, width), lambda g: (g, 0, half)),
         scratch_shapes=[pltpu.VMEM((2, GROUP * width, cells), BF16)],
-        compiler_params=params(),
+        input_output_aliases={4: 0} if half else {},
+        compiler_params=params(),
+        cost_estimate=pl.CostEstimate(
+            flops=4 * owner_count * capacity * width * cells, bytes_accessed=4 * owner_count * capacity * width, transcendentals=0
+        ),
         name="pack_slots",
-    )(owners, hot, high, low)
+    )(owners, hot, high, low, *more)
 
 
 BLOCK = 32
@@ -449,38 +454,38 @@
 SOURCES = 2
 
 
-def basis_kernel(inverse, *refs):
-    out = refs[-1]
+def basis_kernel(inverse, panel, out):
     inv_high, inv_low = split(inverse[...])
     for b in range(SOURCES):
-        high, low = split(jnp.concatenate([ref[b] for ref in refs[:-1]], 1))
+        high, low = split(panel[b])
         rows = high.shape[0]
         out[b * rows : (b + 1) * rows, :] = bf_dot(high, inv_high, NT) + (
             bf_dot(high, inv_low, NT) + bf_dot(low, inv_high, NT)
         )
 
 
-def basis_of(inverse, panels):
-    sources, capacity, width = panels[0].shape
-    order = inverse.shape[0]
+def basis_of(inverse, panel):
+    sources, capacity, order = panel.shape
     return pl.pallas_call(
         basis_kernel,
         grid=(sources // SOURCES,),
         out_shape=jax.ShapeDtypeStruct((sources * capacity, order), F32),
-        in_specs=[pl.BlockSpec((order, order), lambda b: (0, 0))]
-        + [pl.BlockSpec((SOURCES, capacity, width), lambda b: (b, 0, 0)) for _ in panels],
+        in_specs=[
+            pl.BlockSpec((order, order), lambda b: (0, 0)),
+            pl.BlockSpec((SOURCES, capacity, order), lambda b: (b, 0, 0)),
+        ],
         out_specs=pl.BlockSpec((SOURCES * capacity, order), lambda b: (b, 0)),
         compiler_params=params(),
         name="basis_rows",
-    )(inverse, *panels)
+    )(inverse, panel)
 
 
 def ring(size, shift):
     return [(i, (i + shift) % size) for i in range(size)]
 
 
-def reduced(value):
-    for axis in ("slab", "z", "x"):
+def summed(value, *axes):
+    for axis in axes:
         size = lax.axis_size(axis)
         for level in range(size.bit_length() - 1):
             value = value + lax.ppermute(value, axis, [(i, i ^ 1 << level) for i in range(size)])
@@ -526,14 +531,19 @@
     home_two = swap(records_two.reshape(block))
     hot = rank_hot(owners, owner_count, capacity)
     high_a, low_a, gram_a = prep(home_one.reshape(-1, lanes), (), fields, HALF)
-    high_b, low_b, gram_b = prep(home_two.reshape(-1, lanes), (high_a, low_a), fields, HALF)
-    panels = [
-        lax.all_to_all(pack(owners, hot, high, low, owner_count), ("x", "z"), split_axis=0, concat_axis=0, tiled=True)
-        for high, low in ((high_a, low_a), (high_b, low_b))
-    ]
-    lead, lead_inv = factor_lead(reduced(gram_a))
-    r_factor, inverse = factor_trail(reduced(gram_b), lead, lead_inv)
-    basis = basis_of(inverse, panels)
+    part_a = summed(gram_a, "x")
+    slots = pack(owners, hot, high_a, low_a, owner_count, 0)
+    high_b, low_b, gram_b = prep(home_two.reshape(-1, lanes), (high_a, low_a), fields, HALF, (slots, part_a))
+    part_a = summed(part_a, "z")
+    part_b = summed(gram_b, "x")
+    slots = pack(owners, hot, high_b, low_b, owner_count, 1, slots)
+    slots, part_b = lax.optimization_barrier((slots, part_b))
+    part_b = summed(part_b, "z")
+    slots, part_a, part_b = lax.optimization_barrier((slots, part_a, part_b))
+    panel = lax.all_to_all(slots, ("x", "z"), split_axis=0, concat_axis=0, tiled=True)
+    lead, lead_inv = factor_lead(summed(part_a, "slab"))
+    r_factor, inverse = factor_trail(summed(part_b, "slab"), lead, lead_inv)
+    basis = basis_of(inverse, panel)
     return home_two[:, HALF - 1], r_factor, basis
 
 

time: 234 us -> 199 us (0.85); the launches traced: 230 us -> 198 us
  waiting for transfers between devices: 87.6 us -> 68.8 us
  starting transfers between devices: 64.4 us -> 57.2 us
  local copies, waits for them, and re-layouts: 11.7 us -> 4.84 us
    ppermute x14, waiting for transfers between devices: 31.3 us -> 22 us  [summed(): lax.ppermute(value, axis, [(i, i ^ 1 << level) for i in range(size)])]
    all_to_all x2 -> x1, waiting for transfers between devices: 16.2 us -> 9.41 us  [on_device(): lax.all_to_all(slots, ('x', 'z'), split_axis=0, concat_axis=0, tiled=True)]
    unnamed x23 -> x11, local copies, waits for them, and re-layouts: 9.2 us -> 3.26 us
    all_to_all x2 -> x1, starting transfers between devices: 12.7 us -> 7.15 us  [on_device(): lax.all_to_all(slots, ('x', 'z'), split_axis=0, concat_axis=0, tiled=True)]
    all_to_all x4, waiting for transfers between devices: 22.4 us -> 19.7 us  [swap(): return lax.all_to_all(value, plane, split_axis=0, concat_axis=0, tiled=True)]
  transfers between devices with their start and end apart: 26 -> 25, of which waited for: 17 -> 15; matrix products, arithmetic and copies ran while one was open for 2% -> 1% of each run, Pallas kernels for 24% -> 27%
where the time goes in v3:
time: 199 us; the launch traced here: 198 us
  waiting for transfers between devices  68.8 us (35%)
  Pallas kernels  62.4 us (31%)
  starting transfers between devices  57.2 us (29%)
  local copies, waits for them, and re-layouts  4.84 us (2%)
  other arithmetic  3.52 us (2%)
    all_to_all x4, starting transfers between devices, swap(): return lax.all_to_all(value, plane, split_axis=0, concat_axis=0, tiled=True)  28.3 us
    ppermute x14, waiting for transfers between devices, summed(): lax.ppermute(value, axis, [(i, i ^ 1 << level) for i in range(size)])  22 us
    all_to_all x4, waiting for transfers between devices, swap(): return lax.all_to_all(value, plane, split_axis=0, concat_axis=0, tiled=True)  19.7 us
    ppermute x14, starting transfers between devices, summed(): lax.ppermute(value, axis, [(i, i ^ 1 << level) for i in range(size)])  14.8 us
    pallas_call x1, Pallas kernels, factor_trail(): pl.pallas_call(trail_kernel, out_shape=(jax.ShapeDtypeStruct((2 * order,...  14 us
    pallas_call x2, Pallas kernels, pack(): pl.pallas_call(pack_kernel, grid=(owner_count // GROUP,), out_shape=jax.S...  12.5 us
    ppermute x2, waiting for transfers between devices, edges(): high = lax.ppermute(by_row[:, 0], 'x', ring(x_size, -1))  12.5 us
    pallas_call x1, Pallas kernels, factor_lead(): pl.pallas_call(lead_kernel, out_shape=(jax.ShapeDtypeStruct((order, order...  12.4 us
  transfers between devices with their start and end apart: 25, of which 15 were waited for; matrix products, arithmetic and copies ran while one was open for 1% of the time, Pallas kernels for 27%

profile of v3, /device:TPU:64, one launch (start us, length us, event | category | flops | bytes accessed | tf_op | source)
XLA Modules:
  0.0 197.7 jit_solution(3071779513246254600)
XLA Ops:
  0.6 1.6 copy.26
  4.4 7.8 %all-to-all-start.1 = ((f32[32,5,2,8,128]{4,3,2,1,0:T(8,128)}), f32[32,5,2,8,128]{4,3,2,1,0:T(8,128)S(1)}, u32[]{:S(2)}, u32[]{:S(2)}) async-start(f32[32,5,2,8,128]{4,3,2,1,0:T(8,128)} %pad_maximum_fusion), calls=%async_computation.1 | async-start | bytes 2621440 | tf_op jit(solution)/shard_map/all_to_all | solution.py:504
  13.3 17.0 %all-to-all-done.1 = f32[32,5,2,8,128]{4,3,2,1,0:T(8,128)S(1)} async-done(((f32[32,5,2,8,128]{4,3,2,1,0:T(8,128)}), f32[32,5,2,8,128]{4,3,2,1,0:T(8,128)S(1)}, u32[]{:S(2)}, u32[]{:S(2)}) %all-to-all-start.1) | async-done | bytes 1310752 | tf_op jit(solution)/shard_map/all_to_all | solution.py:504
  30.3 5.6 %all-to-all-start = ((f32[32,4,2,8,128]{4,3,2,1,0:T(8,128)}), f32[32,4,2,8,128]{4,3,2,1,0:T(8,128)S(1)}, u32[]{:S(2)}, u32[]{:S(2)}) async-start(f32[32,4,2,8,128]{4,3,2,1,0:T(8,128)} %slice_convert_fusion), calls=%async_computation | async-start | bytes 2097152 | tf_op jit(solution)/shard_map/all_to_all | solution.py:504
  36.7 2.8 %collective-permute-start.3 = (f32[8,5,2,8,128]{4,3,2,1,0:T(8,128)}, f32[8,5,2,8,128]{4,3,2,1,0:T(8,128)S(1)}, u32[]{:S(2)}, u32[]{:S(2)}) collective-permute-start(f32[8,5,2,8,128]{4,3,2,1,0:T(8,128)} %get-tuple-element.41), channel_id=1, source_target_pairs={{0,12},{4,0},{8,4},{12,8},{1,13},{5,1},{9,5},{13,9},{2,14},{6,2},{... | collective-permute-start | bytes 983048 | tf_op jit(solution)/shard_map/ppermute | solution.py:516
  39.5 7.5 %collective-permute-done.3 = f32[8,5,2,8,128]{4,3,2,1,0:T(8,128)S(1)} collective-permute-done((f32[8,5,2,8,128]{4,3,2,1,0:T(8,128)}, f32[8,5,2,8,128]{4,3,2,1,0:T(8,128)S(1)}, u32[]{:S(2)}, u32[]{:S(2)}) %collective-permute-start.3) | collective-permute-done | bytes 327712 | tf_op jit(solution)/shard_map/ppermute | solution.py:516
  47.1 3.1 %collective-permute-done.2 = f32[8,5,2,8,128]{4,3,2,1,0:T(8,128)S(1)} collective-permute-done((f32[8,5,2,8,128]{4,3,2,1,0:T(8,128)S(1)}, f32[8,5,2,8,128]{4,3,2,1,0:T(8,128)S(1)}, u32[]{:S(2)}, u32[]{:S(2)}) %collective-permute-start.2) | collective-permute-done | bytes 327712 | tf_op jit(solution)/shard_map/ppermute | solution.py:515
  51.9 6.3 %diffuse_first.1 = (f32[2048,128]{1,0:T(8,128)}, f32[32,2,8,128]{3,2,1,0:T(8,128)S(1)}, f32[48,2,8,128]{3,2,1,0:T(8,128)S(1)}) custom-call(s32[2]{0:T(128)S(1)} %add_convert_fusion.edge, f32[2560,128]{1,0:T(8,128)S(1)} %bitcast.42, f32[640,128]{1,0:T(8,128)S(1)} %bitcast.48, f32[640,128]{1,0:T(8,128)S(1)} %bitcast.47), custom_call_target="tpu_custom_call" | custom-call | tf_op jit(solution)/shard_map/diffuse_first/pallas_call | solution.py:215
  58.2 7.5 %all-to-all-start.3 = ((f32[32,4,2,8,128]{4,3,2,1,0:T(8,128)}), f32[32,4,2,8,128]{4,3,2,1,0:T(8,128)S(1)}, u32[]{:S(2)}, u32[]{:S(2)}) async-start(f32[32,4,2,8,128]{4,3,2,1,0:T(8,128)} %bitcast.21), calls=%async_computation.3 | async-start | bytes 2097152 | tf_op jit(solution)/shard_map/all_to_all | solution.py:504
  66.3 1.5 collective-permute-start
  67.8 1.8 collective-permute-start.5
  69.9 4.9 %collective-permute-done.1 = f32[8,4,2,8,128]{4,3,2,1,0:T(8,128)S(1)} collective-permute-done((f32[8,4,2,8,128]{4,3,2,1,0:T(8,128)S(1)}, f32[8,4,2,8,128]{4,3,2,1,0:T(8,128)S(1)}, u32[]{:S(2)}, u32[]{:S(2)}) %collective-permute-start.1) | collective-permute-done | bytes 262176 | tf_op jit(solution)/shard_map/ppermute | solution.py:516
  77.0 5.8 %diffuse_second.1 = (f32[2048,128]{1,0:T(8,128)}, f32[32,2,8,128]{3,2,1,0:T(8,128)}) custom-call(f32[2048,128]{1,0:T(8,128)S(1)} %bitcast.44, f32[512,128]{1,0:T(8,128)S(1)} %bitcast.50, f32[512,128]{1,0:T(8,128)S(1)} %bitcast.49, f32[32,2,8,128]{3,2,1,0:T(8,128)S(1)} %get-tuple-element.22.start, f32[8,2,8,128]{3,2,1,0:T(8,128)S(1)} %collective-permute-done.4.start_low, ...), custom_call_target="tpu_custom_call" | custom-call | tf_op jit(solution)/shard_map/diffuse_second/pallas_call | solution.py:232
  82.8 7.5 %all-to-all-start.2 = ((f32[32,4,2,8,128]{4,3,2,1,0:T(8,128)}), f32[32,4,2,8,128]{4,3,2,1,0:T(8,128)S(1)}, u32[]{:S(2)}, u32[]{:S(2)}) async-start(f32[32,4,2,8,128]{4,3,2,1,0:T(8,128)} %bitcast.17), calls=%async_computation.2 | async-start | bytes 2097152 | tf_op jit(solution)/shard_map/all_to_all | solution.py:504
  92.9 3.1 %collective-permute-done.6 = f32[128,128]{1,0:T(8,128)S(1)} collective-permute-done((f32[128,128]{1,0:T(8,128)S(1)}, f32[128,128]{1,0:T(8,128)S(1)}, u32[]{:S(2)}, u32[]{:S(2)}) %collective-permute-start.6) | collective-permute-done | bytes 65568 | tf_op jit(solution)/shard_map/ppermute | solution.py:491
  96.8 6.2 %pack_slots.2.refs_3_.refs_0_ = f32[16,256,256]{2,1,0:T(8,128)} custom-call(s32[16,128]{1,0:T(8,128)S(1)} %bitcast.52, bf16[256,2048]{1,0:T(8,128)(2,1)S(1)} %slot_ranks.1.hot, bf16[128,2048]{1,0:T(8,128)(2,1)S(1)} %get-tuple-element.26.high.refs_1_, bf16[128,2048]{1,0:T(8,128)(2,1)S(1)} %get-tuple-element.27.low.refs_2_), custom_call_target="tpu_custom_call" | custom-call | flops 4294967296 | bytes 2097152 | tf_op jit(solution)/shard_map/pack_slots/pallas_call | solution.py:348
  103.0 2.6 %all-to-all-done.2 = f32[32,4,2,8,128]{4,3,2,1,0:T(8,128)S(1)} async-done(((f32[32,4,2,8,128]{4,3,2,1,0:T(8,128)}), f32[32,4,2,8,128]{4,3,2,1,0:T(8,128)S(1)}, u32[]{:S(2)}, u32[]{:S(2)}) %all-to-all-start.2) | async-done | bytes 1048608 | tf_op jit(solution)/shard_map/all_to_all | solution.py:504
  105.6 1.5 gram_blocks.3
  107.6 4.6 %collective-permute-done.8 = f32[128,256]{1,0:T(8,128)S(1)} collective-permute-done((f32[128,256]{1,0:T(8,128)S(1)}, f32[128,256]{1,0:T(8,128)S(1)}, u32[]{:S(2)}, u32[]{:S(2)}) %collective-permute-start.8) | collective-permute-done | bytes 131104 | tf_op jit(solution)/shard_map/ppermute | solution.py:491
  113.0 6.3 %pack_slots.3 = f32[16,256,256]{2,1,0:T(8,128)} custom-call(s32[16,128]{1,0:T(8,128)S(1)} %bitcast.53, bf16[256,2048]{1,0:T(8,128)(2,1)S(1)} %slot_ranks.1.hot, bf16[128,2048]{1,0:T(8,128)(2,1)S(1)} %get-tuple-element.29.high, bf16[128,2048]{1,0:T(8,128)(2,1)S(1)} %get-tuple-element.30.low, ...), custom_call_target="tpu_custom_call", output_to_operand_aliasing={{}: (4, {})} | custom-call | flops 4294967296 | bytes 2097152 | tf_op jit(solution)/shard_map/pack_slots/pallas_call | solution.py:348
  121.4 2.9 %collective-permute-done.12 = f32[128,256]{1,0:T(8,128)S(1)} collective-permute-done((f32[128,256]{1,0:T(8,128)S(1)}, f32[128,256]{1,0:T(8,128)S(1)}, u32[]{:S(2)}, u32[]{:S(2)}) %collective-permute-start.12) | collective-permute-done | bytes 131104 | tf_op jit(solution)/shard_map/ppermute | solution.py:491
  124.3 2.1 %collective-permute-start.13 = (f32[128,256]{1,0:T(8,128)S(1)}, f32[128,256]{1,0:T(8,128)S(1)}, u32[]{:S(2)}, u32[]{:S(2)}) collective-permute-start(f32[128,256]{1,0:T(8,128)S(1)} %add.52), channel_id=1, source_target_pairs={{0,2},{1,3},{2,0},{3,1},{4,6},{5,7},{6,4},{7,5},{8,10},{9,11},{10,... | collective-permute-start | bytes 393224 | tf_op jit(solution)/shard_map/ppermute | solution.py:491
  126.5 1.6 collective-permute-start.11
  128.0 4.3 %collective-permute-done.11 = f32[128,128]{1,0:T(8,128)S(1)} collective-permute-done((f32[128,128]{1,0:T(8,128)S(1)}, f32[128,128]{1,0:T(8,128)S(1)}, u32[]{:S(2)}, u32[]{:S(2)}) %collective-permute-start.11) | collective-permute-done | bytes 65568 | tf_op jit(solution)/shard_map/ppermute | solution.py:491
  132.4 7.2 %all-to-all-start.4 = ((f32[16,256,256]{2,1,0:T(8,128)}), f32[16,256,256]{2,1,0:T(8,128)}, u32[]{:S(2)}, u32[]{:S(2)}) async-start(f32[16,256,256]{2,1,0:T(8,128)} %pack_slots.3), calls=%async_computation.4 | async-start | bytes 8388608 | tf_op jit(solution)/shard_map/all_to_all | solution.py:543
  143.1 4.8 %collective-permute-done.18 = f32[128,128]{1,0:T(8,128)S(1)} collective-permute-done((f32[128,128]{1,0:T(8,128)S(1)}, f32[128,128]{1,0:T(8,128)S(1)}, u32[]{:S(2)}, u32[]{:S(2)}) %collective-permute-start.18) | collective-permute-done | bytes 65568 | tf_op jit(solution)/shard_map/ppermute | solution.py:491
  147.9 2.2 %collective-permute-start.19 = (f32[128,128]{1,0:T(8,128)S(1)}, f32[128,128]{1,0:T(8,128)S(1)}, u32[]{:S(2)}, u32[]{:S(2)}) collective-permute-start(f32[128,128]{1,0:T(8,128)S(1)} %add.58), channel_id=1, source_target_pairs={{0,64},{16,80},{32,96},{48,112},{64,0},{80,16},{96,32},{112,48},{1... | collective-permute-start | bytes 196616 | tf_op jit(solution)/shard_map/ppermute | solution.py:491
  150.1 1.7 collective-permute-start.16
  154.0 12.4 %factor_lead.1 = (f32[128,128]{1,0:T(8,128)S(1)}, f32[128,128]{1,0:T(8,128)S(1)}) custom-call(f32[128,128]{1,0:T(8,128)S(1)} %add.59.gram), custom_call_target="tpu_custom_call" | custom-call | tf_op jit(solution)/shard_map/factor_lead/pallas_call | solution.py:430
  166.4 14.0 %factor_trail.1 = (f32[256,256]{1,0:T(8,128)}, f32[256,256]{1,0:T(8,128)S(1)}) custom-call(f32[128,256]{1,0:T(8,128)S(1)} %add.56.gram, f32[128,128]{1,0:T(8,128)S(1)} %get-tuple-element.36.lead, f32[128,128]{1,0:T(8,128)S(1)} %get-tuple-element.37.lead_inv), custom_call_target="tpu_custom_call" | custom-call | tf_op jit(solution)/shard_map/factor_trail/pallas_call | solution.py:443
  180.4 9.4 %all-to-all-done.4.panel = f32[16,256,256]{2,1,0:T(8,128)} async-done(((f32[16,256,256]{2,1,0:T(8,128)}), f32[16,256,256]{2,1,0:T(8,128)}, u32[]{:S(2)}, u32[]{:S(2)}) %all-to-all-start.4) | async-done | bytes 4194336 | tf_op jit(solution)/shard_map/all_to_all | solution.py:543
  189.8 7.9 %basis_rows.1 = f32[4096,256]{1,0:T(8,128)} custom-call(f32[256,256]{1,0:T(8,128)S(1)} %get-tuple-element.39.inverse, f32[16,256,256]{2,1,0:T(8,128)} %all-to-all-done.4.panel), custom_call_target="tpu_custom_call" | custom-call | tf_op jit(solution)/shard_map/basis_rows/pallas_call | solution.py:469
  (63 shorter events, 21.3 us)
Async XLA Ops:
  0.6 1.6 copy-start.3
  2.2 1.0 copy-start.4
  4.4 25.9 %all-to-all-start.1 = ((f32[32,5,2,8,128]{4,3,2,1,0:T(8,128)}), f32[32,5,2,8,128]{4,3,2,1,0:T(8,128)S(1)}, u32[]{:S(2)}, u32[]{:S(2)}) async-start(f32[32,5,2,8,128]{4,3,2,1,0:T(8,128)} %pad_maximum_fusion), calls=%async_computation.1 | async-start | bytes 2621440 | tf_op jit(solution)/shard_map/all_to_all | solution.py:504
  30.3 27.8 %all-to-all-start = ((f32[32,4,2,8,128]{4,3,2,1,0:T(8,128)}), f32[32,4,2,8,128]{4,3,2,1,0:T(8,128)S(1)}, u32[]{:S(2)}, u32[]{:S(2)}) async-start(f32[32,4,2,8,128]{4,3,2,1,0:T(8,128)} %slice_convert_fusion), calls=%async_computation | async-start | bytes 2097152 | tf_op jit(solution)/shard_map/all_to_all | solution.py:504
  36.7 10.4 %collective-permute-start.3 = (f32[8,5,2,8,128]{4,3,2,1,0:T(8,128)}, f32[8,5,2,8,128]{4,3,2,1,0:T(8,128)S(1)}, u32[]{:S(2)}, u32[]{:S(2)}) collective-permute-start(f32[8,5,2,8,128]{4,3,2,1,0:T(8,128)} %get-tuple-element.41), channel_id=1, source_target_pairs={{0,12},{4,0},{8,4},{12,8},{1,13},{5,1},{9,5},{13,9},{2,14},{6,2},{... | collective-permute-start | bytes 983048 | tf_op jit(solution)/shard_map/ppermute | solution.py:516
  39.5 10.7 %collective-permute-start.2 = (f32[8,5,2,8,128]{4,3,2,1,0:T(8,128)S(1)}, f32[8,5,2,8,128]{4,3,2,1,0:T(8,128)S(1)}, u32[]{:S(2)}, u32[]{:S(2)}) collective-permute-start(f32[8,5,2,8,128]{4,3,2,1,0:T(8,128)S(1)} %get-tuple-element.42), channel_id=1, source_target_pairs={{0,4},{4,8},{8,12},{12,0},{1,5},{5,9},{9,13},{13,1},{2,6},{6,10},{... | collective-permute-start | bytes 983048 | tf_op jit(solution)/shard_map/ppermute | solution.py:515
  50.2 0.7 copy-start
  50.9 1.0 copy-start.1
  58.2 24.6 %all-to-all-start.3 = ((f32[32,4,2,8,128]{4,3,2,1,0:T(8,128)}), f32[32,4,2,8,128]{4,3,2,1,0:T(8,128)S(1)}, u32[]{:S(2)}, u32[]{:S(2)}) async-start(f32[32,4,2,8,128]{4,3,2,1,0:T(8,128)} %bitcast.21), calls=%async_computation.3 | async-start | bytes 2097152 | tf_op jit(solution)/shard_map/all_to_all | solution.py:504
  65.7 9.1 %collective-permute-start.1 = (f32[8,4,2,8,128]{4,3,2,1,0:T(8,128)S(1)}, f32[8,4,2,8,128]{4,3,2,1,0:T(8,128)S(1)}, u32[]{:S(2)}, u32[]{:S(2)}) collective-permute-start(f32[8,4,2,8,128]{4,3,2,1,0:T(8,128)S(1)} %get-tuple-element.43), channel_id=1, source_target_pairs={{0,12},{4,0},{8,4},{12,8},{1,13},{5,1},{9,5},{13,9},{2,14},{6,2},{... | collective-permute-start | bytes 786440 | tf_op jit(solution)/shard_map/ppermute | solution.py:516
  66.3 10.0 %collective-permute-start = (f32[8,4,2,8,128]{4,3,2,1,0:T(8,128)S(1)}, f32[8,4,2,8,128]{4,3,2,1,0:T(8,128)S(1)}, u32[]{:S(2)}, u32[]{:S(2)}) collective-permute-start(f32[8,4,2,8,128]{4,3,2,1,0:T(8,128)S(1)} %get-tuple-element.44), channel_id=1, source_target_pairs={{0,4},{4,8},{8,12},{12,0},{1,5},{5,9},{9,13},{13,1},{2,6},{6,10},{... | collective-permute-start | bytes 786440 | tf_op jit(solution)/shard_map/ppermute | solution.py:515
  67.8 8.5 %collective-permute-start.5 = (f32[8,2,8,128]{3,2,1,0:T(8,128)S(1)}, f32[8,2,8,128]{3,2,1,0:T(8,128)S(1)}, u32[]{:S(2)}, u32[]{:S(2)}) collective-permute-start(f32[8,2,8,128]{3,2,1,0:T(8,128)S(1)} %get-tuple-element.45), channel_id=1, source_target_pairs={{0,12},{4,0},{8,4},{12,8},{1,13},{5,1},{9,5},{13,9},{2,14},{6,2},{... | collective-permute-start | bytes 196616 | tf_op jit(solution)/shard_map/ppermute | solution.py:525
  69.6 7.4 %collective-permute-start.4 = (f32[8,2,8,128]{3,2,1,0:T(8,128)S(1)}, f32[8,2,8,128]{3,2,1,0:T(8,128)S(1)}, u32[]{:S(2)}, u32[]{:S(2)}) collective-permute-start(f32[8,2,8,128]{3,2,1,0:T(8,128)S(1)} %get-tuple-element.46), channel_id=1, source_target_pairs={{0,4},{4,8},{8,12},{12,0},{1,5},{5,9},{9,13},{13,1},{2,6},{6,10},{... | collective-permute-start | bytes 196616 | tf_op jit(solution)/shard_map/ppermute | solution.py:524
  82.8 9.3 %copy-start.2 = (s32[1,1,2048,1]{2,3,1,0:T(1,128)S(1)}, s32[1,1,2048,1]{2,3,1,0:T(1,128)}, u32[]{:S(2)}) copy-start(s32[1,1,2048,1]{2,3,1,0:T(1,128)} %param.7) | copy-start | bytes 24580
  82.8 22.9 %all-to-all-start.2 = ((f32[32,4,2,8,128]{4,3,2,1,0:T(8,128)}), f32[32,4,2,8,128]{4,3,2,1,0:T(8,128)S(1)}, u32[]{:S(2)}, u32[]{:S(2)}) async-start(f32[32,4,2,8,128]{4,3,2,1,0:T(8,128)} %bitcast.17), calls=%async_computation.2 | async-start | bytes 2097152 | tf_op jit(solution)/shard_map/all_to_all | solution.py:504
  91.5 4.5 %collective-permute-start.6 = (f32[128,128]{1,0:T(8,128)S(1)}, f32[128,128]{1,0:T(8,128)S(1)}, u32[]{:S(2)}, u32[]{:S(2)}) collective-permute-start(f32[128,128]{1,0:T(8,128)S(1)} %get-tuple-element.28), channel_id=1, source_target_pairs={{0,4},{4,0},{8,12},{12,8},{1,5},{5,1},{9,13},{13,9},{2,6},{6,2},{1... | collective-permute-start | bytes 196616 | tf_op jit(solution)/shard_map/ppermute | solution.py:491
  96.1 7.0 %collective-permute-start.7 = (f32[128,128]{1,0:T(8,128)S(1)}, f32[128,128]{1,0:T(8,128)S(1)}, u32[]{:S(2)}, u32[]{:S(2)}) collective-permute-start(f32[128,128]{1,0:T(8,128)S(1)} %add.46), channel_id=1, source_target_pairs={{0,8},{4,12},{8,0},{12,4},{1,9},{5,13},{9,1},{13,5},{2,10},{6,14},... | collective-permute-start | bytes 196616 | tf_op jit(solution)/shard_map/ppermute | solution.py:491
  107.2 5.0 %collective-permute-start.8 = (f32[128,256]{1,0:T(8,128)S(1)}, f32[128,256]{1,0:T(8,128)S(1)}, u32[]{:S(2)}, u32[]{:S(2)}) collective-permute-start(f32[128,256]{1,0:T(8,128)S(1)} %get-tuple-element.31), channel_id=1, source_target_pairs={{0,4},{4,0},{8,12},{12,8},{1,5},{5,1},{9,13},{13,9},{2,6},{6,2},{1... | collective-permute-start | bytes 393224 | tf_op jit(solution)/shard_map/ppermute | solution.py:491
  112.3 7.0 %collective-permute-start.9 = (f32[128,256]{1,0:T(8,128)S(1)}, f32[128,256]{1,0:T(8,128)S(1)}, u32[]{:S(2)}, u32[]{:S(2)}) collective-permute-start(f32[128,256]{1,0:T(8,128)S(1)} %add.48), channel_id=1, source_target_pairs={{0,8},{4,12},{8,0},{12,4},{1,9},{5,13},{9,1},{13,5},{2,10},{6,14},... | collective-permute-start | bytes 393224 | tf_op jit(solution)/shard_map/ppermute | solution.py:491
  119.3 5.0 %collective-permute-start.12 = (f32[128,256]{1,0:T(8,128)S(1)}, f32[128,256]{1,0:T(8,128)S(1)}, u32[]{:S(2)}, u32[]{:S(2)}) collective-permute-start(f32[128,256]{1,0:T(8,128)S(1)} %add.49), channel_id=1, source_target_pairs={{0,1},{1,0},{2,3},{3,2},{4,5},{5,4},{6,7},{7,6},{8,9},{9,8},{10,11... | collective-permute-start | bytes 393224 | tf_op jit(solution)/shard_map/ppermute | solution.py:491
  120.7 5.7 %collective-permute-start.10 = (f32[128,128]{1,0:T(8,128)S(1)}, f32[128,128]{1,0:T(8,128)S(1)}, u32[]{:S(2)}, u32[]{:S(2)}) collective-permute-start(f32[128,128]{1,0:T(8,128)S(1)} %add.47.refs_4_), channel_id=1, source_target_pairs={{0,1},{1,0},{2,3},{3,2},{4,5},{5,4},{6,7},{7,6},{8,9},{9,8},{10,11... | collective-permute-start | bytes 196616 | tf_op jit(solution)/shard_map/ppermute | solution.py:491
  124.3 8.0 %collective-permute-start.13 = (f32[128,256]{1,0:T(8,128)S(1)}, f32[128,256]{1,0:T(8,128)S(1)}, u32[]{:S(2)}, u32[]{:S(2)}) collective-permute-start(f32[128,256]{1,0:T(8,128)S(1)} %add.52), channel_id=1, source_target_pairs={{0,2},{1,3},{2,0},{3,1},{4,6},{5,7},{6,4},{7,5},{8,10},{9,11},{10,... | collective-permute-start | bytes 393224 | tf_op jit(solution)/shard_map/ppermute | solution.py:491
  126.5 5.8 %collective-permute-start.11 = (f32[128,128]{1,0:T(8,128)S(1)}, f32[128,128]{1,0:T(8,128)S(1)}, u32[]{:S(2)}, u32[]{:S(2)}) collective-permute-start(f32[128,128]{1,0:T(8,128)S(1)} %add.50), channel_id=1, source_target_pairs={{0,2},{1,3},{2,0},{3,1},{4,6},{5,7},{6,4},{7,5},{8,10},{9,11},{10,... | collective-permute-start | bytes 196616 | tf_op jit(solution)/shard_map/ppermute | solution.py:491
  132.4 57.4 %all-to-all-start.4 = ((f32[16,256,256]{2,1,0:T(8,128)}), f32[16,256,256]{2,1,0:T(8,128)}, u32[]{:S(2)}, u32[]{:S(2)}) async-start(f32[16,256,256]{2,1,0:T(8,128)} %pack_slots.3), calls=%async_computation.4 | async-start | bytes 8388608 | tf_op jit(solution)/shard_map/all_to_all | solution.py:543
  139.5 1.3 collective-permute-start.14
  139.5 2.2 %collective-permute-start.17 = (f32[128,128]{1,0:T(8,128)S(1)}, f32[128,128]{1,0:T(8,128)S(1)}, u32[]{:S(2)}, u32[]{:S(2)}) collective-permute-start(f32[128,128]{1,0:T(8,128)S(1)} %add.51), channel_id=1, source_target_pairs={{0,16},{16,0},{32,48},{48,32},{64,80},{80,64},{96,112},{112,96},{1... | collective-permute-start | bytes 196616 | tf_op jit(solution)/shard_map/ppermute | solution.py:491
  140.9 9.2 %collective-permute-start.15 = (f32[128,256]{1,0:T(8,128)S(1)}, f32[128,256]{1,0:T(8,128)S(1)}, u32[]{:S(2)}, u32[]{:S(2)}) collective-permute-start(f32[128,256]{1,0:T(8,128)S(1)} %add.54), channel_id=1, source_target_pairs={{0,32},{16,48},{32,0},{48,16},{64,96},{80,112},{96,64},{112,80},{1... | collective-permute-start | bytes 393224 | tf_op jit(solution)/shard_map/ppermute | solution.py:491
  141.7 6.2 %collective-permute-start.18 = (f32[128,128]{1,0:T(8,128)S(1)}, f32[128,128]{1,0:T(8,128)S(1)}, u32[]{:S(2)}, u32[]{:S(2)}) collective-permute-start(f32[128,128]{1,0:T(8,128)S(1)} %add.57), channel_id=1, source_target_pairs={{0,32},{16,48},{32,0},{48,16},{64,96},{80,112},{96,64},{112,80},{1... | collective-permute-start | bytes 196616 | tf_op jit(solution)/shard_map/ppermute | solution.py:491
  147.9 6.0 %collective-permute-start.19 = (f32[128,128]{1,0:T(8,128)S(1)}, f32[128,128]{1,0:T(8,128)S(1)}, u32[]{:S(2)}, u32[]{:S(2)}) collective-permute-start(f32[128,128]{1,0:T(8,128)S(1)} %add.58), channel_id=1, source_target_pairs={{0,64},{16,80},{32,96},{48,112},{64,0},{80,16},{96,32},{112,48},{1... | collective-permute-start | bytes 196616 | tf_op jit(solution)/shard_map/ppermute | solution.py:491
  150.1 16.3 %collective-permute-start.16 = (f32[128,256]{1,0:T(8,128)S(1)}, f32[128,256]{1,0:T(8,128)S(1)}, u32[]{:S(2)}, u32[]{:S(2)}) collective-permute-start(f32[128,256]{1,0:T(8,128)S(1)} %add.55), channel_id=1, source_target_pairs={{0,64},{16,80},{32,96},{48,112},{64,0},{80,16},{96,32},{112,48},{1... | collective-permute-start | bytes 393224 | tf_op jit(solution)/shard_map/ppermute | solution.py:491

commit v4 on v3

--- a/solution.py
+++ b/solution.py
@@ -243,10 +243,10 @@
     )(main, low, high, start, start_low, start_high, visc)
 
 
-def prep_kernel(fields, snaps, count, *refs):
+def prep_kernel(fields, snaps, count, core, *refs):
     rec = refs[0]
     before = refs[1 : 1 + 2 * count]
-    high_out, low_out, gram = refs[-3:]
+    high_out, low_out, keep, send, gram = refs[-5:]
     for cell_row in range(16):
         for s in range(snaps):
             for f in range(0, fields, 16):
@@ -265,9 +265,13 @@
         oh, ol = other_high[...], other_low[...]
         block = bf_dot(high, oh, NT) + (bf_dot(high, ol, NT) + bf_dot(low, oh, NT))
         gram[:, c * width : (c + 1) * width] = block
-
-
-def prep(rec, before, fields, snaps, after=()):
+    half = width // 2
+    mine = core[0]
+    keep[...] = gram[pl.ds(mine * half, half), :]
+    send[...] = gram[pl.ds((1 - mine) * half, half), :]
+
+
+def prep(core, rec, before, fields, snaps, after=()):
     width = fields * snaps
     cells = 2048
     return pl.pallas_call(
@@ -275,13 +279,14 @@
         out_shape=(
             jax.ShapeDtypeStruct((width, cells), BF16),
             jax.ShapeDtypeStruct((width, cells), BF16),
-            jax.ShapeDtypeStruct((width, width * (len(before) // 2 + 1)), F32),
-        ),
-        in_specs=[VMEM] * (1 + len(before)) + [pl.BlockSpec(memory_space=pl.ANY)] * len(after),
-        out_specs=(VMEM,) * 3,
+        )
+        + (jax.ShapeDtypeStruct((width // 2, width * (len(before) // 2 + 1)), F32),) * 2,
+        in_specs=[SMEM] + [VMEM] * (1 + len(before)) + [pl.BlockSpec(memory_space=pl.ANY)] * len(after),
+        out_specs=(VMEM,) * 4,
+        scratch_shapes=[pltpu.VMEM((width, width * (len(before) // 2 + 1)), F32)],
         compiler_params=params(),
         name="gram_blocks",
-    )(rec, *before, *after)
+    )(core, rec, *before, *after)
 
 
 def rank_kernel(owner_count, owners, hot):
@@ -323,10 +328,10 @@
 GROUP = 4
 
 
-def pack_kernel(owners, hot, high, low, *refs):
+def pack_kernel(first, owners, hot, high, low, *refs):
     out, picked = refs[-2:]
     width = high.shape[0]
-    base = pl.program_id(0) * GROUP
+    base = (first + pl.program_id(0)) * GROUP
     own = owners[...]
     rows = own.shape[0]
     for part, source in enumerate((high, low)):
@@ -341,21 +346,25 @@
         out[g] = sums[:, g * width : (g + 1) * width]
 
 
-def pack(owners, hot, high, low, owner_count, half, slots=None):
+def pack(owners, hot, high, low, owner_count, half, slots=None, part=0, parts=1):
     width, cells = high.shape
     capacity = hot.shape[0]
-    more = (slots,) if half else ()
-    return pl.pallas_call(
-        pack_kernel,
-        grid=(owner_count // GROUP,),
+    more = () if slots is None else (slots,)
+    groups = owner_count // GROUP // parts
+    first = part * groups
+    return pl.pallas_call(
+        functools.partial(pack_kernel, first),
+        grid=(groups,),
         out_shape=jax.ShapeDtypeStruct((owner_count, capacity, 2 * width), F32),
         in_specs=[VMEM] * 4 + [pl.BlockSpec(memory_space=pl.ANY)] * len(more),
-        out_specs=pl.BlockSpec((GROUP, capacity, width), lambda g: (g, 0, half)),
+        out_specs=pl.BlockSpec((GROUP, capacity, width), lambda g: (first + g, 0, half)),
         scratch_shapes=[pltpu.VMEM((2, GROUP * width, cells), BF16)],
-        input_output_aliases={4: 0} if half else {},
+        input_output_aliases={4: 0} if more else {},
         compiler_params=params(),
         cost_estimate=pl.CostEstimate(
-            flops=4 * owner_count * capacity * width * cells, bytes_accessed=4 * owner_count * capacity * width, transcendentals=0
+            flops=4 * GROUP * groups * capacity * width * cells,
+            bytes_accessed=4 * GROUP * groups * capacity * width,
+            transcendentals=0,
         ),
         name="pack_slots",
     )(owners, hot, high, low, *more)
@@ -397,17 +406,25 @@
     return jnp.where(at <= lax.broadcasted_iota(jnp.int32, value.shape, 1), value, 0.0)
 
 
-def lead_kernel(gram, r_out, inv_out, work):
-    order = gram.shape[0]
-    work[:, 0:order] = gram[...]
+def joined(core, own, other, whole, width):
+    half = own.shape[0]
+    mine = core[0]
+    whole[pl.ds(mine * half, half), 0:width] = own[...]
+    whole[pl.ds((1 - mine) * half, half), 0:width] = other[...]
+
+
+def lead_kernel(core, own, other, r_out, inv_out, work):
+    order = 2 * own.shape[0]
+    joined(core, own, other, work, order)
     work[:, order:] = identity(order)
     eliminate(work, order)
     r_out[...] = upper(work[:, 0:order])
     inv_out[...] = work[:, order:]
 
 
-def trail_kernel(gram, lead, lead_inv, r_out, inv_out, work):
+def trail_kernel(core, own_half, other_half, lead, lead_inv, r_out, inv_out, work, gram):
     order = lead.shape[0]
+    joined(core, own_half, other_half, gram, 2 * order)
     inverse = lead_inv[...]
     cross = exact_dot(inverse, gram[:, 0:order], NT)
     work[:, 0:order] = gram[:, order:] - exact_dot(cross, cross, TN)
@@ -425,33 +442,33 @@
     inv_out[order:, order:] = own
 
 
-def factor_lead(gram):
-    order = gram.shape[0]
+def factor_lead(core, own, other):
+    order = 2 * own.shape[0]
     return pl.pallas_call(
         lead_kernel,
         out_shape=(jax.ShapeDtypeStruct((order, order), F32),) * 2,
-        in_specs=[VMEM],
+        in_specs=[SMEM, VMEM, VMEM],
         out_specs=(VMEM,) * 2,
         scratch_shapes=[pltpu.VMEM((order, 2 * order), F32)],
         compiler_params=params(),
         name="factor_lead",
-    )(gram)
-
-
-def factor_trail(gram, lead, lead_inv):
+    )(core, own, other)
+
+
+def factor_trail(core, own, other, lead, lead_inv):
     order = lead.shape[0]
     return pl.pallas_call(
         trail_kernel,
         out_shape=(jax.ShapeDtypeStruct((2 * order, 2 * order), F32),) * 2,
-        in_specs=[VMEM] * 3,
+        in_specs=[SMEM] + [VMEM] * 4,
         out_specs=(VMEM,) * 2,
-        scratch_shapes=[pltpu.VMEM((order, 2 * order), F32)],
+        scratch_shapes=[pltpu.VMEM((order, 2 * order), F32)] * 2,
         compiler_params=params(),
         name="factor_trail",
-    )(gram, lead, lead_inv)
-
-
-SOURCES = 2
+    )(core, own, other, lead, lead_inv)
+
+
+SOURCES = 8
 
 
 def basis_kernel(inverse, panel, out):
@@ -484,11 +501,14 @@
     return [(i, (i + shift) % size) for i in range(size)]
 
 
-def summed(value, *axes):
-    for axis in axes:
-        size = lax.axis_size(axis)
-        for level in range(size.bit_length() - 1):
-            value = value + lax.ppermute(value, axis, [(i, i ^ 1 << level) for i in range(size)])
+def swapped(value):
+    return lax.ppermute(value, "core", [(0, 1), (1, 0)])
+
+
+def summed(value, axis, levels):
+    size = lax.axis_size(axis)
+    for level in levels:
+        value = value + lax.ppermute(value, axis, [(i, i ^ 1 << level) for i in range(size)])
     return value
 
 
@@ -496,7 +516,7 @@
     fields, wide, deep, lanes = state_start.shape
     x_size, pieces = lax.axis_size("x"), lax.axis_size("z")
     owner_count = x_size * pieces
-    plane = ("slab", "z")
+    plane = ("y", "core", "z")
     capacity = 2 * viscosity.size // owner_count
     owners = target.reshape(wide * deep, lanes)
 
@@ -530,38 +550,49 @@
     home_one = swap(records_one.reshape(block))
     home_two = swap(records_two.reshape(block))
     hot = rank_hot(owners, owner_count, capacity)
-    high_a, low_a, gram_a = prep(home_one.reshape(-1, lanes), (), fields, HALF)
-    part_a = summed(gram_a, "x")
+    core = lax.axis_index("core").astype(jnp.int32).reshape(1)
+    both = (0, 1)
+    high_a, low_a, keep_a, send_a = prep(core, home_one.reshape(-1, lanes), (), fields, HALF)
+    part_a = summed(keep_a + swapped(send_a), "x", both)
     slots = pack(owners, hot, high_a, low_a, owner_count, 0)
-    high_b, low_b, gram_b = prep(home_two.reshape(-1, lanes), (high_a, low_a), fields, HALF, (slots, part_a))
-    part_a = summed(part_a, "z")
-    part_b = summed(gram_b, "x")
-    slots = pack(owners, hot, high_b, low_b, owner_count, 1, slots)
+    high_b, low_b, keep_b, send_b = prep(
+        core, home_two.reshape(-1, lanes), (high_a, low_a), fields, HALF, (slots, part_a)
+    )
+    part_b = summed(keep_b + swapped(send_b), "x", (0,))
+    slots = pack(owners, hot, high_b, low_b, owner_count, 1, slots, 0, 2)
     slots, part_b = lax.optimization_barrier((slots, part_b))
-    part_b = summed(part_b, "z")
-    slots, part_a, part_b = lax.optimization_barrier((slots, part_a, part_b))
+    part_b = summed(part_b, "x", (1,))
+    slots = pack(owners, hot, high_b, low_b, owner_count, 1, slots, 1, 2)
+    slots, part_b, part_a = lax.optimization_barrier((slots, part_b, part_a))
+    part = summed(jnp.concatenate([part_a, part_b], 1), "z", (0,))
+    part = summed(part, "z", (1,))
+    slots, part = lax.optimization_barrier((slots, part))
     panel = lax.all_to_all(slots, ("x", "z"), split_axis=0, concat_axis=0, tiled=True)
-    lead, lead_inv = factor_lead(summed(part_a, "slab"))
-    r_factor, inverse = factor_trail(summed(part_b, "slab"), lead, lead_inv)
+    part = summed(part, "y", both)
+    other = swapped(part)
+    width = fields * HALF
+    lead, lead_inv = factor_lead(core, part[:, :width], other[:, :width])
+    r_factor, inverse = factor_trail(core, part[:, width:], other[:, width:], lead, lead_inv)
     basis = basis_of(inverse, panel)
     return home_two[:, HALF - 1], r_factor, basis
 
 
 def solution(mesh):
     slab_size, row_size = mesh.shape["slab"], mesh.shape["row"]
-    z_size = 4
-    cut = Mesh(mesh.devices.reshape(slab_size, row_size // z_size, z_size), ("slab", "x", "z"))
-    row = ("x", "z")
+    cores, z_size = 2, 4
+    axes = (slab_size // cores, cores, row_size // z_size, z_size)
+    cut = Mesh(mesh.devices.reshape(axes), ("y", "core", "x", "z"))
+    slab, row = ("y", "core"), ("x", "z")
     placed = (
-        P(None, "slab", row, None),
-        P("slab", row, None),
-        P(None, None, "slab", row, None),
-        P("slab", row, None, None),
+        P(None, slab, row, None),
+        P(slab, row, None),
+        P(None, None, slab, row, None),
+        P(slab, row, None, None),
     )
     return jax.shard_map(
         on_device,
         mesh=cut,
         in_specs=placed,
-        out_specs=(P(None, "slab", row, None), P(), P(("slab",) + row, None)),
+        out_specs=(P(None, slab, row, None), P(), P(slab + row, None)),
         check_vma=False,
     )

time: 199 us -> 194 us (0.975)
  starting transfers between devices: 57.2 us -> 51.7 us
  Pallas kernels: 62.4 us -> 60.4 us
    ppermute x14 -> x8, starting transfers between devices: 14.8 us -> 9.36 us  [summed(): lax.ppermute(value, axis, [(i, i ^ 1 << level) for i in range(size)])]
    pallas_call x1, Pallas kernels: 7.9 us -> 4.97 us  [basis_of(): pl.pallas_call(basis_kernel, grid=(sources // SOURCES,), out_shape=jax.Sh...]
    ppermute x0 -> x3, waiting for transfers between devices: none -> 2.85 us  [swapped(): return lax.ppermute(value, 'core', [(0, 1), (1, 0)])]
    ppermute x14 -> x8, waiting for transfers between devices: 22 us -> 19.5 us  [summed(): lax.ppermute(value, axis, [(i, i ^ 1 << level) for i in range(size)])]
    pallas_call x2 -> x3, Pallas kernels: 12.5 us -> 13.3 us  [pack(): pl.pallas_call(functools.partial(pack_kernel, first), grid=(groups,), out...]
  transfers between devices with their start and end apart: 25 -> 22, of which waited for: 15 -> 18; matrix products, arithmetic and copies ran while one was open for 1% -> 1% of each run, Pallas kernels for 27% -> 28%
where the time goes in v4:
time: 194 us; the launch traced here: 191 us
  waiting for transfers between devices  70.1 us (36%)
  Pallas kernels  60.4 us (31%)
  starting transfers between devices  51.7 us (27%)
  local copies, waits for them, and re-layouts  4.87 us (3%)
  other arithmetic  3.41 us (2%)
    all_to_all x4, starting transfers between devices, swap(): return lax.all_to_all(value, plane, split_axis=0, concat_axis=0, tiled=True)  28.3 us
    ppermute x8, waiting for transfers between devices, summed(): lax.ppermute(value, axis, [(i, i ^ 1 << level) for i in range(size)])  19.5 us
    all_to_all x4, waiting for transfers between devices, swap(): return lax.all_to_all(value, plane, split_axis=0, concat_axis=0, tiled=True)  18.9 us
    pallas_call x1, Pallas kernels, factor_trail(): pl.pallas_call(trail_kernel, out_shape=(jax.ShapeDtypeStruct((2 * order,...  14 us
    pallas_call x3, Pallas kernels, pack(): pl.pallas_call(functools.partial(pack_kernel, first), grid=(groups,), out...  13.3 us
    ppermute x2, waiting for transfers between devices, edges(): high = lax.ppermute(by_row[:, 0], 'x', ring(x_size, -1))  12.5 us
    pallas_call x1, Pallas kernels, factor_lead(): pl.pallas_call(lead_kernel, out_shape=(jax.ShapeDtypeStruct((order, order...  12.4 us
    all_to_all x1, waiting for transfers between devices, on_device(): lax.all_to_all(slots, ('x', 'z'), split_axis=0, concat_axis=0, tiled=True)  11.2 us
  transfers between devices with their start and end apart: 22, of which 18 were waited for; matrix products, arithmetic and copies ran while one was open for 1% of the time, Pallas kernels for 28%

profile of v4, /device:TPU:64, one launch (start us, length us, event | category | flops | bytes accessed | tf_op | source)
XLA Modules:
  0.0 191.4 jit_solution(530161167067675899)
XLA Ops:
  0.6 1.6 copy.27
  4.4 7.8 %all-to-all-start.1 = ((f32[32,5,2,8,128]{4,3,2,1,0:T(8,128)}), f32[32,5,2,8,128]{4,3,2,1,0:T(8,128)S(1)}, u32[]{:S(2)}, u32[]{:S(2)}) async-start(f32[32,5,2,8,128]{4,3,2,1,0:T(8,128)} %pad_maximum_fusion), calls=%async_computation.1 | async-start | bytes 2621440 | tf_op jit(solution)/shard_map/all_to_all | solution.py:524
  13.3 17.1 %all-to-all-done.1 = f32[32,5,2,8,128]{4,3,2,1,0:T(8,128)S(1)} async-done(((f32[32,5,2,8,128]{4,3,2,1,0:T(8,128)}), f32[32,5,2,8,128]{4,3,2,1,0:T(8,128)S(1)}, u32[]{:S(2)}, u32[]{:S(2)}) %all-to-all-start.1) | async-done | bytes 1310752 | tf_op jit(solution)/shard_map/all_to_all | solution.py:524
  30.3 5.6 %all-to-all-start = ((f32[32,4,2,8,128]{4,3,2,1,0:T(8,128)}), f32[32,4,2,8,128]{4,3,2,1,0:T(8,128)S(1)}, u32[]{:S(2)}, u32[]{:S(2)}) async-start(f32[32,4,2,8,128]{4,3,2,1,0:T(8,128)} %slice_convert_fusion), calls=%async_computation | async-start | bytes 2097152 | tf_op jit(solution)/shard_map/all_to_all | solution.py:524
  36.7 2.8 %collective-permute-start.3 = (f32[8,5,2,8,128]{4,3,2,1,0:T(8,128)}, f32[8,5,2,8,128]{4,3,2,1,0:T(8,128)S(1)}, u32[]{:S(2)}, u32[]{:S(2)}) collective-permute-start(f32[8,5,2,8,128]{4,3,2,1,0:T(8,128)} %get-tuple-element.49), channel_id=1, source_target_pairs={{0,12},{4,0},{8,4},{12,8},{1,13},{5,1},{9,5},{13,9},{2,14},{6,2},{... | collective-permute-start | bytes 983048 | tf_op jit(solution)/shard_map/ppermute | solution.py:536
  39.5 7.5 %collective-permute-done.3 = f32[8,5,2,8,128]{4,3,2,1,0:T(8,128)S(1)} collective-permute-done((f32[8,5,2,8,128]{4,3,2,1,0:T(8,128)}, f32[8,5,2,8,128]{4,3,2,1,0:T(8,128)S(1)}, u32[]{:S(2)}, u32[]{:S(2)}) %collective-permute-start.3) | collective-permute-done | bytes 327712 | tf_op jit(solution)/shard_map/ppermute | solution.py:536
  47.1 3.1 %collective-permute-done.2 = f32[8,5,2,8,128]{4,3,2,1,0:T(8,128)S(1)} collective-permute-done((f32[8,5,2,8,128]{4,3,2,1,0:T(8,128)S(1)}, f32[8,5,2,8,128]{4,3,2,1,0:T(8,128)S(1)}, u32[]{:S(2)}, u32[]{:S(2)}) %collective-permute-start.2) | collective-permute-done | bytes 327712 | tf_op jit(solution)/shard_map/ppermute | solution.py:535
  51.9 6.3 %diffuse_first.1 = (f32[2048,128]{1,0:T(8,128)}, f32[32,2,8,128]{3,2,1,0:T(8,128)S(1)}, f32[48,2,8,128]{3,2,1,0:T(8,128)S(1)}) custom-call(s32[2]{0:T(128)S(1)} %add_convert_fusion.edge, f32[2560,128]{1,0:T(8,128)S(1)} %bitcast.43, f32[640,128]{1,0:T(8,128)S(1)} %bitcast.49, f32[640,128]{1,0:T(8,128)S(1)} %bitcast.48), custom_call_target="tpu_custom_call" | custom-call | tf_op jit(solution)/shard_map/diffuse_first/pallas_call | solution.py:215
  58.2 7.5 %all-to-all-start.3 = ((f32[32,4,2,8,128]{4,3,2,1,0:T(8,128)}), f32[32,4,2,8,128]{4,3,2,1,0:T(8,128)S(1)}, u32[]{:S(2)}, u32[]{:S(2)}) async-start(f32[32,4,2,8,128]{4,3,2,1,0:T(8,128)} %bitcast.22), calls=%async_computation.3 | async-start | bytes 2097152 | tf_op jit(solution)/shard_map/all_to_all | solution.py:524
  66.3 1.5 collective-permute-start
  67.8 1.8 collective-permute-start.5
  69.9 4.9 %collective-permute-done.1 = f32[8,4,2,8,128]{4,3,2,1,0:T(8,128)S(1)} collective-permute-done((f32[8,4,2,8,128]{4,3,2,1,0:T(8,128)S(1)}, f32[8,4,2,8,128]{4,3,2,1,0:T(8,128)S(1)}, u32[]{:S(2)}, u32[]{:S(2)}) %collective-permute-start.1) | collective-permute-done | bytes 262176 | tf_op jit(solution)/shard_map/ppermute | solution.py:536
  74.8 1.4 collective-permute-done
  77.0 5.8 %diffuse_second.1 = (f32[2048,128]{1,0:T(8,128)}, f32[32,2,8,128]{3,2,1,0:T(8,128)}) custom-call(f32[2048,128]{1,0:T(8,128)S(1)} %bitcast.45, f32[512,128]{1,0:T(8,128)S(1)} %bitcast.51, f32[512,128]{1,0:T(8,128)S(1)} %bitcast.50, f32[32,2,8,128]{3,2,1,0:T(8,128)S(1)} %get-tuple-element.26.start, f32[8,2,8,128]{3,2,1,0:T(8,128)S(1)} %collective-permute-done.4.start_low, ...), custom_call_target="tpu_custom_call" | custom-call | tf_op jit(solution)/shard_map/diffuse_second/pallas_call | solution.py:232
  82.8 7.5 %all-to-all-start.2 = ((f32[32,4,2,8,128]{4,3,2,1,0:T(8,128)}), f32[32,4,2,8,128]{4,3,2,1,0:T(8,128)S(1)}, u32[]{:S(2)}, u32[]{:S(2)}) async-start(f32[32,4,2,8,128]{4,3,2,1,0:T(8,128)} %bitcast.17), calls=%async_computation.2 | async-start | bytes 2097152 | tf_op jit(solution)/shard_map/all_to_all | solution.py:524
  94.2 2.8 %collective-permute-done.7 = f32[64,128]{1,0:T(8,128)S(1)} collective-permute-done((f32[64,128]{1,0:T(8,128)S(1)}, f32[64,128]{1,0:T(8,128)S(1)}, u32[]{:S(2)}, u32[]{:S(2)}) %collective-permute-start.7) | collective-permute-done | bytes 32800 | tf_op jit(solution)/shard_map/ppermute | solution.py:511
  97.6 6.2 %pack_slots.3.refs_3_.refs_0_ = f32[16,256,256]{2,1,0:T(8,128)} custom-call(s32[16,128]{1,0:T(8,128)S(1)} %bitcast.53, bf16[256,2048]{1,0:T(8,128)(2,1)S(1)} %slot_ranks.1.hot, bf16[128,2048]{1,0:T(8,128)(2,1)S(1)} %get-tuple-element.30.high.refs_1_, bf16[128,2048]{1,0:T(8,128)(2,1)S(1)} %get-tuple-element.31.low.refs_2_), custom_call_target="tpu_custom_call" | custom-call | flops 4294967296 | bytes 2097152 | tf_op jit(solution)/shard_map/pack_slots/pallas_call | solution.py:355
  103.8 1.8 all-to-all-done.2
  105.6 1.6 gram_blocks.3
  109.0 3.5 %pack_slots.4.refs_0_ = f32[16,256,256]{2,1,0:T(8,128)} custom-call(s32[16,128]{1,0:T(8,128)S(1)} %bitcast.54, bf16[256,2048]{1,0:T(8,128)(2,1)S(1)} %slot_ranks.1.hot, bf16[128,2048]{1,0:T(8,128)(2,1)S(1)} %get-tuple-element.34.high, bf16[128,2048]{1,0:T(8,128)(2,1)S(1)} %get-tuple-element.35.low, ...), custom_call_target="tpu_custom_call", output_to_operand_aliasing={{}: (4, {})} | custom-call | flops 2147483648 | bytes 1048576 | tf_op jit(solution)/shard_map/pack_slots/pallas_call | solution.py:355
  114.3 3.5 %pack_slots.5 = f32[16,256,256]{2,1,0:T(8,128)} custom-call(s32[16,128]{1,0:T(8,128)S(1)} %bitcast.55, bf16[256,2048]{1,0:T(8,128)(2,1)S(1)} %slot_ranks.1.hot, bf16[128,2048]{1,0:T(8,128)(2,1)S(1)} %get-tuple-element.34.high, bf16[128,2048]{1,0:T(8,128)(2,1)S(1)} %get-tuple-element.35.low, ...), custom_call_target="tpu_custom_call", output_to_operand_aliasing={{}: (4, {})} | custom-call | flops 2147483648 | bytes 1048576 | tf_op jit(solution)/shard_map/pack_slots/pallas_call | solution.py:355
  120.1 3.4 %collective-permute-done.12 = f32[64,384]{1,0:T(8,128)S(1)} collective-permute-done((f32[64,384]{1,0:T(8,128)S(1)}, f32[64,384]{1,0:T(8,128)S(1)}, u32[]{:S(2)}, u32[]{:S(2)}) %collective-permute-start.12) | collective-permute-done | bytes 98336 | tf_op jit(solution)/shard_map/ppermute | solution.py:511
  123.5 2.1 %collective-permute-start.13 = (f32[64,384]{1,0:T(8,128)S(1)}, f32[64,384]{1,0:T(8,128)S(1)}, u32[]{:S(2)}, u32[]{:S(2)}) collective-permute-start(f32[64,384]{1,0:T(8,128)S(1)} %add.40), channel_id=1, source_target_pairs={{0,2},{1,3},{2,0},{3,1},{4,6},{5,7},{6,4},{7,5},{8,10},{9,11},{10,... | collective-permute-start | bytes 294920 | tf_op jit(solution)/shard_map/ppermute | solution.py:511
  125.6 4.1 %collective-permute-done.13 = f32[64,384]{1,0:T(8,128)S(1)} collective-permute-done((f32[64,384]{1,0:T(8,128)S(1)}, f32[64,384]{1,0:T(8,128)S(1)}, u32[]{:S(2)}, u32[]{:S(2)}) %collective-permute-start.13) | collective-permute-done | bytes 98336 | tf_op jit(solution)/shard_map/ppermute | solution.py:511
  129.8 6.3 %all-to-all-start.4 = ((f32[16,256,256]{2,1,0:T(8,128)}), f32[16,256,256]{2,1,0:T(8,128)}, u32[]{:S(2)}, u32[]{:S(2)}) async-start(f32[16,256,256]{2,1,0:T(8,128)} %pack_slots.5), calls=%async_computation.4 | async-start | bytes 8388608 | tf_op jit(solution)/shard_map/all_to_all | solution.py:570
  136.8 4.2 %collective-permute-done.14 = f32[64,384]{1,0:T(8,128)S(1)} collective-permute-done((f32[64,384]{1,0:T(8,128)S(1)}, f32[64,384]{1,0:T(8,128)S(1)}, u32[]{:S(2)}, u32[]{:S(2)}) %collective-permute-start.14) | collective-permute-done | bytes 98336 | tf_op jit(solution)/shard_map/ppermute | solution.py:511
  141.0 2.6 %collective-permute-start.15 = (f32[64,384]{1,0:T(8,128)S(1)}, f32[64,384]{1,0:T(8,128)S(1)}, u32[]{:S(2)}, u32[]{:S(2)}) collective-permute-start(f32[64,384]{1,0:T(8,128)S(1)} %add.42), channel_id=1, source_target_pairs={{0,64},{32,96},{64,0},{96,32},{1,65},{33,97},{65,1},{97,33},{2,66}... | collective-permute-start | bytes 294920 | tf_op jit(solution)/shard_map/ppermute | solution.py:511
  143.6 3.6 %collective-permute-done.15 = f32[64,384]{1,0:T(8,128)S(1)} collective-permute-done((f32[64,384]{1,0:T(8,128)S(1)}, f32[64,384]{1,0:T(8,128)S(1)}, u32[]{:S(2)}, u32[]{:S(2)}) %collective-permute-start.15) | collective-permute-done | bytes 98336 | tf_op jit(solution)/shard_map/ppermute | solution.py:511
  148.8 12.4 %factor_lead.1 = (f32[128,128]{1,0:T(8,128)S(1)}, f32[128,128]{1,0:T(8,128)S(1)}) custom-call(s32[1]{0:T(128)} %bitcast.19.core, f32[64,128]{1,0:T(8,128)S(1)} %slice.65.own, f32[64,128]{1,0:T(8,128)S(1)} %slice.66.other), custom_call_target="tpu_custom_call" | custom-call | tf_op jit(solution)/shard_map/factor_lead/pallas_call | solution.py:447
  161.3 14.0 %factor_trail.1 = (f32[256,256]{1,0:T(8,128)}, f32[256,256]{1,0:T(8,128)S(1)}) custom-call(s32[1]{0:T(128)} %bitcast.19.core, f32[64,256]{1,0:T(8,128)S(1)} %slice.63.own_half, f32[64,256]{1,0:T(8,128)S(1)} %slice.64.other_half, f32[128,128]{1,0:T(8,128)S(1)} %get-tuple-element.44.lead, f32[128,128]{1,0:T(8,128)S(1)} %get-tuple-element.45.lead_inv), custom_call_target="tpu_custom_call" | custom-call | tf_op jit(solution)/shard_map/factor_trail/pallas_call | solution.py:460
  175.2 11.2 %all-to-all-done.4.panel = f32[16,256,256]{2,1,0:T(8,128)} async-done(((f32[16,256,256]{2,1,0:T(8,128)}), f32[16,256,256]{2,1,0:T(8,128)}, u32[]{:S(2)}, u32[]{:S(2)}) %all-to-all-start.4) | async-done | bytes 4194336 | tf_op jit(solution)/shard_map/all_to_all | solution.py:570
  186.4 5.0 %basis_rows.1 = f32[4096,256]{1,0:T(8,128)} custom-call(f32[256,256]{1,0:T(8,128)S(1)} %get-tuple-element.47.inverse, f32[16,256,256]{2,1,0:T(8,128)} %all-to-all-done.4.panel), custom_call_target="tpu_custom_call" | custom-call | tf_op jit(solution)/shard_map/basis_rows/pallas_call | solution.py:486
  (60 shorter events, 20.1 us)
Async XLA Ops:
  0.6 1.6 copy-start.3
  2.2 1.0 copy-start.4
  4.4 25.9 %all-to-all-start.1 = ((f32[32,5,2,8,128]{4,3,2,1,0:T(8,128)}), f32[32,5,2,8,128]{4,3,2,1,0:T(8,128)S(1)}, u32[]{:S(2)}, u32[]{:S(2)}) async-start(f32[32,5,2,8,128]{4,3,2,1,0:T(8,128)} %pad_maximum_fusion), calls=%async_computation.1 | async-start | bytes 2621440 | tf_op jit(solution)/shard_map/all_to_all | solution.py:524
  30.3 27.8 %all-to-all-start = ((f32[32,4,2,8,128]{4,3,2,1,0:T(8,128)}), f32[32,4,2,8,128]{4,3,2,1,0:T(8,128)S(1)}, u32[]{:S(2)}, u32[]{:S(2)}) async-start(f32[32,4,2,8,128]{4,3,2,1,0:T(8,128)} %slice_convert_fusion), calls=%async_computation | async-start | bytes 2097152 | tf_op jit(solution)/shard_map/all_to_all | solution.py:524
  36.7 10.4 %collective-permute-start.3 = (f32[8,5,2,8,128]{4,3,2,1,0:T(8,128)}, f32[8,5,2,8,128]{4,3,2,1,0:T(8,128)S(1)}, u32[]{:S(2)}, u32[]{:S(2)}) collective-permute-start(f32[8,5,2,8,128]{4,3,2,1,0:T(8,128)} %get-tuple-element.49), channel_id=1, source_target_pairs={{0,12},{4,0},{8,4},{12,8},{1,13},{5,1},{9,5},{13,9},{2,14},{6,2},{... | collective-permute-start | bytes 983048 | tf_op jit(solution)/shard_map/ppermute | solution.py:536
  39.5 10.7 %collective-permute-start.2 = (f32[8,5,2,8,128]{4,3,2,1,0:T(8,128)S(1)}, f32[8,5,2,8,128]{4,3,2,1,0:T(8,128)S(1)}, u32[]{:S(2)}, u32[]{:S(2)}) collective-permute-start(f32[8,5,2,8,128]{4,3,2,1,0:T(8,128)S(1)} %get-tuple-element.50), channel_id=1, source_target_pairs={{0,4},{4,8},{8,12},{12,0},{1,5},{5,9},{9,13},{13,1},{2,6},{6,10},{... | collective-permute-start | bytes 983048 | tf_op jit(solution)/shard_map/ppermute | solution.py:535
  50.2 0.7 copy-start
  50.9 1.0 copy-start.1
  58.2 24.6 %all-to-all-start.3 = ((f32[32,4,2,8,128]{4,3,2,1,0:T(8,128)}), f32[32,4,2,8,128]{4,3,2,1,0:T(8,128)S(1)}, u32[]{:S(2)}, u32[]{:S(2)}) async-start(f32[32,4,2,8,128]{4,3,2,1,0:T(8,128)} %bitcast.22), calls=%async_computation.3 | async-start | bytes 2097152 | tf_op jit(solution)/shard_map/all_to_all | solution.py:524
  65.7 9.1 %collective-permute-start.1 = (f32[8,4,2,8,128]{4,3,2,1,0:T(8,128)S(1)}, f32[8,4,2,8,128]{4,3,2,1,0:T(8,128)S(1)}, u32[]{:S(2)}, u32[]{:S(2)}) collective-permute-start(f32[8,4,2,8,128]{4,3,2,1,0:T(8,128)S(1)} %get-tuple-element.51), channel_id=1, source_target_pairs={{0,12},{4,0},{8,4},{12,8},{1,13},{5,1},{9,5},{13,9},{2,14},{6,2},{... | collective-permute-start | bytes 786440 | tf_op jit(solution)/shard_map/ppermute | solution.py:536
  66.3 10.0 %collective-permute-start = (f32[8,4,2,8,128]{4,3,2,1,0:T(8,128)S(1)}, f32[8,4,2,8,128]{4,3,2,1,0:T(8,128)S(1)}, u32[]{:S(2)}, u32[]{:S(2)}) collective-permute-start(f32[8,4,2,8,128]{4,3,2,1,0:T(8,128)S(1)} %get-tuple-element.52), channel_id=1, source_target_pairs={{0,4},{4,8},{8,12},{12,0},{1,5},{5,9},{9,13},{13,1},{2,6},{6,10},{... | collective-permute-start | bytes 786440 | tf_op jit(solution)/shard_map/ppermute | solution.py:535
  67.8 8.5 %collective-permute-start.5 = (f32[8,2,8,128]{3,2,1,0:T(8,128)S(1)}, f32[8,2,8,128]{3,2,1,0:T(8,128)S(1)}, u32[]{:S(2)}, u32[]{:S(2)}) collective-permute-start(f32[8,2,8,128]{3,2,1,0:T(8,128)S(1)} %get-tuple-element.53), channel_id=1, source_target_pairs={{0,12},{4,0},{8,4},{12,8},{1,13},{5,1},{9,5},{13,9},{2,14},{6,2},{... | collective-permute-start | bytes 196616 | tf_op jit(solution)/shard_map/ppermute | solution.py:545
  69.6 7.4 %collective-permute-start.4 = (f32[8,2,8,128]{3,2,1,0:T(8,128)S(1)}, f32[8,2,8,128]{3,2,1,0:T(8,128)S(1)}, u32[]{:S(2)}, u32[]{:S(2)}) collective-permute-start(f32[8,2,8,128]{3,2,1,0:T(8,128)S(1)} %get-tuple-element.54), channel_id=1, source_target_pairs={{0,4},{4,8},{8,12},{12,0},{1,5},{5,9},{9,13},{13,1},{2,6},{6,10},{... | collective-permute-start | bytes 196616 | tf_op jit(solution)/shard_map/ppermute | solution.py:544
  82.8 10.5 %copy-start.2 = (s32[1,1,2048,1]{2,3,1,0:T(1,128)S(1)}, s32[1,1,2048,1]{2,3,1,0:T(1,128)}, u32[]{:S(2)}) copy-start(s32[1,1,2048,1]{2,3,1,0:T(1,128)} %param.7) | copy-start | bytes 24580
  82.8 22.9 %all-to-all-start.2 = ((f32[32,4,2,8,128]{4,3,2,1,0:T(8,128)}), f32[32,4,2,8,128]{4,3,2,1,0:T(8,128)S(1)}, u32[]{:S(2)}, u32[]{:S(2)}) async-start(f32[32,4,2,8,128]{4,3,2,1,0:T(8,128)} %bitcast.17), calls=%async_computation.2 | async-start | bytes 2097152 | tf_op jit(solution)/shard_map/all_to_all | solution.py:524
  91.5 1.5 collective-permute-start.6
  93.0 3.9 %collective-permute-start.7 = (f32[64,128]{1,0:T(8,128)S(1)}, f32[64,128]{1,0:T(8,128)S(1)}, u32[]{:S(2)}, u32[]{:S(2)}) collective-permute-start(f32[64,128]{1,0:T(8,128)S(1)} %add.34), channel_id=1, source_target_pairs={{0,4},{4,0},{8,12},{12,8},{1,5},{5,1},{9,13},{13,9},{2,6},{6,2},{1... | collective-permute-start | bytes 98312 | tf_op jit(solution)/shard_map/ppermute | solution.py:511
  96.9 6.9 %collective-permute-start.8 = (f32[64,128]{1,0:T(8,128)S(1)}, f32[64,128]{1,0:T(8,128)S(1)}, u32[]{:S(2)}, u32[]{:S(2)}) collective-permute-start(f32[64,128]{1,0:T(8,128)S(1)} %add.35), channel_id=1, source_target_pairs={{0,8},{4,12},{8,0},{12,4},{1,9},{5,13},{9,1},{13,5},{2,10},{6,14},... | collective-permute-start | bytes 98312 | tf_op jit(solution)/shard_map/ppermute | solution.py:511
  107.2 1.3 collective-permute-start.9
  108.6 4.3 %collective-permute-start.10 = (f32[64,256]{1,0:T(8,128)S(1)}, f32[64,256]{1,0:T(8,128)S(1)}, u32[]{:S(2)}, u32[]{:S(2)}) collective-permute-start(f32[64,256]{1,0:T(8,128)S(1)} %add.37), channel_id=1, source_target_pairs={{0,4},{4,0},{8,12},{12,8},{1,5},{5,1},{9,13},{13,9},{2,6},{6,2},{1... | collective-permute-start | bytes 196616 | tf_op jit(solution)/shard_map/ppermute | solution.py:511
  112.9 5.8 %collective-permute-start.11 = (f32[64,256]{1,0:T(8,128)S(1)}, f32[64,256]{1,0:T(8,128)S(1)}, u32[]{:S(2)}, u32[]{:S(2)}) collective-permute-start(f32[64,256]{1,0:T(8,128)S(1)} %add.38), channel_id=1, source_target_pairs={{0,8},{4,12},{8,0},{12,4},{1,9},{5,13},{9,1},{13,5},{2,10},{6,14},... | collective-permute-start | bytes 196616 | tf_op jit(solution)/shard_map/ppermute | solution.py:511
  118.8 4.7 %collective-permute-start.12 = (f32[64,384]{1,0:T(8,128)S(1)}, f32[64,384]{1,0:T(8,128)S(1)}, u32[]{:S(2)}, u32[]{:S(2)}) collective-permute-start(f32[64,384]{1,0:T(8,128)S(1)} %constant_dynamic-update-slice_fusion), channel_id=1, source_target_pairs={{0,1},{1,0},{2,3},{3,2},{4,5},{5,4},{6,7},{7,6},{8,9},{9,8},{10,11... | collective-permute-start | bytes 294920 | tf_op jit(solution)/shard_map/ppermute | solution.py:511
  123.5 6.2 %collective-permute-start.13 = (f32[64,384]{1,0:T(8,128)S(1)}, f32[64,384]{1,0:T(8,128)S(1)}, u32[]{:S(2)}, u32[]{:S(2)}) collective-permute-start(f32[64,384]{1,0:T(8,128)S(1)} %add.40), channel_id=1, source_target_pairs={{0,2},{1,3},{2,0},{3,1},{4,6},{5,7},{6,4},{7,5},{8,10},{9,11},{10,... | collective-permute-start | bytes 294920 | tf_op jit(solution)/shard_map/ppermute | solution.py:511
  129.8 56.7 %all-to-all-start.4 = ((f32[16,256,256]{2,1,0:T(8,128)}), f32[16,256,256]{2,1,0:T(8,128)}, u32[]{:S(2)}, u32[]{:S(2)}) async-start(f32[16,256,256]{2,1,0:T(8,128)} %pack_slots.5), calls=%async_computation.4 | async-start | bytes 8388608 | tf_op jit(solution)/shard_map/all_to_all | solution.py:570
  136.1 4.9 %collective-permute-start.14 = (f32[64,384]{1,0:T(8,128)S(1)}, f32[64,384]{1,0:T(8,128)S(1)}, u32[]{:S(2)}, u32[]{:S(2)}) collective-permute-start(f32[64,384]{1,0:T(8,128)S(1)} %add.41), channel_id=1, source_target_pairs={{0,32},{32,0},{64,96},{96,64},{1,33},{33,1},{65,97},{97,65},{2,34}... | collective-permute-start | bytes 294920 | tf_op jit(solution)/shard_map/ppermute | solution.py:511
  141.0 6.2 %collective-permute-start.15 = (f32[64,384]{1,0:T(8,128)S(1)}, f32[64,384]{1,0:T(8,128)S(1)}, u32[]{:S(2)}, u32[]{:S(2)}) collective-permute-start(f32[64,384]{1,0:T(8,128)S(1)} %add.42), channel_id=1, source_target_pairs={{0,64},{32,96},{64,0},{96,32},{1,65},{33,97},{65,1},{97,33},{2,66}... | collective-permute-start | bytes 294920 | tf_op jit(solution)/shard_map/ppermute | solution.py:511
  147.2 1.6 collective-permute-start.16

commit v5 on v4

--- a/solution.py
+++ b/solution.py
@@ -10,7 +10,6 @@
 SNAPS = 8
 STEPS = 2
 HALF = SNAPS // 2
-DEEP = HALF * STEPS
 ROWS = 8
 step_size = 0.08
 F32 = jnp.float32
@@ -35,6 +34,16 @@
     return lax.dot_general(left, right, dims, preferred_element_type=F32)
 
 
+SIDE = HALF * STEPS
+VMEM = pl.BlockSpec(memory_space=pltpu.VMEM)
+SMEM = pl.BlockSpec(memory_space=pltpu.SMEM)
+HBM = pl.BlockSpec(memory_space=pltpu.HBM)
+
+
+def params(size=8):
+    return pltpu.CompilerParams(vmem_limit_bytes=size * 1024 * 1024)
+
+
 def lane_next(value):
     return pltpu.roll(value, value.shape[-1] - 1, value.ndim - 1)
 
@@ -43,204 +52,314 @@
     return pltpu.roll(value, 1, value.ndim - 1)
 
 
-def make_coefs(visc, coefs, rows):
+def reader(main, low, high, heights, pieces):
+    blocks = len(heights)
+    rows = sum(heights)
+    own = 8 * pieces
+
+    def read(block, y, i):
+        y -= SIDE
+        if 0 <= y < own:
+            z, j = divmod(y, 8)
+            start = (z * blocks + block) * 16 + i * 8 + j
+            return main[pl.ds(start, 8, stride=pieces * blocks * 16), :]
+        first = i * rows + sum(heights[:block])
+        if y < 0:
+            return low[pl.ds(first + heights[block] + y, 8, stride=2 * rows), :]
+        return high[pl.ds(first + y - own, 8, stride=2 * rows), :]
+
+    return read
+
+
+def row_coefs(visc, y, with_rest, store):
     half = 0.5 * step_size
     slab = lax.broadcasted_iota(jnp.int32, (8, 128), 0)
-
-    def row_body(y, carry):
-        v0, v1 = visc[y, 0], visc[y, 1]
-        pair = half * (v0 + v1)
-        up = jnp.where(slab < 7, pltpu.roll(v0, 7, 0), 0.0)
-        cross_up = half * (v1 + up)
-        down = jnp.where(slab > 0, pltpu.roll(v1, 1, 0), 0.0)
-        cross_down = half * (v0 + down)
-        for i, v, cross in ((0, v0, cross_down), (1, v1, cross_up)):
-            nxt, prv = visc[y + 1, i], visc[y - 1, i]
+    here = [visc(y, 0), visc(y, 1)]
+    if with_rest:
+        pair = half * (here[0] + here[1])
+        up = jnp.where(slab < 7, pltpu.roll(here[0], 7, 0), 0.0)
+        down = jnp.where(slab > 0, pltpu.roll(here[1], 1, 0), 0.0)
+        crosses = (half * (here[0] + down), half * (here[1] + up))
+    for i in range(2):
+        v, nxt = here[i], visc(y + 1, i)
+        inside = v > 0.0
+        to_next = half * (v + nxt)
+        store(1, y, i, jnp.where(inside & (nxt > 0.0), to_next, 0.0))
+        if with_rest:
             z_next = half * (v + lane_next(v))
             z_prev = lane_prev(z_next)
-            to_next = half * (v + nxt)
-            to_prev = half * (v + prv)
-            total = to_next + to_prev + pair + cross + z_next + z_prev
-            inside = v > 0.0
-            coefs[0, y, i] = jnp.where(inside, 1.0 - total, 0.0)
-            coefs[1, y, i] = jnp.where(inside & (nxt > 0.0), to_next, 0.0)
-            coefs[2, y, i] = jnp.where(inside, pair, 0.0)
-            wall = (slab == 0) if i == 0 else (slab == 7)
-            coefs[3, y, i] = jnp.where(inside & ~wall, cross, 0.0)
-            coefs[4, y, i] = jnp.where(inside, z_next, 0.0)
-            coefs[5, y, i] = jnp.where(inside, z_prev, 0.0)
-        return carry
-
-    v0, v1 = visc[0, 0], visc[0, 1]
-    for i, v in ((0, v0), (1, v1)):
-        nxt = visc[1, i]
-        coefs[1, 0, i] = jnp.where((v > 0.0) & (nxt > 0.0), half * (v + nxt), 0.0)
-    lax.fori_loop(1, rows - 1, row_body, 0, unroll=6)
-
-
-def diffuse(source, dest, coefs, low, high, plus=None):
-    def block_body(block, carry):
-        base = low + block * ROWS
-        u = [[source[base - 1 + r, i] for i in range(2)] for r in range(ROWS + 2)]
-        face = [[coefs[1, base - 1 + r, i] for i in range(2)] for r in range(ROWS + 1)]
-        for r in range(1, ROWS + 1):
-            y = base - 1 + r
-            for i in range(2):
-                mine, other = u[r][i], u[r][1 - i]
-                cross = pltpu.roll(other, 1 if i == 0 else 7, 0)
-                total = (coefs[0, y, i] * mine + coefs[2, y, i] * other) + (
-                    face[r][i] * u[r + 1][i] + face[r - 1][i] * u[r - 1][i]
-                )
-                total = total + (
-                    (coefs[4, y, i] * lane_next(mine) + coefs[5, y, i] * lane_prev(mine))
-                    + coefs[3, y, i] * cross
-                )
-                dest[y, i] = total
-        return carry
-
-    lax.fori_loop(0, (high - low + ROWS - 1) // ROWS, block_body, 0, unroll=True)
-
-
-def run_steps(fields, forcing, coefs, pieces, own, snaps, records, last):
-    rows = own + 2 * snaps * STEPS
-    side = snaps * STEPS
+            total = to_next + half * (v + visc(y - 1, i)) + pair + crosses[i] + z_next + z_prev
+            wall = slab == (0 if i == 0 else 7)
+            store(0, y, i, jnp.where(inside, 1.0 - total, 0.0))
+            store(2, y, i, jnp.where(inside, pair, 0.0))
+            store(3, y, i, jnp.where(inside & ~wall, crosses[i], 0.0))
+            store(4, y, i, jnp.where(inside, z_next, 0.0))
+            store(5, y, i, jnp.where(inside, z_prev, 0.0))
+
+
+def own_coefs_kernel(pieces, blocks, main, coefs):
+    own = 8 * pieces
+    read = reader(main, None, None, (0,) * blocks, pieces)
+    cache = {}
+
+    def visc(y, i):
+        if (y, i) not in cache:
+            cache[y, i] = read(0, y, i)
+        return cache[y, i]
+
+    def store(c, y, i, value):
+        coefs[c, y - SIDE, i] = value
+
+    for y in range(SIDE + 1, SIDE + own - 1):
+        row_coefs(visc, y, True, store)
+
+
+def edge_coefs(edge_visc, pieces, edge):
+    own = 8 * pieces
+    cache = {}
+
+    def visc(y, i):
+        if (y, i) not in cache:
+            cache[y, i] = edge_visc[y if y <= SIDE + 1 else y - own + 4, i]
+        return cache[y, i]
+
+    def store(c, y, i, value):
+        edge[c, y if y <= SIDE else y - own + 2, i] = value
+
+    for y in range(0, SIDE + 1):
+        row_coefs(visc, y, y > 0, store)
+    for y in range(SIDE + own - 1, 2 * SIDE + own - 1):
+        row_coefs(visc, y, True, store)
+
+
+def run_steps(read, blocks, fields, own_coefs, edge, pieces, snaps, records, last, kept, sems):
+    own = 8 * pieces
+    rows = own + 2 * SIDE
+
+    def coef(c, y, i):
+        if SIDE < y < SIDE + own - 1:
+            return own_coefs[c, y - SIDE, i]
+        return edge[c, y if y <= SIDE else y - own + 2, i]
+
+    def diffuse(source, dest, low, high):
+        for base in range(low, high, ROWS):
+            top = min(base + ROWS, high)
+            u = {(y, i): source[y, i] for y in range(base - 1, top + 1) for i in range(2)}
+            face = {(y, i): coef(1, y, i) for y in range(base - 1, top) for i in range(2)}
+            for y in range(base, top):
+                for i in range(2):
+                    mine, other = u[y, i], u[y, 1 - i]
+                    cross = pltpu.roll(other, 1 if i == 0 else 7, 0)
+                    total = (coef(0, y, i) * mine + coef(2, y, i) * other) + (
+                        face[y, i] * u[y + 1, i] + face[y - 1, i] * u[y - 1, i]
+                    )
+                    total = total + (
+                        (coef(4, y, i) * lane_next(mine) + coef(5, y, i) * lane_prev(mine))
+                        + coef(3, y, i) * cross
+                    )
+                    dest[y, i] = total
+
     done = 0
+    copies = []
     for k in range(snaps):
         first = fields[0]
         if k:
-
-            def add_body(y, carry):
-                first[y, 0] = first[y, 0] + forcing[k - 1, y, 0]
-                first[y, 1] = first[y, 1] + forcing[k - 1, y, 1]
-                return carry
-
-            lax.fori_loop(done, rows - done, add_body, 0, unroll=4)
+            for y in range(done, rows - done):
+                for i in range(2):
+                    first[y, i] = first[y, i] + read(blocks[k], y, i)
         for step in range(STEPS):
             done += 1
-            diffuse(fields[step % 2], fields[(step + 1) % 2], coefs, done, rows - done)
+            diffuse(fields[step % 2], fields[(step + 1) % 2], done, rows - done)
         for y in range(own):
             z, j = divmod(y, 8)
             for i in range(2):
-                value = first[side + y, i]
-                records[pl.ds((z * snaps + k) * 16 + i * 8 + j, 8, stride=pieces * snaps * 16), :] = value
-                if k == snaps - 1:
+                value = first[SIDE + y, i]
+                kept[pl.ds((z * snaps + k) * 16 + i * 8 + j, 8, stride=pieces * snaps * 16), :] = value
+                if last is not None and k == snaps - 1:
                     last[y, i] = value
-
-
-def collect(main, low, high, blocks, pieces, block, store):
-    for i in range(2):
-        for j in range(8):
-            at = block * 16 + i * 8 + j
-            store(j, i, low[pl.ds(at, 8, stride=blocks * 16), :])
-            store(8 + 8 * pieces + j, i, high[pl.ds(at, 8, stride=blocks * 16), :])
-            for z in range(pieces):
-                start = (z * blocks + block) * 16 + i * 8 + j
-                store(8 + 8 * z + j, i, main[pl.ds(start, 8, stride=pieces * blocks * 16), :])
-
-
-def first_kernel(pieces, snaps, edge, main, low, high, records, last, visc_out, buf0, buf1, forcing, coefs):
+        blocks_of = (8 * pieces, snaps, 16, 128)
+        copies.append(
+            pltpu.make_async_copy(
+                kept.reshape(*blocks_of).at[:, k], records.at[:, k], sems.at[k]
+            )
+        )
+        copies[-1].start()
+    for copy in copies:
+        copy.wait()
+
+
+def first_kernel(
+    pieces, heights, around, main, low_from, high_from, own_coefs, records, last, edge_visc, buf0, buf1, kept, sems, edge, low, high, edge_sems
+):
+    arriving = [
+        pltpu.make_async_copy(low_from, low, edge_sems.at[0]),
+        pltpu.make_async_copy(high_from, high, edge_sems.at[1]),
+    ]
+    for copy in arriving:
+        copy.start()
+    read = reader(main, low, high, heights, pieces)
+    has_low = jnp.where(around[0] > 0, 1.0, 0.0)
+    has_high = jnp.where(around[1] > 0, 1.0, 0.0)
     own = 8 * pieces
-    rows = own + 2 * snaps * STEPS
-    blocks = snaps + 1
-    has_low = jnp.where(edge[0] > 0, 1.0, 0.0)
-    has_high = jnp.where(edge[1] > 0, 1.0, 0.0)
-
-    def put_visc(y, i, value):
-        if y < 8:
-            value = value * has_low
-        elif y >= 8 + own:
-            value = value * has_high
-        visc_out[y, i] = value
-
-    collect(main, low, high, blocks, pieces, 0, put_visc)
-
-    def put_start(y, i, value):
-        buf0[y, i] = value
-
-    collect(main, low, high, blocks, pieces, 1, put_start)
-    for k in range(1, snaps):
-
-        def put_force(y, i, value, k=k):
-            forcing[k - 1, y, i] = value
-
-        collect(main, low, high, blocks, pieces, k + 1, put_force)
-    make_coefs(visc_out, coefs, rows)
-    run_steps((buf0, buf1), forcing, coefs, pieces, own, snaps, records, last)
-
-
-def second_kernel(pieces, snaps, main, low, high, start, start_low, start_high, visc, records, last, buf0, buf1, forcing, coefs):
+    for y in range(SIDE, SIDE + own):
+        for i in range(2):
+            buf0[y, i] = read(1, y, i)
+    for copy in arriving:
+        copy.wait()
+    for y in list(range(SIDE)) + list(range(SIDE + own, own + 2 * SIDE)):
+        for i in range(2):
+            buf0[y, i] = read(1, y, i)
+    for y in list(range(SIDE + 2)) + list(range(SIDE + own - 2, own + 2 * SIDE)):
+        for i in range(2):
+            value = read(0, y, i)
+            if y < SIDE:
+                value = value * has_low
+            elif y >= SIDE + own:
+                value = value * has_high
+            edge_visc[y if y <= SIDE + 1 else y - own + 4, i] = value
+    edge_coefs(edge_visc, pieces, edge)
+    snaps = len(heights) - 1
+    run_steps(read, range(1, snaps + 1), (buf0, buf1), own_coefs, edge, pieces, snaps, records, last, kept, sems)
+
+
+def second_kernel(pieces, heights, main, low, high, start, start_low, start_high, own_coefs, edge_visc, records, buf0, buf1, kept, sems, edge):
+    read = reader(main, low, high, heights, pieces)
     own = 8 * pieces
-    rows = own + 2 * snaps * STEPS
-    blocks = snaps
-
-    def put_start(y, i, value):
-        if y < 8:
-            buf0[y, i] = value + start_low[y, i]
-        elif y >= 8 + own:
-            buf0[y, i] = value + start_high[y - 8 - own, i]
-        else:
-            buf0[y, i] = value + start[y - 8, i]
-
-    collect(main, low, high, blocks, pieces, 0, put_start)
-    for k in range(1, snaps):
-
-        def put_force(y, i, value, k=k):
-            forcing[k - 1, y, i] = value
-
-        collect(main, low, high, blocks, pieces, k, put_force)
-    make_coefs(visc, coefs, rows)
-    run_steps((buf0, buf1), forcing, coefs, pieces, own, snaps, records, last)
-
-
-VMEM = pl.BlockSpec(memory_space=pltpu.VMEM)
-SMEM = pl.BlockSpec(memory_space=pltpu.SMEM)
-
-
-def params(size=48):
-    return pltpu.CompilerParams(vmem_limit_bytes=size * 1024 * 1024)
-
-
-def step_scratch(rows, snaps):
-    padded = rows + ROWS
-    return [
-        pltpu.VMEM((padded, 2, 8, 128), F32),
-        pltpu.VMEM((padded, 2, 8, 128), F32),
-        pltpu.VMEM((snaps - 1, rows, 2, 8, 128), F32),
-        pltpu.VMEM((6, padded, 2, 8, 128), F32),
+    for y in range(own + 2 * SIDE):
+        for i in range(2):
+            if y < SIDE:
+                before = start_low[y, i]
+            elif y >= SIDE + own:
+                before = start_high[y - SIDE - own, i]
+            else:
+                before = start[y - SIDE, i]
+            buf0[y, i] = before + read(0, y, i)
+    edge_coefs(edge_visc, pieces, edge)
+    snaps = len(heights)
+    run_steps(read, range(snaps), (buf0, buf1), own_coefs, edge, pieces, snaps, records, None, kept, sems)
+
+
+def own_coefs_of(main, pieces, blocks):
+    return pl.pallas_call(
+        functools.partial(own_coefs_kernel, pieces, blocks),
+        out_shape=jax.ShapeDtypeStruct((6, 8 * pieces, 2, 8, 128), F32),
+        in_specs=[VMEM],
+        out_specs=VMEM,
+        compiler_params=params(4),
+        name="own_coefficients",
+    )(main)
+
+
+def buffers(pieces, snaps):
+    return [pltpu.VMEM((8 * pieces + 2 * SIDE, 2, 8, 128), F32)] * 2 + [
+        pltpu.VMEM((8 * pieces * snaps * 16, 128), F32),
+        pltpu.SemaphoreType.DMA((snaps,)),
+        pltpu.VMEM((6, 2 * SIDE + 2, 2, 8, 128), F32),
     ]
 
 
-def first_half(edge, main, low, high, pieces, snaps):
-    rows = 8 * pieces + 2 * snaps * STEPS
-    return pl.pallas_call(
-        functools.partial(first_kernel, pieces, snaps),
+def first_half(around, main, low, high, own_coefs, pieces, heights):
+    snaps = len(heights) - 1
+    return pl.pallas_call(
+        functools.partial(first_kernel, pieces, heights),
         out_shape=(
-            jax.ShapeDtypeStruct((8 * pieces * snaps * 16, 128), F32),
+            jax.ShapeDtypeStruct((8 * pieces, snaps, 16, 128), F32),
             jax.ShapeDtypeStruct((8 * pieces, 2, 8, 128), F32),
-            jax.ShapeDtypeStruct((rows, 2, 8, 128), F32),
+            jax.ShapeDtypeStruct((2 * SIDE + 4, 2, 8, 128), F32),
         ),
-        in_specs=[SMEM, VMEM, VMEM, VMEM],
-        out_specs=(VMEM, VMEM, VMEM),
-        scratch_shapes=step_scratch(rows, snaps),
-        compiler_params=params(),
+        in_specs=[SMEM, VMEM, HBM, HBM, VMEM],
+        out_specs=(HBM, VMEM, VMEM),
+        scratch_shapes=buffers(pieces, snaps)
+        + [pltpu.VMEM(low.shape, F32), pltpu.VMEM(high.shape, F32), pltpu.SemaphoreType.DMA((2,))],
+        compiler_params=params(6),
         name="diffuse_first",
-    )(edge, main, low, high)
-
-
-def second_half(main, low, high, start, start_low, start_high, visc, pieces, snaps):
-    rows = 8 * pieces + 2 * snaps * STEPS
-    return pl.pallas_call(
-        functools.partial(second_kernel, pieces, snaps),
-        out_shape=(
-            jax.ShapeDtypeStruct((8 * pieces * snaps * 16, 128), F32),
-            jax.ShapeDtypeStruct((8 * pieces, 2, 8, 128), F32),
-        ),
-        in_specs=[VMEM] * 7,
-        out_specs=(VMEM, VMEM),
-        scratch_shapes=step_scratch(rows, snaps),
-        compiler_params=params(),
+    )(around, main, low, high, own_coefs)
+
+
+def second_half(main, low, high, start, start_low, start_high, own_coefs, edge, pieces, heights):
+    snaps = len(heights)
+    return pl.pallas_call(
+        functools.partial(second_kernel, pieces, heights),
+        out_shape=jax.ShapeDtypeStruct((8 * pieces, snaps, 16, 128), F32),
+        in_specs=[VMEM] * 8,
+        out_specs=HBM,
+        scratch_shapes=buffers(pieces, snaps),
+        compiler_params=params(6),
         name="diffuse_second",
-    )(main, low, high, start, start_low, start_high, visc)
+    )(main, low, high, start, start_low, start_high, own_coefs, edge)
+
+
+def edge_kernel(pieces, heights, main, last_rows, first_rows):
+    blocks, rows = len(heights), sum(heights)
+    for a in range(8):
+        for i in range(2):
+            at = (a * 2 + i) * rows
+            for k, height in enumerate(heights):
+                first = (a * pieces * blocks + k) * 16 + i * 8
+                last = first + (pieces - 1) * blocks * 16
+                first_rows[at : at + height, :] = main[first : first + height, :]
+                last_rows[at : at + height, :] = main[last + 8 - height : last + 8, :]
+                at += height
+
+
+def edges_of(main, pieces, heights):
+    return pl.pallas_call(
+        functools.partial(edge_kernel, pieces, heights),
+        out_shape=(jax.ShapeDtypeStruct((16 * sum(heights), 128), F32),) * 2,
+        in_specs=[VMEM],
+        out_specs=(VMEM,) * 2,
+        compiler_params=params(4),
+        name="edge_rows",
+    )(main)
+
+
+def opening_kernel(visc_from, start_from, forcing_from, out_to, visc, start, forcing, out, in_sems, out_sems):
+    snaps, fields = forcing.shape[:2]
+    arriving = [
+        pltpu.make_async_copy(visc_from, visc, in_sems.at[snaps + 1]),
+        pltpu.make_async_copy(start_from, start, in_sems.at[snaps]),
+    ]
+    arriving += [pltpu.make_async_copy(forcing_from.at[k], forcing.at[k], in_sems.at[k]) for k in range(snaps)]
+    for copy in arriving:
+        copy.start()
+    leaving = [
+        pltpu.make_async_copy(out.at[:, k], out_to.at[:, k], out_sems.at[k]) for k in range(snaps + 1)
+    ]
+    arriving[0].wait()
+    value = visc[...]
+    for f in range(fields):
+        out[f, 0] = value
+    leaving[0].start()
+    arriving[1].wait()
+    for k in range(snaps):
+        arriving[2 + k].wait()
+        for f in range(fields):
+            value = forcing[k, f].astype(F32)
+            out[f, k + 1] = value + start[f] if k == 0 else value
+        leaving[k + 1].start()
+    for copy in leaving:
+        copy.wait()
+
+
+def opening(visc, start, forcing, snaps):
+    fields = start.shape[0]
+    cells = start.shape[1:]
+    return pl.pallas_call(
+        opening_kernel,
+        out_shape=jax.ShapeDtypeStruct((fields, snaps + 1) + cells, F32),
+        in_specs=[HBM] * 3,
+        out_specs=HBM,
+        scratch_shapes=[
+            pltpu.VMEM(cells, F32),
+            pltpu.VMEM(start.shape, F32),
+            pltpu.VMEM((snaps,) + forcing.shape[1:], forcing.dtype),
+            pltpu.VMEM((fields, snaps + 1) + cells, F32),
+            pltpu.SemaphoreType.DMA((snaps + 2,)),
+            pltpu.SemaphoreType.DMA((snaps + 1,)),
+        ],
+        compiler_params=params(60),
+        name="opening_blocks",
+    )(visc, start, forcing)
 
 
 def prep_kernel(fields, snaps, count, core, *refs):
@@ -271,7 +390,7 @@
     send[...] = gram[pl.ds((1 - mine) * half, half), :]
 
 
-def prep(core, rec, before, fields, snaps, after=()):
+def prep(core, rec, before, fields, snaps):
     width = fields * snaps
     cells = 2048
     return pl.pallas_call(
@@ -281,12 +400,12 @@
             jax.ShapeDtypeStruct((width, cells), BF16),
         )
         + (jax.ShapeDtypeStruct((width // 2, width * (len(before) // 2 + 1)), F32),) * 2,
-        in_specs=[SMEM] + [VMEM] * (1 + len(before)) + [pl.BlockSpec(memory_space=pl.ANY)] * len(after),
+        in_specs=[SMEM] + [VMEM] * (1 + len(before)),
         out_specs=(VMEM,) * 4,
         scratch_shapes=[pltpu.VMEM((width, width * (len(before) // 2 + 1)), F32)],
         compiler_params=params(),
         name="gram_blocks",
-    )(core, rec, *before, *after)
+    )(core, rec, *before)
 
 
 def rank_kernel(owner_count, owners, hot):
@@ -356,11 +475,11 @@
         functools.partial(pack_kernel, first),
         grid=(groups,),
         out_shape=jax.ShapeDtypeStruct((owner_count, capacity, 2 * width), F32),
-        in_specs=[VMEM] * 4 + [pl.BlockSpec(memory_space=pl.ANY)] * len(more),
+        in_specs=[VMEM] * 4 + [HBM] * len(more),
         out_specs=pl.BlockSpec((GROUP, capacity, width), lambda g: (first + g, 0, half)),
         scratch_shapes=[pltpu.VMEM((2, GROUP * width, cells), BF16)],
         input_output_aliases={4: 0} if more else {},
-        compiler_params=params(),
+        compiler_params=params(48),
         cost_estimate=pl.CostEstimate(
             flops=4 * GROUP * groups * capacity * width * cells,
             bytes_accessed=4 * GROUP * groups * capacity * width,
@@ -492,7 +611,7 @@
             pl.BlockSpec((SOURCES, capacity, order), lambda b: (b, 0, 0)),
         ],
         out_specs=pl.BlockSpec((SOURCES * capacity, order), lambda b: (b, 0)),
-        compiler_params=params(),
+        compiler_params=params(48),
         name="basis_rows",
     )(inverse, panel)
 
@@ -523,28 +642,26 @@
     def swap(value):
         return lax.all_to_all(value, plane, split_axis=0, concat_axis=0, tiled=True)
 
-    start = state_start + forcing[0].astype(F32)
-    visc_blocks = jnp.broadcast_to(viscosity[None, None], (fields, 1, wide, deep, lanes))
-    later = jnp.transpose(forcing, (1, 0, 2, 3, 4))
-    one = swap(jnp.concatenate([visc_blocks, start[:, None], later[:, 1:HALF].astype(F32)], 1))
-    two = swap(later[:, HALF:].astype(F32))
-    slabs = fields // pieces
-
-    def edges(value):
-        by_row = value.reshape((slabs, pieces) + value.shape[1:])
-        low = lax.ppermute(by_row[:, pieces - 1], "x", ring(x_size, 1))
-        high = lax.ppermute(by_row[:, 0], "x", ring(x_size, -1))
-        return low.reshape(-1, lanes), high.reshape(-1, lanes)
-
     x_at = lax.axis_index("x")
-    edge = jnp.stack([x_at > 0, x_at < x_size - 1]).astype(jnp.int32)
-    low_one, high_one = edges(one)
-    records_one, middle, visc = first_half(edge, one.reshape(-1, lanes), low_one, high_one, pieces, HALF)
-    low_two, high_two = edges(two)
-    middle_low = lax.ppermute(middle[-deep:], "x", ring(x_size, 1))
-    middle_high = lax.ppermute(middle[:deep], "x", ring(x_size, -1))
-    records_two, _ = second_half(
-        two.reshape(-1, lanes), low_two, high_two, middle, middle_low, middle_high, visc, pieces, HALF
+    around = jnp.stack([x_at > 0, x_at < x_size - 1]).astype(jnp.int32)
+    heights = tuple(SIDE - STEPS * k for k in range(HALF))
+
+    def shared(value, heights):
+        last, first = edges_of(value, pieces, heights)
+        return lax.ppermute(last, "x", ring(x_size, 1)), lax.ppermute(first, "x", ring(x_size, -1))
+
+    one = swap(opening(viscosity, state_start, forcing, HALF)).reshape(-1, lanes)
+    later = jnp.transpose(forcing[HALF:], (1, 0, 2, 3, 4)).astype(F32)
+    two = swap(later).reshape(-1, lanes)
+    with_visc = (SIDE,) + heights
+    low_one, high_one = shared(one, with_visc)
+    own_coefs = own_coefs_of(one, pieces, len(with_visc))
+    records_one, middle, edge = first_half(around, one, low_one, high_one, own_coefs, pieces, with_visc)
+    low_two, high_two = shared(two, heights)
+    middle_low = lax.ppermute(middle[-SIDE:], "x", ring(x_size, 1))
+    middle_high = lax.ppermute(middle[:SIDE], "x", ring(x_size, -1))
+    records_two = second_half(
+        two, low_two, high_two, middle, middle_low, middle_high, own_coefs, edge, pieces, heights
     )
     block = (fields, HALF, wide, deep, lanes)
     home_one = swap(records_one.reshape(block))
@@ -555,18 +672,22 @@
     high_a, low_a, keep_a, send_a = prep(core, home_one.reshape(-1, lanes), (), fields, HALF)
     part_a = summed(keep_a + swapped(send_a), "x", both)
     slots = pack(owners, hot, high_a, low_a, owner_count, 0)
-    high_b, low_b, keep_b, send_b = prep(
-        core, home_two.reshape(-1, lanes), (high_a, low_a), fields, HALF, (slots, part_a)
-    )
+    home_two, slots, part_a = lax.optimization_barrier((home_two, slots, part_a))
+    high_b, low_b, keep_b, send_b = prep(core, home_two.reshape(-1, lanes), (high_a, low_a), fields, HALF)
+    quarters = 4
+
+    def packed(slots, part, *values):
+        slots = pack(owners, hot, high_b, low_b, owner_count, 1, slots, part, quarters)
+        return lax.optimization_barrier((slots,) + values)
+
     part_b = summed(keep_b + swapped(send_b), "x", (0,))
-    slots = pack(owners, hot, high_b, low_b, owner_count, 1, slots, 0, 2)
-    slots, part_b = lax.optimization_barrier((slots, part_b))
+    slots, part_b = packed(slots, 0, part_b)
     part_b = summed(part_b, "x", (1,))
-    slots = pack(owners, hot, high_b, low_b, owner_count, 1, slots, 1, 2)
-    slots, part_b, part_a = lax.optimization_barrier((slots, part_b, part_a))
+    slots, part_b, part_a = packed(slots, 1, part_b, part_a)
     part = summed(jnp.concatenate([part_a, part_b], 1), "z", (0,))
+    slots, part = packed(slots, 2, part)
     part = summed(part, "z", (1,))
-    slots, part = lax.optimization_barrier((slots, part))
+    slots, part = packed(slots, 3, part)
     panel = lax.all_to_all(slots, ("x", "z"), split_axis=0, concat_axis=0, tiled=True)
     part = summed(part, "y", both)
     other = swapped(part)

time: 194 us -> 184 us (0.948)
  waiting for transfers between devices: 70.1 us -> 55.5 us
  starting transfers between devices: 51.7 us -> 59.3 us
  Pallas kernels: 60.4 us -> 62.6 us
  other arithmetic: 3.41 us -> 1.27 us
    ppermute x6, waiting for transfers between devices: 17.7 us -> 7.7 us  [the longest x2 6.89 us: shared(): lax.ppermute(last, 'x', ring(x_size, 1))]
    ppermute x8, starting transfers between devices: 9.36 us -> 13.5 us  [summed(): lax.ppermute(value, axis, [(i, i ^ 1 << level) for i in range(size)])]
    ppermute x8, waiting for transfers between devices: 19.5 us -> 15.8 us  [summed(): lax.ppermute(value, axis, [(i, i ^ 1 << level) for i in range(size)])]
    ppermute x6, starting transfers between devices: 6.95 us -> 9.85 us  [the longest x2 3.49 us: shared(): lax.ppermute(first, 'x', ring(x_size, -1))]
    pallas_call x3 -> x5, Pallas kernels: 13.3 us -> 14.8 us  [pack(): pl.pallas_call(functools.partial(pack_kernel, first), grid=(groups,), out...]
    pallas_call x2 -> x6, Pallas kernels: 12.1 us -> 12.8 us  [the longest x1 4.38 us: second_half(): pl.pallas_call(functools.partial(second_kernel, pieces, heights), out_sha...]
  transfers between devices with their start and end apart: 22 -> 22, of which waited for: 18 -> 17; matrix products, arithmetic and copies ran while one was open for 1% -> 1% of each run, Pallas kernels for 28% -> 29%
where the time goes in v5:
time: 184 us; the launch traced here: 183 us
  Pallas kernels  62.6 us (34%)
  starting transfers between devices  59.3 us (32%)
  waiting for transfers between devices  55.5 us (30%)
  local copies, waits for them, and re-layouts  3.36 us (2%)
    all_to_all x4, starting transfers between devices, swap(): return lax.all_to_all(value, plane, split_axis=0, concat_axis=0, tiled=True)  28.1 us
    all_to_all x4, waiting for transfers between devices, swap(): return lax.all_to_all(value, plane, split_axis=0, concat_axis=0, tiled=True)  17.8 us
    ppermute x8, waiting for transfers between devices, summed(): lax.ppermute(value, axis, [(i, i ^ 1 << level) for i in range(size)])  15.8 us
    pallas_call x5, Pallas kernels, pack(): pl.pallas_call(functools.partial(pack_kernel, first), grid=(groups,), out...  14.8 us
    pallas_call x1, Pallas kernels, factor_trail(): pl.pallas_call(trail_kernel, out_shape=(jax.ShapeDtypeStruct((2 * order,...  14 us
    ppermute x8, starting transfers between devices, summed(): lax.ppermute(value, axis, [(i, i ^ 1 << level) for i in range(size)])  13.5 us
    pallas_call x1, Pallas kernels, factor_lead(): pl.pallas_call(lead_kernel, out_shape=(jax.ShapeDtypeStruct((order, order...  12.4 us
    all_to_all x1, waiting for transfers between devices, on_device(): lax.all_to_all(slots, ('x', 'z'), split_axis=0, concat_axis=0, tiled=True)  11.4 us
  transfers between devices with their start and end apart: 22, of which 17 were waited for; matrix products, arithmetic and copies ran while one was open for 1% of the time, Pallas kernels for 29%

profile of v5, /device:TPU:64, one launch (start us, length us, event | category | flops | bytes accessed | tf_op | source)
XLA Modules:
  0.0 182.9 jit_solution(8067002752121808106)
XLA Ops:
  0.6 2.2 %opening_blocks.1 = f32[32,5,2,8,128]{4,3,2,1,0:T(8,128)} custom-call(f32[2,8,128]{2,1,0:T(8,128)} %visc_from.1, f32[32,2,8,128]{3,2,1,0:T(8,128)} %start_from.1, bf16[8,32,2,8,128]{4,3,2,1,0:T(8,128)(2,1)} %forcing_from.1), custom_call_target="tpu_custom_call" | custom-call | tf_op jit(solution)/shard_map/opening_blocks/pallas_call | solution.py:347
  2.8 7.8 %all-to-all-start.1 = ((f32[32,5,2,8,128]{4,3,2,1,0:T(8,128)}), f32[32,5,2,8,128]{4,3,2,1,0:T(8,128)S(1)}, u32[]{:S(2)}, u32[]{:S(2)}) async-start(f32[32,5,2,8,128]{4,3,2,1,0:T(8,128)} %opening_blocks.1), calls=%async_computation.1 | async-start | bytes 2621440 | tf_op jit(solution)/shard_map/all_to_all | solution.py:643
  11.7 17.0 %all-to-all-done.1 = f32[32,5,2,8,128]{4,3,2,1,0:T(8,128)S(1)} async-done(((f32[32,5,2,8,128]{4,3,2,1,0:T(8,128)}), f32[32,5,2,8,128]{4,3,2,1,0:T(8,128)S(1)}, u32[]{:S(2)}, u32[]{:S(2)}) %all-to-all-start.1) | async-done | bytes 1310752 | tf_op jit(solution)/shard_map/all_to_all | solution.py:643
  28.7 6.2 %all-to-all-start = ((f32[32,4,2,8,128]{4,3,2,1,0:T(8,128)}), f32[32,4,2,8,128]{4,3,2,1,0:T(8,128)}, u32[]{:S(2)}, u32[]{:S(2)}) async-start(f32[32,4,2,8,128]{4,3,2,1,0:T(8,128)} %convert_bitcast_fusion), calls=%async_computation | async-start | bytes 2097152 | tf_op jit(solution)/shard_map/all_to_all | solution.py:643
  37.3 1.7 collective-permute-start.3
  39.5 5.4 %collective-permute-done.2.low_from = f32[448,128]{1,0:T(8,128)S(1)} collective-permute-done((f32[448,128]{1,0:T(8,128)}, f32[448,128]{1,0:T(8,128)S(1)}, u32[]{:S(2)}, u32[]{:S(2)}) %collective-permute-start.2) | collective-permute-done | bytes 229408 | tf_op jit(solution)/shard_map/ppermute | solution.py:651
  46.5 3.8 %diffuse_first.1 = (f32[32,4,16,128]{3,2,1,0:T(8,128)S(1)}, f32[32,2,8,128]{3,2,1,0:T(8,128)S(1)}, f32[20,2,8,128]{3,2,1,0:T(8,128)S(1)}) custom-call(s32[2]{0:T(128)S(1)} %add_convert_fusion.around, f32[2560,128]{1,0:T(8,128)S(1)} %bitcast.16, f32[448,128]{1,0:T(8,128)S(1)} %collective-permute-done.2.low_from, f32[448,128]{1,0:T(8,128)S(1)} %copy-done.2, ...), custom_call_target="tpu_custom_call" | custom-call | tf_op jit(solution)/shard_map/diffuse_first/pallas_call | solution.py:263
  51.3 7.5 %all-to-all-start.3 = ((f32[32,4,2,8,128]{4,3,2,1,0:T(8,128)}), f32[32,4,2,8,128]{4,3,2,1,0:T(8,128)S(1)}, u32[]{:S(2)}, u32[]{:S(2)}) async-start(f32[32,4,2,8,128]{4,3,2,1,0:T(8,128)} %bitcast.19), calls=%async_computation.3 | async-start | bytes 2097152 | tf_op jit(solution)/shard_map/all_to_all | solution.py:643
  60.0 1.6 collective-permute-start
  61.6 1.7 collective-permute-start.1
  63.7 3.0 %collective-permute-start.5 = (f32[8,2,8,128]{3,2,1,0:T(8,128)S(1)}, f32[8,2,8,128]{3,2,1,0:T(8,128)S(1)}, u32[]{:S(2)}, u32[]{:S(2)}) collective-permute-start(f32[8,2,8,128]{3,2,1,0:T(8,128)S(1)} %get-tuple-element.65), channel_id=1, source_target_pairs={{0,12},{4,0},{8,4},{12,8},{1,13},{5,1},{9,5},{13,9},{2,14},{6,2},{... | collective-permute-start | bytes 196616 | tf_op jit(solution)/shard_map/ppermute | solution.py:662
  69.0 4.4 %diffuse_second.1 = f32[32,4,16,128]{3,2,1,0:T(8,128)} custom-call(f32[2048,128]{1,0:T(8,128)} %bitcast.1.main, f32[320,128]{1,0:T(8,128)S(1)} %collective-permute-done.low, f32[320,128]{1,0:T(8,128)S(1)} %collective-permute-done.1.high, f32[32,2,8,128]{3,2,1,0:T(8,128)S(1)} %get-tuple-element.38.start, ...), custom_call_target="tpu_custom_call" | custom-call | tf_op jit(solution)/shard_map/diffuse_second/pallas_call | solution.py:281
  74.1 6.7 %all-to-all-start.2 = ((f32[32,4,2,8,128]{4,3,2,1,0:T(8,128)}), f32[32,4,2,8,128]{4,3,2,1,0:T(8,128)S(1)}, u32[]{:S(2)}, u32[]{:S(2)}) async-start(f32[32,4,2,8,128]{4,3,2,1,0:T(8,128)} %bitcast.5), calls=%async_computation.2 | async-start | bytes 2097152 | tf_op jit(solution)/shard_map/all_to_all | solution.py:643
  85.3 1.9 %collective-permute-done.7 = f32[64,128]{1,0:T(8,128)S(1)} collective-permute-done((f32[64,128]{1,0:T(8,128)S(1)}, f32[64,128]{1,0:T(8,128)S(1)}, u32[]{:S(2)}, u32[]{:S(2)}) %collective-permute-start.7) | collective-permute-done | bytes 32800 | tf_op jit(solution)/shard_map/ppermute | solution.py:630
  87.2 2.9 %collective-permute-start.8 = (f32[64,128]{1,0:T(8,128)S(1)}, f32[64,128]{1,0:T(8,128)S(1)}, u32[]{:S(2)}, u32[]{:S(2)}) collective-permute-start(f32[64,128]{1,0:T(8,128)S(1)} %add.31), channel_id=1, source_target_pairs={{0,8},{4,12},{8,0},{12,4},{1,9},{5,13},{9,1},{13,5},{2,10},{6,14},... | collective-permute-start | bytes 98312 | tf_op jit(solution)/shard_map/ppermute | solution.py:630
  90.2 6.2 %pack_slots.5.refs_0_ = f32[16,256,256]{2,1,0:T(8,128)} custom-call(s32[16,128]{1,0:T(8,128)S(1)} %bitcast.21, bf16[256,2048]{1,0:T(8,128)(2,1)S(1)} %slot_ranks.1.hot, bf16[128,2048]{1,0:T(8,128)(2,1)S(1)} %get-tuple-element.41.high.refs_1_, bf16[128,2048]{1,0:T(8,128)(2,1)S(1)} %get-tuple-element.42.low.refs_2_), custom_call_target="tpu_custom_call" | custom-call | flops 4294967296 | bytes 2097152 | tf_op jit(solution)/shard_map/pack_slots/pallas_call | solution.py:474
  96.4 1.6 gram_blocks.3
  100.5 2.1 %pack_slots.6.refs_0_ = f32[16,256,256]{2,1,0:T(8,128)} custom-call(s32[16,128]{1,0:T(8,128)S(1)} %bitcast.22, bf16[256,2048]{1,0:T(8,128)(2,1)S(1)} %slot_ranks.1.hot, bf16[128,2048]{1,0:T(8,128)(2,1)S(1)} %get-tuple-element.46.high, bf16[128,2048]{1,0:T(8,128)(2,1)S(1)} %get-tuple-element.47.low, ...), custom_call_target="tpu_custom_call", output_to_operand_aliasing={{}: (4, {})} | custom-call | flops 1073741824 | bytes 524288 | tf_op jit(solution)/shard_map/pack_slots/pallas_call | solution.py:474
  103.7 2.7 %collective-permute-start.11 = (f32[64,256]{1,0:T(8,128)S(1)}, f32[64,256]{1,0:T(8,128)S(1)}, u32[]{:S(2)}, u32[]{:S(2)}) collective-permute-start(f32[64,256]{1,0:T(8,128)S(1)} %add.34), channel_id=1, source_target_pairs={{0,8},{4,12},{8,0},{12,4},{1,9},{5,13},{9,1},{13,5},{2,10},{6,14},... | collective-permute-start | bytes 196616 | tf_op jit(solution)/shard_map/ppermute | solution.py:630
  106.4 2.1 %pack_slots.7.refs_0_ = f32[16,256,256]{2,1,0:T(8,128)} custom-call(s32[16,128]{1,0:T(8,128)S(1)} %bitcast.23, bf16[256,2048]{1,0:T(8,128)(2,1)S(1)} %slot_ranks.1.hot, bf16[128,2048]{1,0:T(8,128)(2,1)S(1)} %get-tuple-element.46.high, bf16[128,2048]{1,0:T(8,128)(2,1)S(1)} %get-tuple-element.47.low, ...), custom_call_target="tpu_custom_call", output_to_operand_aliasing={{}: (4, {})} | custom-call | flops 1073741824 | bytes 524288 | tf_op jit(solution)/shard_map/pack_slots/pallas_call | solution.py:474
  110.8 2.1 %pack_slots.8.refs_0_ = f32[16,256,256]{2,1,0:T(8,128)} custom-call(s32[16,128]{1,0:T(8,128)S(1)} %bitcast.24, bf16[256,2048]{1,0:T(8,128)(2,1)S(1)} %slot_ranks.1.hot, bf16[128,2048]{1,0:T(8,128)(2,1)S(1)} %get-tuple-element.46.high, bf16[128,2048]{1,0:T(8,128)(2,1)S(1)} %get-tuple-element.47.low, ...), custom_call_target="tpu_custom_call", output_to_operand_aliasing={{}: (4, {})} | custom-call | flops 1073741824 | bytes 524288 | tf_op jit(solution)/shard_map/pack_slots/pallas_call | solution.py:474
  114.3 1.8 collective-permute-start.13
  116.1 2.1 %pack_slots.9 = f32[16,256,256]{2,1,0:T(8,128)} custom-call(s32[16,128]{1,0:T(8,128)S(1)} %bitcast.25, bf16[256,2048]{1,0:T(8,128)(2,1)S(1)} %slot_ranks.1.hot, bf16[128,2048]{1,0:T(8,128)(2,1)S(1)} %get-tuple-element.46.high, bf16[128,2048]{1,0:T(8,128)(2,1)S(1)} %get-tuple-element.47.low, ...), custom_call_target="tpu_custom_call", output_to_operand_aliasing={{}: (4, {})} | custom-call | flops 1073741824 | bytes 524288 | tf_op jit(solution)/shard_map/pack_slots/pallas_call | solution.py:474
  118.3 2.2 %collective-permute-done.13 = f32[64,384]{1,0:T(8,128)S(1)} collective-permute-done((f32[64,384]{1,0:T(8,128)S(1)}, f32[64,384]{1,0:T(8,128)S(1)}, u32[]{:S(2)}, u32[]{:S(2)}) %collective-permute-start.13) | collective-permute-done | bytes 98336 | tf_op jit(solution)/shard_map/ppermute | solution.py:630
  120.5 7.1 %all-to-all-start.4 = ((f32[16,256,256]{2,1,0:T(8,128)}), f32[16,256,256]{2,1,0:T(8,128)}, u32[]{:S(2)}, u32[]{:S(2)}) async-start(f32[16,256,256]{2,1,0:T(8,128)} %pack_slots.9), calls=%async_computation.4 | async-start | bytes 8388608 | tf_op jit(solution)/shard_map/all_to_all | solution.py:691
  128.3 4.0 %collective-permute-done.14 = f32[64,384]{1,0:T(8,128)S(1)} collective-permute-done((f32[64,384]{1,0:T(8,128)S(1)}, f32[64,384]{1,0:T(8,128)S(1)}, u32[]{:S(2)}, u32[]{:S(2)}) %collective-permute-start.14) | collective-permute-done | bytes 98336 | tf_op jit(solution)/shard_map/ppermute | solution.py:630
  132.3 1.9 %collective-permute-start.15 = (f32[64,384]{1,0:T(8,128)S(1)}, f32[64,384]{1,0:T(8,128)S(1)}, u32[]{:S(2)}, u32[]{:S(2)}) collective-permute-start(f32[64,384]{1,0:T(8,128)S(1)} %add.38), channel_id=1, source_target_pairs={{0,64},{32,96},{64,0},{96,32},{1,65},{33,97},{65,1},{97,33},{2,66}... | collective-permute-start | bytes 294920 | tf_op jit(solution)/shard_map/ppermute | solution.py:630
  134.2 4.3 %collective-permute-done.15 = f32[64,384]{1,0:T(8,128)S(1)} collective-permute-done((f32[64,384]{1,0:T(8,128)S(1)}, f32[64,384]{1,0:T(8,128)S(1)}, u32[]{:S(2)}, u32[]{:S(2)}) %collective-permute-start.15) | collective-permute-done | bytes 98336 | tf_op jit(solution)/shard_map/ppermute | solution.py:630
  140.1 12.4 %factor_lead.1 = (f32[128,128]{1,0:T(8,128)S(1)}, f32[128,128]{1,0:T(8,128)S(1)}) custom-call(s32[1]{0:T(128)} %bitcast.7.core, f32[64,128]{1,0:T(8,128)S(1)} %slice.34.own, f32[64,128]{1,0:T(8,128)S(1)} %slice.35.other), custom_call_target="tpu_custom_call" | custom-call | tf_op jit(solution)/shard_map/factor_lead/pallas_call | solution.py:566
  152.5 14.0 %factor_trail.1 = (f32[256,256]{1,0:T(8,128)}, f32[256,256]{1,0:T(8,128)S(1)}) custom-call(s32[1]{0:T(128)} %bitcast.7.core, f32[64,256]{1,0:T(8,128)S(1)} %slice.32.own_half, f32[64,256]{1,0:T(8,128)S(1)} %slice.33.other_half, f32[128,128]{1,0:T(8,128)S(1)} %get-tuple-element.60.lead, f32[128,128]{1,0:T(8,128)S(1)} %get-tuple-element.61.lead_inv), custom_call_target="tpu_custom_call" | custom-call | tf_op jit(solution)/shard_map/factor_trail/pallas_call | solution.py:579
  166.5 11.4 %all-to-all-done.4.panel = f32[16,256,256]{2,1,0:T(8,128)} async-done(((f32[16,256,256]{2,1,0:T(8,128)}), f32[16,256,256]{2,1,0:T(8,128)}, u32[]{:S(2)}, u32[]{:S(2)}) %all-to-all-start.4) | async-done | bytes 4194336 | tf_op jit(solution)/shard_map/all_to_all | solution.py:691
  177.9 5.0 %basis_rows.1 = f32[4096,256]{1,0:T(8,128)} custom-call(f32[256,256]{1,0:T(8,128)S(1)} %get-tuple-element.63.inverse, f32[16,256,256]{2,1,0:T(8,128)} %all-to-all-done.4.panel), custom_call_target="tpu_custom_call" | custom-call | tf_op jit(solution)/shard_map/basis_rows/pallas_call | solution.py:605
  (59 shorter events, 25.1 us)
Async XLA Ops:
  0.6 10.0 %copy-start.4 = (bf16[8,32,2,8,128]{4,3,2,1,0:T(8,128)(2,1)S(1)}, bf16[8,32,2,8,128]{4,3,2,1,0:T(8,128)(2,1)}, u32[]{:S(2)}) copy-start(bf16[8,32,2,8,128]{4,3,2,1,0:T(8,128)(2,1)} %forcing_from.1) | copy-start | bytes 3145732
  2.8 25.9 %all-to-all-start.1 = ((f32[32,5,2,8,128]{4,3,2,1,0:T(8,128)}), f32[32,5,2,8,128]{4,3,2,1,0:T(8,128)S(1)}, u32[]{:S(2)}, u32[]{:S(2)}) async-start(f32[32,5,2,8,128]{4,3,2,1,0:T(8,128)} %opening_blocks.1), calls=%async_computation.1 | async-start | bytes 2621440 | tf_op jit(solution)/shard_map/all_to_all | solution.py:643
  28.7 22.5 %all-to-all-start = ((f32[32,4,2,8,128]{4,3,2,1,0:T(8,128)}), f32[32,4,2,8,128]{4,3,2,1,0:T(8,128)}, u32[]{:S(2)}, u32[]{:S(2)}) async-start(f32[32,4,2,8,128]{4,3,2,1,0:T(8,128)} %convert_bitcast_fusion), calls=%async_computation | async-start | bytes 2097152 | tf_op jit(solution)/shard_map/all_to_all | solution.py:643
  35.8 9.1 %collective-permute-start.2 = (f32[448,128]{1,0:T(8,128)}, f32[448,128]{1,0:T(8,128)S(1)}, u32[]{:S(2)}, u32[]{:S(2)}) collective-permute-start(f32[448,128]{1,0:T(8,128)} %get-tuple-element.36), channel_id=1, source_target_pairs={{0,4},{4,8},{8,12},{12,0},{1,5},{5,9},{9,13},{13,1},{2,6},{6,10},{... | collective-permute-start | bytes 688136 | tf_op jit(solution)/shard_map/ppermute | solution.py:651
  37.3 7.6 %collective-permute-start.3 = (f32[448,128]{1,0:T(8,128)}, f32[448,128]{1,0:T(8,128)S(1)}, u32[]{:S(2)}, u32[]{:S(2)}) collective-permute-start(f32[448,128]{1,0:T(8,128)} %get-tuple-element.37), channel_id=1, source_target_pairs={{0,12},{4,0},{8,4},{12,8},{1,13},{5,1},{9,5},{13,9},{2,14},{6,2},{... | collective-permute-start | bytes 688136 | tf_op jit(solution)/shard_map/ppermute | solution.py:651
  44.9 0.7 copy-start.1
  45.6 0.9 copy-start.2
  50.3 1.0 copy-start
  51.3 22.8 %all-to-all-start.3 = ((f32[32,4,2,8,128]{4,3,2,1,0:T(8,128)}), f32[32,4,2,8,128]{4,3,2,1,0:T(8,128)S(1)}, u32[]{:S(2)}, u32[]{:S(2)}) async-start(f32[32,4,2,8,128]{4,3,2,1,0:T(8,128)} %bitcast.19), calls=%async_computation.3 | async-start | bytes 2097152 | tf_op jit(solution)/shard_map/all_to_all | solution.py:643
  60.0 24.5 %copy-start.3 = (s32[1,1,2048,1]{2,3,1,0:T(1,128)S(1)}, s32[1,1,2048,1]{2,3,1,0:T(1,128)}, u32[]{:S(2)}) copy-start(s32[1,1,2048,1]{2,3,1,0:T(1,128)} %param.7) | copy-start | bytes 24580
  60.0 8.1 %collective-permute-start = (f32[320,128]{1,0:T(8,128)S(1)}, f32[320,128]{1,0:T(8,128)S(1)}, u32[]{:S(2)}, u32[]{:S(2)}) collective-permute-start(f32[320,128]{1,0:T(8,128)S(1)} %get-tuple-element.34), channel_id=1, source_target_pairs={{0,4},{4,8},{8,12},{12,0},{1,5},{5,9},{9,13},{13,1},{2,6},{6,10},{... | collective-permute-start | bytes 491528 | tf_op jit(solution)/shard_map/ppermute | solution.py:651
  61.6 6.7 %collective-permute-start.1 = (f32[320,128]{1,0:T(8,128)S(1)}, f32[320,128]{1,0:T(8,128)S(1)}, u32[]{:S(2)}, u32[]{:S(2)}) collective-permute-start(f32[320,128]{1,0:T(8,128)S(1)} %get-tuple-element.35), channel_id=1, source_target_pairs={{0,12},{4,0},{8,4},{12,8},{1,13},{5,1},{9,5},{13,9},{2,14},{6,2},{... | collective-permute-start | bytes 491528 | tf_op jit(solution)/shard_map/ppermute | solution.py:651
  63.4 5.6 %collective-permute-start.4 = (f32[8,2,8,128]{3,2,1,0:T(8,128)S(1)}, f32[8,2,8,128]{3,2,1,0:T(8,128)S(1)}, u32[]{:S(2)}, u32[]{:S(2)}) collective-permute-start(f32[8,2,8,128]{3,2,1,0:T(8,128)S(1)} %get-tuple-element.66), channel_id=1, source_target_pairs={{0,4},{4,8},{8,12},{12,0},{1,5},{5,9},{9,13},{13,1},{2,6},{6,10},{... | collective-permute-start | bytes 196616 | tf_op jit(solution)/shard_map/ppermute | solution.py:661
  63.7 5.3 %collective-permute-start.5 = (f32[8,2,8,128]{3,2,1,0:T(8,128)S(1)}, f32[8,2,8,128]{3,2,1,0:T(8,128)S(1)}, u32[]{:S(2)}, u32[]{:S(2)}) collective-permute-start(f32[8,2,8,128]{3,2,1,0:T(8,128)S(1)} %get-tuple-element.65), channel_id=1, source_target_pairs={{0,12},{4,0},{8,4},{12,8},{1,13},{5,1},{9,5},{13,9},{2,14},{6,2},{... | collective-permute-start | bytes 196616 | tf_op jit(solution)/shard_map/ppermute | solution.py:662
  74.1 22.3 %all-to-all-start.2 = ((f32[32,4,2,8,128]{4,3,2,1,0:T(8,128)}), f32[32,4,2,8,128]{4,3,2,1,0:T(8,128)S(1)}, u32[]{:S(2)}, u32[]{:S(2)}) async-start(f32[32,4,2,8,128]{4,3,2,1,0:T(8,128)} %bitcast.5), calls=%async_computation.2 | async-start | bytes 2097152 | tf_op jit(solution)/shard_map/all_to_all | solution.py:643
  82.0 1.3 collective-permute-start.6
  83.3 3.9 %collective-permute-start.7 = (f32[64,128]{1,0:T(8,128)S(1)}, f32[64,128]{1,0:T(8,128)S(1)}, u32[]{:S(2)}, u32[]{:S(2)}) collective-permute-start(f32[64,128]{1,0:T(8,128)S(1)} %add.30), channel_id=1, source_target_pairs={{0,4},{4,0},{8,12},{12,8},{1,5},{5,1},{9,13},{13,9},{2,6},{6,2},{1... | collective-permute-start | bytes 98312 | tf_op jit(solution)/shard_map/ppermute | solution.py:630
  87.2 9.2 %collective-permute-start.8 = (f32[64,128]{1,0:T(8,128)S(1)}, f32[64,128]{1,0:T(8,128)S(1)}, u32[]{:S(2)}, u32[]{:S(2)}) collective-permute-start(f32[64,128]{1,0:T(8,128)S(1)} %add.31), channel_id=1, source_target_pairs={{0,8},{4,12},{8,0},{12,4},{1,9},{5,13},{9,1},{13,5},{2,10},{6,14},... | collective-permute-start | bytes 98312 | tf_op jit(solution)/shard_map/ppermute | solution.py:630
  98.0 1.3 collective-permute-start.9
  99.3 4.3 %collective-permute-start.10 = (f32[64,256]{1,0:T(8,128)S(1)}, f32[64,256]{1,0:T(8,128)S(1)}, u32[]{:S(2)}, u32[]{:S(2)}) collective-permute-start(f32[64,256]{1,0:T(8,128)S(1)} %add.33), channel_id=1, source_target_pairs={{0,4},{4,0},{8,12},{12,8},{1,5},{5,1},{9,13},{13,9},{2,6},{6,2},{1... | collective-permute-start | bytes 196616 | tf_op jit(solution)/shard_map/ppermute | solution.py:630
  103.7 5.8 %collective-permute-start.11 = (f32[64,256]{1,0:T(8,128)S(1)}, f32[64,256]{1,0:T(8,128)S(1)}, u32[]{:S(2)}, u32[]{:S(2)}) collective-permute-start(f32[64,256]{1,0:T(8,128)S(1)} %add.34), channel_id=1, source_target_pairs={{0,8},{4,12},{8,0},{12,4},{1,9},{5,13},{9,1},{13,5},{2,10},{6,14},... | collective-permute-start | bytes 196616 | tf_op jit(solution)/shard_map/ppermute | solution.py:630
  109.6 4.7 %collective-permute-start.12 = (f32[64,384]{1,0:T(8,128)S(1)}, f32[64,384]{1,0:T(8,128)S(1)}, u32[]{:S(2)}, u32[]{:S(2)}) collective-permute-start(f32[64,384]{1,0:T(8,128)S(1)} %constant_dynamic-update-slice_fusion), channel_id=1, source_target_pairs={{0,1},{1,0},{2,3},{3,2},{4,5},{5,4},{6,7},{7,6},{8,9},{9,8},{10,11... | collective-permute-start | bytes 294920 | tf_op jit(solution)/shard_map/ppermute | solution.py:630
  114.3 6.2 %collective-permute-start.13 = (f32[64,384]{1,0:T(8,128)S(1)}, f32[64,384]{1,0:T(8,128)S(1)}, u32[]{:S(2)}, u32[]{:S(2)}) collective-permute-start(f32[64,384]{1,0:T(8,128)S(1)} %add.36), channel_id=1, source_target_pairs={{0,2},{1,3},{2,0},{3,1},{4,6},{5,7},{6,4},{7,5},{8,10},{9,11},{10,... | collective-permute-start | bytes 294920 | tf_op jit(solution)/shard_map/ppermute | solution.py:630
  120.5 57.4 %all-to-all-start.4 = ((f32[16,256,256]{2,1,0:T(8,128)}), f32[16,256,256]{2,1,0:T(8,128)}, u32[]{:S(2)}, u32[]{:S(2)}) async-start(f32[16,256,256]{2,1,0:T(8,128)} %pack_slots.9), calls=%async_computation.4 | async-start | bytes 8388608 | tf_op jit(solution)/shard_map/all_to_all | solution.py:691
  127.7 4.6 %collective-permute-start.14 = (f32[64,384]{1,0:T(8,128)S(1)}, f32[64,384]{1,0:T(8,128)S(1)}, u32[]{:S(2)}, u32[]{:S(2)}) collective-permute-start(f32[64,384]{1,0:T(8,128)S(1)} %add.37), channel_id=1, source_target_pairs={{0,32},{32,0},{64,96},{96,64},{1,33},{33,1},{65,97},{97,65},{2,34}... | collective-permute-start | bytes 294920 | tf_op jit(solution)/shard_map/ppermute | solution.py:630
  132.3 6.2 %collective-permute-start.15 = (f32[64,384]{1,0:T(8,128)S(1)}, f32[64,384]{1,0:T(8,128)S(1)}, u32[]{:S(2)}, u32[]{:S(2)}) collective-permute-start(f32[64,384]{1,0:T(8,128)S(1)} %add.38), channel_id=1, source_target_pairs={{0,64},{32,96},{64,0},{96,32},{1,65},{33,97},{65,1},{97,33},{2,66}... | collective-permute-start | bytes 294920 | tf_op jit(solution)/shard_map/ppermute | solution.py:630
  138.5 1.6 collective-permute-start.16

commit v6 on v5

--- a/solution.py
+++ b/solution.py
@@ -132,7 +132,7 @@
         row_coefs(visc, y, True, store)
 
 
-def run_steps(read, blocks, fields, own_coefs, edge, pieces, snaps, records, last, kept, sems):
+def run_steps(read, blocks, fields, own_coefs, edge, pieces, snaps, records, last):
     own = 8 * pieces
     rows = own + 2 * SIDE
 
@@ -160,7 +160,6 @@
                     dest[y, i] = total
 
     done = 0
-    copies = []
     for k in range(snaps):
         first = fields[0]
         if k:
@@ -174,39 +173,19 @@
             z, j = divmod(y, 8)
             for i in range(2):
                 value = first[SIDE + y, i]
-                kept[pl.ds((z * snaps + k) * 16 + i * 8 + j, 8, stride=pieces * snaps * 16), :] = value
+                records[pl.ds((z * snaps + k) * 16 + i * 8 + j, 8, stride=pieces * snaps * 16), :] = value
                 if last is not None and k == snaps - 1:
                     last[y, i] = value
-        blocks_of = (8 * pieces, snaps, 16, 128)
-        copies.append(
-            pltpu.make_async_copy(
-                kept.reshape(*blocks_of).at[:, k], records.at[:, k], sems.at[k]
-            )
-        )
-        copies[-1].start()
-    for copy in copies:
-        copy.wait()
 
 
 def first_kernel(
-    pieces, heights, around, main, low_from, high_from, own_coefs, records, last, edge_visc, buf0, buf1, kept, sems, edge, low, high, edge_sems
+    pieces, heights, around, main, low, high, own_coefs, records, last, edge_visc, buf0, buf1, edge
 ):
-    arriving = [
-        pltpu.make_async_copy(low_from, low, edge_sems.at[0]),
-        pltpu.make_async_copy(high_from, high, edge_sems.at[1]),
-    ]
-    for copy in arriving:
-        copy.start()
     read = reader(main, low, high, heights, pieces)
     has_low = jnp.where(around[0] > 0, 1.0, 0.0)
     has_high = jnp.where(around[1] > 0, 1.0, 0.0)
     own = 8 * pieces
-    for y in range(SIDE, SIDE + own):
-        for i in range(2):
-            buf0[y, i] = read(1, y, i)
-    for copy in arriving:
-        copy.wait()
-    for y in list(range(SIDE)) + list(range(SIDE + own, own + 2 * SIDE)):
+    for y in range(own + 2 * SIDE):
         for i in range(2):
             buf0[y, i] = read(1, y, i)
     for y in list(range(SIDE + 2)) + list(range(SIDE + own - 2, own + 2 * SIDE)):
@@ -219,10 +198,10 @@
             edge_visc[y if y <= SIDE + 1 else y - own + 4, i] = value
     edge_coefs(edge_visc, pieces, edge)
     snaps = len(heights) - 1
-    run_steps(read, range(1, snaps + 1), (buf0, buf1), own_coefs, edge, pieces, snaps, records, last, kept, sems)
-
-
-def second_kernel(pieces, heights, main, low, high, start, start_low, start_high, own_coefs, edge_visc, records, buf0, buf1, kept, sems, edge):
+    run_steps(read, range(1, snaps + 1), (buf0, buf1), own_coefs, edge, pieces, snaps, records, last)
+
+
+def second_kernel(pieces, heights, main, low, high, start, start_low, start_high, own_coefs, edge_visc, records, buf0, buf1, edge):
     read = reader(main, low, high, heights, pieces)
     own = 8 * pieces
     for y in range(own + 2 * SIDE):
@@ -236,7 +215,7 @@
             buf0[y, i] = before + read(0, y, i)
     edge_coefs(edge_visc, pieces, edge)
     snaps = len(heights)
-    run_steps(read, range(snaps), (buf0, buf1), own_coefs, edge, pieces, snaps, records, None, kept, sems)
+    run_steps(read, range(snaps), (buf0, buf1), own_coefs, edge, pieces, snaps, records, None)
 
 
 def own_coefs_of(main, pieces, blocks):
@@ -250,10 +229,8 @@
     )(main)
 
 
-def buffers(pieces, snaps):
+def buffers(pieces):
     return [pltpu.VMEM((8 * pieces + 2 * SIDE, 2, 8, 128), F32)] * 2 + [
-        pltpu.VMEM((8 * pieces * snaps * 16, 128), F32),
-        pltpu.SemaphoreType.DMA((snaps,)),
         pltpu.VMEM((6, 2 * SIDE + 2, 2, 8, 128), F32),
     ]
 
@@ -263,15 +240,14 @@
     return pl.pallas_call(
         functools.partial(first_kernel, pieces, heights),
         out_shape=(
-            jax.ShapeDtypeStruct((8 * pieces, snaps, 16, 128), F32),
+            jax.ShapeDtypeStruct((8 * pieces * snaps * 16, 128), F32),
             jax.ShapeDtypeStruct((8 * pieces, 2, 8, 128), F32),
             jax.ShapeDtypeStruct((2 * SIDE + 4, 2, 8, 128), F32),
         ),
-        in_specs=[SMEM, VMEM, HBM, HBM, VMEM],
-        out_specs=(HBM, VMEM, VMEM),
-        scratch_shapes=buffers(pieces, snaps)
-        + [pltpu.VMEM(low.shape, F32), pltpu.VMEM(high.shape, F32), pltpu.SemaphoreType.DMA((2,))],
-        compiler_params=params(6),
+        in_specs=[SMEM] + [VMEM] * 4,
+        out_specs=(VMEM,) * 3,
+        scratch_shapes=buffers(pieces),
+        compiler_params=params(5),
         name="diffuse_first",
     )(around, main, low, high, own_coefs)
 
@@ -280,11 +256,11 @@
     snaps = len(heights)
     return pl.pallas_call(
         functools.partial(second_kernel, pieces, heights),
-        out_shape=jax.ShapeDtypeStruct((8 * pieces, snaps, 16, 128), F32),
+        out_shape=jax.ShapeDtypeStruct((8 * pieces * snaps * 16, 128), F32),
         in_specs=[VMEM] * 8,
-        out_specs=HBM,
-        scratch_shapes=buffers(pieces, snaps),
-        compiler_params=params(6),
+        out_specs=VMEM,
+        scratch_shapes=buffers(pieces),
+        compiler_params=params(5),
         name="diffuse_second",
     )(main, low, high, start, start_low, start_high, own_coefs, edge)
 
@@ -362,10 +338,9 @@
     )(visc, start, forcing)
 
 
-def prep_kernel(fields, snaps, count, core, *refs):
-    rec = refs[0]
-    before = refs[1 : 1 + 2 * count]
-    high_out, low_out, keep, send, gram = refs[-5:]
+def prep_kernel(fields, snaps, core, *refs):
+    rec, before = refs[0], refs[1:-6]
+    whole, high_out, low_out, keep, send, gram = refs[-6:]
     for cell_row in range(16):
         for s in range(snaps):
             for f in range(0, fields, 16):
@@ -373,37 +348,35 @@
                     rec[pl.ds(((f + g) * snaps + s) * 16 + cell_row, 8, stride=snaps * 16), :]
                     for g in (0, 8)
                 ]
-                high, low = split(jnp.concatenate(parts, 0))
+                value = jnp.concatenate(parts, 0)
+                high, low = split(value)
                 at = (slice(s * fields + f, s * fields + f + 16), slice(cell_row * 128, cell_row * 128 + 128))
+                whole[at] = value
                 high_out[at] = high
                 low_out[at] = low
-    high, low = high_out[...], low_out[...]
     width = fields * snaps
-    pairs = [(before[2 * c], before[2 * c + 1]) for c in range(count)] + [(high_out, low_out)]
-    for c, (other_high, other_low) in enumerate(pairs):
-        oh, ol = other_high[...], other_low[...]
-        block = bf_dot(high, oh, NT) + (bf_dot(high, ol, NT) + bf_dot(low, oh, NT))
-        gram[:, c * width : (c + 1) * width] = block
+    mine = whole[...]
+    for c, other in enumerate(before + (whole,)):
+        gram[:, c * width : (c + 1) * width] = exact_dot(mine, other[...], NT)
     half = width // 2
-    mine = core[0]
-    keep[...] = gram[pl.ds(mine * half, half), :]
-    send[...] = gram[pl.ds((1 - mine) * half, half), :]
+    kept = core[0]
+    keep[...] = gram[pl.ds(kept * half, half), :]
+    send[...] = gram[pl.ds((1 - kept) * half, half), :]
 
 
 def prep(core, rec, before, fields, snaps):
     width = fields * snaps
     cells = 2048
-    return pl.pallas_call(
-        functools.partial(prep_kernel, fields, snaps, len(before) // 2),
-        out_shape=(
-            jax.ShapeDtypeStruct((width, cells), BF16),
-            jax.ShapeDtypeStruct((width, cells), BF16),
-        )
-        + (jax.ShapeDtypeStruct((width // 2, width * (len(before) // 2 + 1)), F32),) * 2,
+    columns = width * (len(before) + 1)
+    return pl.pallas_call(
+        functools.partial(prep_kernel, fields, snaps),
+        out_shape=(jax.ShapeDtypeStruct((width, cells), F32),)
+        + (jax.ShapeDtypeStruct((width, cells), BF16),) * 2
+        + (jax.ShapeDtypeStruct((width // 2, columns), F32),) * 2,
         in_specs=[SMEM] + [VMEM] * (1 + len(before)),
-        out_specs=(VMEM,) * 4,
-        scratch_shapes=[pltpu.VMEM((width, width * (len(before) // 2 + 1)), F32)],
-        compiler_params=params(),
+        out_specs=(VMEM,) * 5,
+        scratch_shapes=[pltpu.VMEM((width, columns), F32)],
+        compiler_params=params(12),
         name="gram_blocks",
     )(core, rec, *before)
 
@@ -624,10 +597,10 @@
     return lax.ppermute(value, "core", [(0, 1), (1, 0)])
 
 
-def summed(value, axis, levels):
+def summed(value, axis, masks):
     size = lax.axis_size(axis)
-    for level in levels:
-        value = value + lax.ppermute(value, axis, [(i, i ^ 1 << level) for i in range(size)])
+    for mask in masks:
+        value = value + lax.ppermute(value, axis, [(i, i ^ mask) for i in range(size)])
     return value
 
 
@@ -668,25 +641,25 @@
     home_two = swap(records_two.reshape(block))
     hot = rank_hot(owners, owner_count, capacity)
     core = lax.axis_index("core").astype(jnp.int32).reshape(1)
-    both = (0, 1)
-    high_a, low_a, keep_a, send_a = prep(core, home_one.reshape(-1, lanes), (), fields, HALF)
+    both = (1, 3)
+    whole_a, high_a, low_a, keep_a, send_a = prep(core, home_one.reshape(-1, lanes), (), fields, HALF)
     part_a = summed(keep_a + swapped(send_a), "x", both)
     slots = pack(owners, hot, high_a, low_a, owner_count, 0)
     home_two, slots, part_a = lax.optimization_barrier((home_two, slots, part_a))
-    high_b, low_b, keep_b, send_b = prep(core, home_two.reshape(-1, lanes), (high_a, low_a), fields, HALF)
+    _, high_b, low_b, keep_b, send_b = prep(core, home_two.reshape(-1, lanes), (whole_a,), fields, HALF)
     quarters = 4
 
     def packed(slots, part, *values):
         slots = pack(owners, hot, high_b, low_b, owner_count, 1, slots, part, quarters)
         return lax.optimization_barrier((slots,) + values)
 
-    part_b = summed(keep_b + swapped(send_b), "x", (0,))
+    part_b = summed(keep_b + swapped(send_b), "x", (1,))
     slots, part_b = packed(slots, 0, part_b)
-    part_b = summed(part_b, "x", (1,))
+    part_b = summed(part_b, "x", (3,))
     slots, part_b, part_a = packed(slots, 1, part_b, part_a)
-    part = summed(jnp.concatenate([part_a, part_b], 1), "z", (0,))
+    part = summed(jnp.concatenate([part_a, part_b], 1), "z", (1,))
     slots, part = packed(slots, 2, part)
-    part = summed(part, "z", (1,))
+    part = summed(part, "z", (3,))
     slots, part = packed(slots, 3, part)
     panel = lax.all_to_all(slots, ("x", "z"), split_axis=0, concat_axis=0, tiled=True)
     part = summed(part, "y", both)

time: 184 us -> 184 us (level)
  starting transfers between devices: 59.3 us -> 52.2 us
  waiting for transfers between devices: 55.5 us -> 62.2 us
    ppermute x8, starting transfers between devices: 13.5 us -> 6.74 us  [summed(): lax.ppermute(value, axis, [(i, i ^ mask) for i in range(size)])]
    ppermute x8, waiting for transfers between devices: 15.8 us -> 18.9 us  [summed(): lax.ppermute(value, axis, [(i, i ^ mask) for i in range(size)])]
  transfers between devices with their start and end apart: 22 -> 22, of which waited for: 17 -> 19; matrix products, arithmetic and copies ran while one was open for 1% -> 1% of each run, Pallas kernels for 29% -> 29%
where the time goes in v6:
time: 184 us; the launch traced here: 183 us
  Pallas kernels  63.5 us (35%)
  waiting for transfers between devices  62.2 us (34%)
  starting transfers between devices  52.2 us (28%)
  local copies, waits for them, and re-layouts  3.36 us (2%)
    all_to_all x4, starting transfers between devices, swap(): return lax.all_to_all(value, plane, split_axis=0, concat_axis=0, tiled=True)  28.8 us
    ppermute x8, waiting for transfers between devices, summed(): lax.ppermute(value, axis, [(i, i ^ mask) for i in range(size)])  18.9 us
    all_to_all x4, waiting for transfers between devices, swap(): return lax.all_to_all(value, plane, split_axis=0, concat_axis=0, tiled=True)  18 us
    pallas_call x5, Pallas kernels, pack(): pl.pallas_call(functools.partial(pack_kernel, first), grid=(groups,), out...  14.9 us
    pallas_call x1, Pallas kernels, factor_trail(): pl.pallas_call(trail_kernel, out_shape=(jax.ShapeDtypeStruct((2 * order,...  14 us
    pallas_call x1, Pallas kernels, factor_lead(): pl.pallas_call(lead_kernel, out_shape=(jax.ShapeDtypeStruct((order, order...  12.4 us
    all_to_all x1, waiting for transfers between devices, on_device(): lax.all_to_all(slots, ('x', 'z'), split_axis=0, concat_axis=0, tiled=True)  11.8 us
    all_to_all x1, starting transfers between devices, on_device(): lax.all_to_all(slots, ('x', 'z'), split_axis=0, concat_axis=0, tiled=True)  7.5 us
  transfers between devices with their start and end apart: 22, of which 19 were waited for; matrix products, arithmetic and copies ran while one was open for 1% of the time, Pallas kernels for 29%

profile of v6, /device:TPU:64, one launch (start us, length us, event | category | flops | bytes accessed | tf_op | source)
XLA Modules:
  0.0 183.5 jit_solution(12160348810024617495)
XLA Ops:
  0.6 2.2 %opening_blocks.1 = f32[32,5,2,8,128]{4,3,2,1,0:T(8,128)} custom-call(f32[2,8,128]{2,1,0:T(8,128)} %visc_from.1, f32[32,2,8,128]{3,2,1,0:T(8,128)} %start_from.1, bf16[8,32,2,8,128]{4,3,2,1,0:T(8,128)(2,1)} %forcing_from.1), custom_call_target="tpu_custom_call" | custom-call | tf_op jit(solution)/shard_map/opening_blocks/pallas_call | solution.py:323
  2.8 7.8 %all-to-all-start.1 = ((f32[32,5,2,8,128]{4,3,2,1,0:T(8,128)}), f32[32,5,2,8,128]{4,3,2,1,0:T(8,128)S(1)}, u32[]{:S(2)}, u32[]{:S(2)}) async-start(f32[32,5,2,8,128]{4,3,2,1,0:T(8,128)} %opening_blocks.1), calls=%async_computation.1 | async-start | bytes 2621440 | tf_op jit(solution)/shard_map/all_to_all | solution.py:616
  11.7 17.0 %all-to-all-done.1 = f32[32,5,2,8,128]{4,3,2,1,0:T(8,128)S(1)} async-done(((f32[32,5,2,8,128]{4,3,2,1,0:T(8,128)}), f32[32,5,2,8,128]{4,3,2,1,0:T(8,128)S(1)}, u32[]{:S(2)}, u32[]{:S(2)}) %all-to-all-start.1) | async-done | bytes 1310752 | tf_op jit(solution)/shard_map/all_to_all | solution.py:616
  28.7 6.2 %all-to-all-start = ((f32[32,4,2,8,128]{4,3,2,1,0:T(8,128)}), f32[32,4,2,8,128]{4,3,2,1,0:T(8,128)}, u32[]{:S(2)}, u32[]{:S(2)}) async-start(f32[32,4,2,8,128]{4,3,2,1,0:T(8,128)} %convert_bitcast_fusion), calls=%async_computation | async-start | bytes 2097152 | tf_op jit(solution)/shard_map/all_to_all | solution.py:616
  37.3 1.7 collective-permute-start.3
  39.5 5.4 %collective-permute-done.2.low = f32[448,128]{1,0:T(8,128)S(1)} collective-permute-done((f32[448,128]{1,0:T(8,128)}, f32[448,128]{1,0:T(8,128)S(1)}, u32[]{:S(2)}, u32[]{:S(2)}) %collective-permute-start.2) | collective-permute-done | bytes 229408 | tf_op jit(solution)/shard_map/ppermute | solution.py:624
  46.5 2.9 %diffuse_first.1 = (f32[2048,128]{1,0:T(8,128)S(1)}, f32[32,2,8,128]{3,2,1,0:T(8,128)S(1)}, f32[20,2,8,128]{3,2,1,0:T(8,128)S(1)}) custom-call(s32[2]{0:T(128)S(1)} %add_convert_fusion.around, f32[2560,128]{1,0:T(8,128)S(1)} %bitcast.16, f32[448,128]{1,0:T(8,128)S(1)} %collective-permute-done.2.low, f32[448,128]{1,0:T(8,128)S(1)} %copy-done.2, ...), custom_call_target="tpu_custom_call" | custom-call | tf_op jit(solution)/shard_map/diffuse_first/pallas_call | solution.py:240
  50.5 7.4 %all-to-all-start.3 = ((f32[32,4,2,8,128]{4,3,2,1,0:T(8,128)}), f32[32,4,2,8,128]{4,3,2,1,0:T(8,128)S(1)}, u32[]{:S(2)}, u32[]{:S(2)}) async-start(f32[32,4,2,8,128]{4,3,2,1,0:T(8,128)} %bitcast.19), calls=%async_computation.3 | async-start | bytes 2097152 | tf_op jit(solution)/shard_map/all_to_all | solution.py:616
  59.2 1.6 collective-permute-start
  60.8 1.7 collective-permute-start.1
  62.5 1.8 collective-permute-start.5
  64.6 2.1 %collective-permute-done.low = f32[320,128]{1,0:T(8,128)S(1)} collective-permute-done((f32[320,128]{1,0:T(8,128)S(1)}, f32[320,128]{1,0:T(8,128)S(1)}, u32[]{:S(2)}, u32[]{:S(2)}) %collective-permute-start) | collective-permute-done | bytes 163872 | tf_op jit(solution)/shard_map/ppermute | solution.py:624
  68.1 1.7 collective-permute-done.4.start_low
  69.8 4.6 %diffuse_second.1 = f32[2048,128]{1,0:T(8,128)} custom-call(f32[2048,128]{1,0:T(8,128)} %bitcast.1.main, f32[320,128]{1,0:T(8,128)S(1)} %collective-permute-done.low, f32[320,128]{1,0:T(8,128)S(1)} %collective-permute-done.1.high, f32[32,2,8,128]{3,2,1,0:T(8,128)S(1)} %get-tuple-element.39.start, f32[8,2,8,128]{3,2,1,0:T(8,128)S(1)} %collective-permute-done.4.start_low, ...), custom_call_target="tpu_custom_call" | custom-call | tf_op jit(solution)/shard_map/diffuse_second/pallas_call | solution.py:257
  74.4 7.4 %all-to-all-start.2 = ((f32[32,4,2,8,128]{4,3,2,1,0:T(8,128)}), f32[32,4,2,8,128]{4,3,2,1,0:T(8,128)S(1)}, u32[]{:S(2)}, u32[]{:S(2)}) async-start(f32[32,4,2,8,128]{4,3,2,1,0:T(8,128)} %bitcast.5), calls=%async_computation.2 | async-start | bytes 2097152 | tf_op jit(solution)/shard_map/all_to_all | solution.py:616
  85.5 3.1 %collective-permute-done.7 = f32[64,128]{1,0:T(8,128)S(1)} collective-permute-done((f32[64,128]{1,0:T(8,128)S(1)}, f32[64,128]{1,0:T(8,128)S(1)}, u32[]{:S(2)}, u32[]{:S(2)}) %collective-permute-start.7) | collective-permute-done | bytes 32800 | tf_op jit(solution)/shard_map/ppermute | solution.py:603
  89.9 6.3 %pack_slots.5.refs_0_ = f32[16,256,256]{2,1,0:T(8,128)} custom-call(s32[16,128]{1,0:T(8,128)S(1)} %bitcast.21, bf16[256,2048]{1,0:T(8,128)(2,1)S(1)} %slot_ranks.1.hot, bf16[128,2048]{1,0:T(8,128)(2,1)S(1)} %get-tuple-element.42.high, bf16[128,2048]{1,0:T(8,128)(2,1)S(1)} %get-tuple-element.43.low), custom_call_target="tpu_custom_call" | custom-call | flops 4294967296 | bytes 2097152 | tf_op jit(solution)/shard_map/pack_slots/pallas_call | solution.py:447
  97.1 2.8 %gram_blocks.3 = (f32[128,2048]{1,0:T(8,128)}, bf16[128,2048]{1,0:T(8,128)(2,1)S(1)}, bf16[128,2048]{1,0:T(8,128)(2,1)S(1)}, f32[64,256]{1,0:T(8,128)S(1)}, f32[64,256]{1,0:T(8,128)S(1)}) custom-call(s32[1]{0:T(128)} %bitcast.7.core, f32[2048,128]{1,0:T(8,128)S(1)} %bitcast.17, f32[128,2048]{1,0:T(8,128)S(1)} %get-tuple-element.47.refs_1_), custom_call_target="tpu_custom_call" | custom-call | tf_op jit(solution)/shard_map/gram_blocks/pallas_call | solution.py:371
  101.3 2.2 %pack_slots.6.refs_0_ = f32[16,256,256]{2,1,0:T(8,128)} custom-call(s32[16,128]{1,0:T(8,128)S(1)} %bitcast.22, bf16[256,2048]{1,0:T(8,128)(2,1)S(1)} %slot_ranks.1.hot, bf16[128,2048]{1,0:T(8,128)(2,1)S(1)} %get-tuple-element.48.high, bf16[128,2048]{1,0:T(8,128)(2,1)S(1)} %get-tuple-element.49.low, ...), custom_call_target="tpu_custom_call", output_to_operand_aliasing={{}: (4, {})} | custom-call | flops 1073741824 | bytes 524288 | tf_op jit(solution)/shard_map/pack_slots/pallas_call | solution.py:447
  103.5 2.1 %collective-permute-done.10 = f32[64,256]{1,0:T(8,128)S(1)} collective-permute-done((f32[64,256]{1,0:T(8,128)S(1)}, f32[64,256]{1,0:T(8,128)S(1)}, u32[]{:S(2)}, u32[]{:S(2)}) %collective-permute-start.10) | collective-permute-done | bytes 65568 | tf_op jit(solution)/shard_map/ppermute | solution.py:603
  107.0 2.1 %pack_slots.7.refs_0_ = f32[16,256,256]{2,1,0:T(8,128)} custom-call(s32[16,128]{1,0:T(8,128)S(1)} %bitcast.23, bf16[256,2048]{1,0:T(8,128)(2,1)S(1)} %slot_ranks.1.hot, bf16[128,2048]{1,0:T(8,128)(2,1)S(1)} %get-tuple-element.48.high, bf16[128,2048]{1,0:T(8,128)(2,1)S(1)} %get-tuple-element.49.low, ...), custom_call_target="tpu_custom_call", output_to_operand_aliasing={{}: (4, {})} | custom-call | flops 1073741824 | bytes 524288 | tf_op jit(solution)/shard_map/pack_slots/pallas_call | solution.py:447
  109.2 2.0 %collective-permute-done.11 = f32[64,256]{1,0:T(8,128)S(1)} collective-permute-done((f32[64,256]{1,0:T(8,128)S(1)}, f32[64,256]{1,0:T(8,128)S(1)}, u32[]{:S(2)}, u32[]{:S(2)}) %collective-permute-start.11) | collective-permute-done | bytes 65568 | tf_op jit(solution)/shard_map/ppermute | solution.py:603
  112.5 2.1 %pack_slots.8.refs_0_ = f32[16,256,256]{2,1,0:T(8,128)} custom-call(s32[16,128]{1,0:T(8,128)S(1)} %bitcast.24, bf16[256,2048]{1,0:T(8,128)(2,1)S(1)} %slot_ranks.1.hot, bf16[128,2048]{1,0:T(8,128)(2,1)S(1)} %get-tuple-element.48.high, bf16[128,2048]{1,0:T(8,128)(2,1)S(1)} %get-tuple-element.49.low, ...), custom_call_target="tpu_custom_call", output_to_operand_aliasing={{}: (4, {})} | custom-call | flops 1073741824 | bytes 524288 | tf_op jit(solution)/shard_map/pack_slots/pallas_call | solution.py:447
  116.5 2.1 %pack_slots.9 = f32[16,256,256]{2,1,0:T(8,128)} custom-call(s32[16,128]{1,0:T(8,128)S(1)} %bitcast.25, bf16[256,2048]{1,0:T(8,128)(2,1)S(1)} %slot_ranks.1.hot, bf16[128,2048]{1,0:T(8,128)(2,1)S(1)} %get-tuple-element.48.high, bf16[128,2048]{1,0:T(8,128)(2,1)S(1)} %get-tuple-element.49.low, ...), custom_call_target="tpu_custom_call", output_to_operand_aliasing={{}: (4, {})} | custom-call | flops 1073741824 | bytes 524288 | tf_op jit(solution)/shard_map/pack_slots/pallas_call | solution.py:447
  118.7 1.9 %collective-permute-done.13 = f32[64,384]{1,0:T(8,128)S(1)} collective-permute-done((f32[64,384]{1,0:T(8,128)S(1)}, f32[64,384]{1,0:T(8,128)S(1)}, u32[]{:S(2)}, u32[]{:S(2)}) %collective-permute-start.13) | collective-permute-done | bytes 98336 | tf_op jit(solution)/shard_map/ppermute | solution.py:603
  120.6 7.5 %all-to-all-start.4 = ((f32[16,256,256]{2,1,0:T(8,128)}), f32[16,256,256]{2,1,0:T(8,128)}, u32[]{:S(2)}, u32[]{:S(2)}) async-start(f32[16,256,256]{2,1,0:T(8,128)} %pack_slots.9), calls=%async_computation.4 | async-start | bytes 8388608 | tf_op jit(solution)/shard_map/all_to_all | solution.py:664
  128.5 4.2 %collective-permute-done.14 = f32[64,384]{1,0:T(8,128)S(1)} collective-permute-done((f32[64,384]{1,0:T(8,128)S(1)}, f32[64,384]{1,0:T(8,128)S(1)}, u32[]{:S(2)}, u32[]{:S(2)}) %collective-permute-start.14) | collective-permute-done | bytes 98336 | tf_op jit(solution)/shard_map/ppermute | solution.py:603
  134.2 4.5 %collective-permute-done.15 = f32[64,384]{1,0:T(8,128)S(1)} collective-permute-done((f32[64,384]{1,0:T(8,128)S(1)}, f32[64,384]{1,0:T(8,128)S(1)}, u32[]{:S(2)}, u32[]{:S(2)}) %collective-permute-start.15) | collective-permute-done | bytes 98336 | tf_op jit(solution)/shard_map/ppermute | solution.py:603
  140.3 12.4 %factor_lead.1 = (f32[128,128]{1,0:T(8,128)S(1)}, f32[128,128]{1,0:T(8,128)S(1)}) custom-call(s32[1]{0:T(128)} %bitcast.7.core, f32[64,128]{1,0:T(8,128)S(1)} %slice.34.own, f32[64,128]{1,0:T(8,128)S(1)} %slice.35.other), custom_call_target="tpu_custom_call" | custom-call | tf_op jit(solution)/shard_map/factor_lead/pallas_call | solution.py:539
  152.7 14.0 %factor_trail.1 = (f32[256,256]{1,0:T(8,128)}, f32[256,256]{1,0:T(8,128)S(1)}) custom-call(s32[1]{0:T(128)} %bitcast.7.core, f32[64,256]{1,0:T(8,128)S(1)} %slice.32.own_half, f32[64,256]{1,0:T(8,128)S(1)} %slice.33.other_half, f32[128,128]{1,0:T(8,128)S(1)} %get-tuple-element.62.lead, f32[128,128]{1,0:T(8,128)S(1)} %get-tuple-element.63.lead_inv), custom_call_target="tpu_custom_call" | custom-call | tf_op jit(solution)/shard_map/factor_trail/pallas_call | solution.py:552
  166.7 11.8 %all-to-all-done.4.panel = f32[16,256,256]{2,1,0:T(8,128)} async-done(((f32[16,256,256]{2,1,0:T(8,128)}), f32[16,256,256]{2,1,0:T(8,128)}, u32[]{:S(2)}, u32[]{:S(2)}) %all-to-all-start.4) | async-done | bytes 4194336 | tf_op jit(solution)/shard_map/all_to_all | solution.py:664
  178.5 5.0 %basis_rows.1 = f32[4096,256]{1,0:T(8,128)} custom-call(f32[256,256]{1,0:T(8,128)S(1)} %get-tuple-element.65.inverse, f32[16,256,256]{2,1,0:T(8,128)} %all-to-all-done.4.panel), custom_call_target="tpu_custom_call" | custom-call | tf_op jit(solution)/shard_map/basis_rows/pallas_call | solution.py:578
  (59 shorter events, 25.0 us)
Async XLA Ops:
  0.6 10.0 %copy-start.4 = (bf16[8,32,2,8,128]{4,3,2,1,0:T(8,128)(2,1)S(1)}, bf16[8,32,2,8,128]{4,3,2,1,0:T(8,128)(2,1)}, u32[]{:S(2)}) copy-start(bf16[8,32,2,8,128]{4,3,2,1,0:T(8,128)(2,1)} %forcing_from.1) | copy-start | bytes 3145732
  2.8 25.9 %all-to-all-start.1 = ((f32[32,5,2,8,128]{4,3,2,1,0:T(8,128)}), f32[32,5,2,8,128]{4,3,2,1,0:T(8,128)S(1)}, u32[]{:S(2)}, u32[]{:S(2)}) async-start(f32[32,5,2,8,128]{4,3,2,1,0:T(8,128)} %opening_blocks.1), calls=%async_computation.1 | async-start | bytes 2621440 | tf_op jit(solution)/shard_map/all_to_all | solution.py:616
  28.7 21.7 %all-to-all-start = ((f32[32,4,2,8,128]{4,3,2,1,0:T(8,128)}), f32[32,4,2,8,128]{4,3,2,1,0:T(8,128)}, u32[]{:S(2)}, u32[]{:S(2)}) async-start(f32[32,4,2,8,128]{4,3,2,1,0:T(8,128)} %convert_bitcast_fusion), calls=%async_computation | async-start | bytes 2097152 | tf_op jit(solution)/shard_map/all_to_all | solution.py:616
  35.8 9.1 %collective-permute-start.2 = (f32[448,128]{1,0:T(8,128)}, f32[448,128]{1,0:T(8,128)S(1)}, u32[]{:S(2)}, u32[]{:S(2)}) collective-permute-start(f32[448,128]{1,0:T(8,128)} %get-tuple-element.37), channel_id=1, source_target_pairs={{0,4},{4,8},{8,12},{12,0},{1,5},{5,9},{9,13},{13,1},{2,6},{6,10},{... | collective-permute-start | bytes 688136 | tf_op jit(solution)/shard_map/ppermute | solution.py:624
  37.3 7.6 %collective-permute-start.3 = (f32[448,128]{1,0:T(8,128)}, f32[448,128]{1,0:T(8,128)S(1)}, u32[]{:S(2)}, u32[]{:S(2)}) collective-permute-start(f32[448,128]{1,0:T(8,128)} %get-tuple-element.38), channel_id=1, source_target_pairs={{0,12},{4,0},{8,4},{12,8},{1,13},{5,1},{9,5},{13,9},{2,14},{6,2},{... | collective-permute-start | bytes 688136 | tf_op jit(solution)/shard_map/ppermute | solution.py:624
  44.9 0.7 copy-start.1
  45.6 0.9 copy-start.2
  49.5 1.0 copy-start
  50.5 23.9 %all-to-all-start.3 = ((f32[32,4,2,8,128]{4,3,2,1,0:T(8,128)}), f32[32,4,2,8,128]{4,3,2,1,0:T(8,128)S(1)}, u32[]{:S(2)}, u32[]{:S(2)}) async-start(f32[32,4,2,8,128]{4,3,2,1,0:T(8,128)} %bitcast.19), calls=%async_computation.3 | async-start | bytes 2097152 | tf_op jit(solution)/shard_map/all_to_all | solution.py:616
  59.2 25.4 %copy-start.3 = (s32[1,1,2048,1]{2,3,1,0:T(1,128)S(1)}, s32[1,1,2048,1]{2,3,1,0:T(1,128)}, u32[]{:S(2)}) copy-start(s32[1,1,2048,1]{2,3,1,0:T(1,128)} %param.7) | copy-start | bytes 24580
  59.2 7.5 %collective-permute-start = (f32[320,128]{1,0:T(8,128)S(1)}, f32[320,128]{1,0:T(8,128)S(1)}, u32[]{:S(2)}, u32[]{:S(2)}) collective-permute-start(f32[320,128]{1,0:T(8,128)S(1)} %get-tuple-element.35), channel_id=1, source_target_pairs={{0,4},{4,8},{8,12},{12,0},{1,5},{5,9},{9,13},{13,1},{2,6},{6,10},{... | collective-permute-start | bytes 491528 | tf_op jit(solution)/shard_map/ppermute | solution.py:624
  60.8 6.7 %collective-permute-start.1 = (f32[320,128]{1,0:T(8,128)S(1)}, f32[320,128]{1,0:T(8,128)S(1)}, u32[]{:S(2)}, u32[]{:S(2)}) collective-permute-start(f32[320,128]{1,0:T(8,128)S(1)} %get-tuple-element.36), channel_id=1, source_target_pairs={{0,12},{4,0},{8,4},{12,8},{1,13},{5,1},{9,5},{13,9},{2,14},{6,2},{... | collective-permute-start | bytes 491528 | tf_op jit(solution)/shard_map/ppermute | solution.py:624
  62.5 5.6 %collective-permute-start.5 = (f32[8,2,8,128]{3,2,1,0:T(8,128)S(1)}, f32[8,2,8,128]{3,2,1,0:T(8,128)S(1)}, u32[]{:S(2)}, u32[]{:S(2)}) collective-permute-start(f32[8,2,8,128]{3,2,1,0:T(8,128)S(1)} %get-tuple-element.67), channel_id=1, source_target_pairs={{0,12},{4,0},{8,4},{12,8},{1,13},{5,1},{9,5},{13,9},{2,14},{6,2},{... | collective-permute-start | bytes 196616 | tf_op jit(solution)/shard_map/ppermute | solution.py:635
  64.3 5.5 %collective-permute-start.4 = (f32[8,2,8,128]{3,2,1,0:T(8,128)S(1)}, f32[8,2,8,128]{3,2,1,0:T(8,128)S(1)}, u32[]{:S(2)}, u32[]{:S(2)}) collective-permute-start(f32[8,2,8,128]{3,2,1,0:T(8,128)S(1)} %get-tuple-element.68), channel_id=1, source_target_pairs={{0,4},{4,8},{8,12},{12,0},{1,5},{5,9},{9,13},{13,1},{2,6},{6,10},{... | collective-permute-start | bytes 196616 | tf_op jit(solution)/shard_map/ppermute | solution.py:634
  74.4 22.7 %all-to-all-start.2 = ((f32[32,4,2,8,128]{4,3,2,1,0:T(8,128)}), f32[32,4,2,8,128]{4,3,2,1,0:T(8,128)S(1)}, u32[]{:S(2)}, u32[]{:S(2)}) async-start(f32[32,4,2,8,128]{4,3,2,1,0:T(8,128)} %bitcast.5), calls=%async_computation.2 | async-start | bytes 2097152 | tf_op jit(solution)/shard_map/all_to_all | solution.py:616
  83.3 1.3 collective-permute-start.6
  84.6 3.9 %collective-permute-start.7 = (f32[64,128]{1,0:T(8,128)S(1)}, f32[64,128]{1,0:T(8,128)S(1)}, u32[]{:S(2)}, u32[]{:S(2)}) collective-permute-start(f32[64,128]{1,0:T(8,128)S(1)} %add.30), channel_id=1, source_target_pairs={{0,4},{4,0},{8,12},{12,8},{1,5},{5,1},{9,13},{13,9},{2,6},{6,2},{1... | collective-permute-start | bytes 98312 | tf_op jit(solution)/shard_map/ppermute | solution.py:603
  88.6 7.6 %collective-permute-start.8 = (f32[64,128]{1,0:T(8,128)S(1)}, f32[64,128]{1,0:T(8,128)S(1)}, u32[]{:S(2)}, u32[]{:S(2)}) collective-permute-start(f32[64,128]{1,0:T(8,128)S(1)} %add.31), channel_id=1, source_target_pairs={{0,12},{4,8},{8,4},{12,0},{1,13},{5,9},{9,5},{13,1},{2,14},{6,10},... | collective-permute-start | bytes 98312 | tf_op jit(solution)/shard_map/ppermute | solution.py:603
  99.9 1.3 collective-permute-start.9
  101.2 4.3 %collective-permute-start.10 = (f32[64,256]{1,0:T(8,128)S(1)}, f32[64,256]{1,0:T(8,128)S(1)}, u32[]{:S(2)}, u32[]{:S(2)}) collective-permute-start(f32[64,256]{1,0:T(8,128)S(1)} %add.33), channel_id=1, source_target_pairs={{0,4},{4,0},{8,12},{12,8},{1,5},{5,1},{9,13},{13,9},{2,6},{6,2},{1... | collective-permute-start | bytes 196616 | tf_op jit(solution)/shard_map/ppermute | solution.py:603
  105.6 5.6 %collective-permute-start.11 = (f32[64,256]{1,0:T(8,128)S(1)}, f32[64,256]{1,0:T(8,128)S(1)}, u32[]{:S(2)}, u32[]{:S(2)}) collective-permute-start(f32[64,256]{1,0:T(8,128)S(1)} %add.34), channel_id=1, source_target_pairs={{0,12},{4,8},{8,4},{12,0},{1,13},{5,9},{9,5},{13,1},{2,14},{6,10},... | collective-permute-start | bytes 196616 | tf_op jit(solution)/shard_map/ppermute | solution.py:603
  111.2 4.7 %collective-permute-start.12 = (f32[64,384]{1,0:T(8,128)S(1)}, f32[64,384]{1,0:T(8,128)S(1)}, u32[]{:S(2)}, u32[]{:S(2)}) collective-permute-start(f32[64,384]{1,0:T(8,128)S(1)} %constant_dynamic-update-slice_fusion), channel_id=1, source_target_pairs={{0,1},{1,0},{2,3},{3,2},{4,5},{5,4},{6,7},{7,6},{8,9},{9,8},{10,11... | collective-permute-start | bytes 294920 | tf_op jit(solution)/shard_map/ppermute | solution.py:603
  115.9 4.7 %collective-permute-start.13 = (f32[64,384]{1,0:T(8,128)S(1)}, f32[64,384]{1,0:T(8,128)S(1)}, u32[]{:S(2)}, u32[]{:S(2)}) collective-permute-start(f32[64,384]{1,0:T(8,128)S(1)} %add.36), channel_id=1, source_target_pairs={{0,3},{1,2},{2,1},{3,0},{4,7},{5,6},{6,5},{7,4},{8,11},{9,10},{10,... | collective-permute-start | bytes 294920 | tf_op jit(solution)/shard_map/ppermute | solution.py:603
  120.6 57.9 %all-to-all-start.4 = ((f32[16,256,256]{2,1,0:T(8,128)}), f32[16,256,256]{2,1,0:T(8,128)}, u32[]{:S(2)}, u32[]{:S(2)}) async-start(f32[16,256,256]{2,1,0:T(8,128)} %pack_slots.9), calls=%async_computation.4 | async-start | bytes 8388608 | tf_op jit(solution)/shard_map/all_to_all | solution.py:664
  128.1 4.6 %collective-permute-start.14 = (f32[64,384]{1,0:T(8,128)S(1)}, f32[64,384]{1,0:T(8,128)S(1)}, u32[]{:S(2)}, u32[]{:S(2)}) collective-permute-start(f32[64,384]{1,0:T(8,128)S(1)} %add.37), channel_id=1, source_target_pairs={{0,32},{32,0},{64,96},{96,64},{1,33},{33,1},{65,97},{97,65},{2,34}... | collective-permute-start | bytes 294920 | tf_op jit(solution)/shard_map/ppermute | solution.py:603
  132.7 5.9 %collective-permute-start.15 = (f32[64,384]{1,0:T(8,128)S(1)}, f32[64,384]{1,0:T(8,128)S(1)}, u32[]{:S(2)}, u32[]{:S(2)}) collective-permute-start(f32[64,384]{1,0:T(8,128)S(1)} %add.38), channel_id=1, source_target_pairs={{0,96},{32,64},{64,32},{96,0},{1,97},{33,65},{65,33},{97,1},{2,98}... | collective-permute-start | bytes 294920 | tf_op jit(solution)/shard_map/ppermute | solution.py:603
  138.7 1.6 collective-permute-start.16

commit v7 on v6

--- a/solution.py
+++ b/solution.py
@@ -338,22 +338,15 @@
     )(visc, start, forcing)
 
 
-def prep_kernel(fields, snaps, core, *refs):
-    rec, before = refs[0], refs[1:-6]
-    whole, high_out, low_out, keep, send, gram = refs[-6:]
+def gram_kernel(fields, snaps, core, *refs):
+    rec, before = refs[0], refs[1:-4]
+    whole, keep, send, gram = refs[-4:]
     for cell_row in range(16):
         for s in range(snaps):
-            for f in range(0, fields, 16):
-                parts = [
-                    rec[pl.ds(((f + g) * snaps + s) * 16 + cell_row, 8, stride=snaps * 16), :]
-                    for g in (0, 8)
-                ]
-                value = jnp.concatenate(parts, 0)
-                high, low = split(value)
-                at = (slice(s * fields + f, s * fields + f + 16), slice(cell_row * 128, cell_row * 128 + 128))
+            for f in range(0, fields, 8):
+                value = rec[pl.ds((f * snaps + s) * 16 + cell_row, 8, stride=snaps * 16), :]
+                at = (slice(s * fields + f, s * fields + f + 8), slice(cell_row * 128, cell_row * 128 + 128))
                 whole[at] = value
-                high_out[at] = high
-                low_out[at] = low
     width = fields * snaps
     mine = whole[...]
     for c, other in enumerate(before + (whole,)):
@@ -364,21 +357,37 @@
     send[...] = gram[pl.ds((1 - kept) * half, half), :]
 
 
-def prep(core, rec, before, fields, snaps):
+def gram_of(core, rec, before, fields, snaps):
     width = fields * snaps
     cells = 2048
     columns = width * (len(before) + 1)
     return pl.pallas_call(
-        functools.partial(prep_kernel, fields, snaps),
+        functools.partial(gram_kernel, fields, snaps),
         out_shape=(jax.ShapeDtypeStruct((width, cells), F32),)
-        + (jax.ShapeDtypeStruct((width, cells), BF16),) * 2
         + (jax.ShapeDtypeStruct((width // 2, columns), F32),) * 2,
         in_specs=[SMEM] + [VMEM] * (1 + len(before)),
-        out_specs=(VMEM,) * 5,
+        out_specs=(VMEM,) * 3,
         scratch_shapes=[pltpu.VMEM((width, columns), F32)],
         compiler_params=params(12),
         name="gram_blocks",
     )(core, rec, *before)
+
+
+def terms_kernel(whole, high_out, low_out):
+    high, low = split(whole[...])
+    high_out[...] = high
+    low_out[...] = low
+
+
+def terms_of(whole):
+    return pl.pallas_call(
+        terms_kernel,
+        out_shape=(jax.ShapeDtypeStruct(whole.shape, BF16),) * 2,
+        in_specs=[VMEM],
+        out_specs=(VMEM,) * 2,
+        compiler_params=params(),
+        name="two_terms",
+    )(whole)
 
 
 def rank_kernel(owner_count, owners, hot):
@@ -642,11 +651,13 @@
     hot = rank_hot(owners, owner_count, capacity)
     core = lax.axis_index("core").astype(jnp.int32).reshape(1)
     both = (1, 3)
-    whole_a, high_a, low_a, keep_a, send_a = prep(core, home_one.reshape(-1, lanes), (), fields, HALF)
+    whole_a, keep_a, send_a = gram_of(core, home_one.reshape(-1, lanes), (), fields, HALF)
+    high_a, low_a = terms_of(whole_a)
     part_a = summed(keep_a + swapped(send_a), "x", both)
     slots = pack(owners, hot, high_a, low_a, owner_count, 0)
     home_two, slots, part_a = lax.optimization_barrier((home_two, slots, part_a))
-    _, high_b, low_b, keep_b, send_b = prep(core, home_two.reshape(-1, lanes), (whole_a,), fields, HALF)
+    whole_b, keep_b, send_b = gram_of(core, home_two.reshape(-1, lanes), (whole_a,), fields, HALF)
+    high_b, low_b = terms_of(whole_b)
     quarters = 4
 
     def packed(slots, part, *values):
@@ -654,17 +665,17 @@
         return lax.optimization_barrier((slots,) + values)
 
     part_b = summed(keep_b + swapped(send_b), "x", (1,))
-    slots, part_b = packed(slots, 0, part_b)
-    part_b = summed(part_b, "x", (3,))
-    slots, part_b, part_a = packed(slots, 1, part_b, part_a)
+    slots, part_a, part_b = packed(slots, 0, part_a, part_b)
     part = summed(jnp.concatenate([part_a, part_b], 1), "z", (1,))
-    slots, part = packed(slots, 2, part)
-    part = summed(part, "z", (3,))
+    slots, part = packed(slots, 1, part)
+    width = fields * HALF
+    part_a, part_b = part[:, :width], summed(part[:, width:], "x", (3,))
+    slots, part_a, part_b = packed(slots, 2, part_a, part_b)
+    part = summed(jnp.concatenate([part_a, part_b], 1), "z", (3,))
     slots, part = packed(slots, 3, part)
     panel = lax.all_to_all(slots, ("x", "z"), split_axis=0, concat_axis=0, tiled=True)
     part = summed(part, "y", both)
     other = swapped(part)
-    width = fields * HALF
     lead, lead_inv = factor_lead(core, part[:, :width], other[:, :width])
     r_factor, inverse = factor_trail(core, part[:, width:], other[:, width:], lead, lead_inv)
     basis = basis_of(inverse, panel)

time: 184 us -> 183 us (level)
  waiting for transfers between devices: 62.2 us -> 56.2 us
  starting transfers between devices: 52.2 us -> 57.3 us
    ppermute x8, starting transfers between devices: 6.74 us -> 11 us  [summed(): lax.ppermute(value, axis, [(i, i ^ mask) for i in range(size)])]
    ppermute x8, waiting for transfers between devices: 18.9 us -> 16.3 us  [summed(): lax.ppermute(value, axis, [(i, i ^ mask) for i in range(size)])]
    pallas_call x2 -> x4, Pallas kernels: 4.33 us -> 3.94 us  [the longest x2 3.63 us: gram_of(): pl.pallas_call(functools.partial(gram_kernel, fields, snaps), out_shape=(...]
  transfers between devices with their start and end apart: 22 -> 22, of which waited for: 19 -> 18; matrix products, arithmetic and copies ran while one was open for 1% -> 1% of each run, Pallas kernels for 29% -> 30%
where the time goes in v7:
time: 183 us; the launch traced here: 182 us
  Pallas kernels  63.1 us (34%)
  starting transfers between devices  57.3 us (31%)
  waiting for transfers between devices  56.2 us (31%)
  local copies, waits for them, and re-layouts  3.38 us (2%)
    all_to_all x4, starting transfers between devices, swap(): return lax.all_to_all(value, plane, split_axis=0, concat_axis=0, tiled=True)  28.3 us
    all_to_all x4, waiting for transfers between devices, swap(): return lax.all_to_all(value, plane, split_axis=0, concat_axis=0, tiled=True)  17.7 us
    ppermute x8, waiting for transfers between devices, summed(): lax.ppermute(value, axis, [(i, i ^ mask) for i in range(size)])  16.3 us
    pallas_call x5, Pallas kernels, pack(): pl.pallas_call(functools.partial(pack_kernel, first), grid=(groups,), out...  14.8 us
    pallas_call x1, Pallas kernels, factor_trail(): pl.pallas_call(trail_kernel, out_shape=(jax.ShapeDtypeStruct((2 * order,...  14 us
    pallas_call x1, Pallas kernels, factor_lead(): pl.pallas_call(lead_kernel, out_shape=(jax.ShapeDtypeStruct((order, order...  12.4 us
    all_to_all x1, waiting for transfers between devices, on_device(): lax.all_to_all(slots, ('x', 'z'), split_axis=0, concat_axis=0, tiled=True)  11.8 us
    ppermute x8, starting transfers between devices, summed(): lax.ppermute(value, axis, [(i, i ^ mask) for i in range(size)])  11 us
  transfers between devices with their start and end apart: 22, of which 18 were waited for; matrix products, arithmetic and copies ran while one was open for 1% of the time, Pallas kernels for 30%

profile of v7, /device:TPU:64, one launch (start us, length us, event | category | flops | bytes accessed | tf_op | source)
XLA Modules:
  0.0 182.2 jit_solution(8313217462038434898)
XLA Ops:
  0.6 2.2 %opening_blocks.1 = f32[32,5,2,8,128]{4,3,2,1,0:T(8,128)} custom-call(f32[2,8,128]{2,1,0:T(8,128)} %visc_from.1, f32[32,2,8,128]{3,2,1,0:T(8,128)} %start_from.1, bf16[8,32,2,8,128]{4,3,2,1,0:T(8,128)(2,1)} %forcing_from.1), custom_call_target="tpu_custom_call" | custom-call | tf_op jit(solution)/shard_map/opening_blocks/pallas_call | solution.py:323
  2.8 7.8 %all-to-all-start.1 = ((f32[32,5,2,8,128]{4,3,2,1,0:T(8,128)}), f32[32,5,2,8,128]{4,3,2,1,0:T(8,128)S(1)}, u32[]{:S(2)}, u32[]{:S(2)}) async-start(f32[32,5,2,8,128]{4,3,2,1,0:T(8,128)} %opening_blocks.1), calls=%async_computation.1 | async-start | bytes 2621440 | tf_op jit(solution)/shard_map/all_to_all | solution.py:625
  11.7 17.1 %all-to-all-done.1 = f32[32,5,2,8,128]{4,3,2,1,0:T(8,128)S(1)} async-done(((f32[32,5,2,8,128]{4,3,2,1,0:T(8,128)}), f32[32,5,2,8,128]{4,3,2,1,0:T(8,128)S(1)}, u32[]{:S(2)}, u32[]{:S(2)}) %all-to-all-start.1) | async-done | bytes 1310752 | tf_op jit(solution)/shard_map/all_to_all | solution.py:625
  28.7 6.2 %all-to-all-start = ((f32[32,4,2,8,128]{4,3,2,1,0:T(8,128)}), f32[32,4,2,8,128]{4,3,2,1,0:T(8,128)}, u32[]{:S(2)}, u32[]{:S(2)}) async-start(f32[32,4,2,8,128]{4,3,2,1,0:T(8,128)} %convert_bitcast_fusion), calls=%async_computation | async-start | bytes 2097152 | tf_op jit(solution)/shard_map/all_to_all | solution.py:625
  37.3 1.7 collective-permute-start.3
  39.5 5.4 %collective-permute-done.2.low = f32[448,128]{1,0:T(8,128)S(1)} collective-permute-done((f32[448,128]{1,0:T(8,128)}, f32[448,128]{1,0:T(8,128)S(1)}, u32[]{:S(2)}, u32[]{:S(2)}) %collective-permute-start.2) | collective-permute-done | bytes 229408 | tf_op jit(solution)/shard_map/ppermute | solution.py:633
  46.5 2.9 %diffuse_first.1 = (f32[2048,128]{1,0:T(8,128)S(1)}, f32[32,2,8,128]{3,2,1,0:T(8,128)S(1)}, f32[20,2,8,128]{3,2,1,0:T(8,128)S(1)}) custom-call(s32[2]{0:T(128)S(1)} %add_convert_fusion.around, f32[2560,128]{1,0:T(8,128)S(1)} %bitcast.16, f32[448,128]{1,0:T(8,128)S(1)} %collective-permute-done.2.low, f32[448,128]{1,0:T(8,128)S(1)} %copy-done.2, ...), custom_call_target="tpu_custom_call" | custom-call | tf_op jit(solution)/shard_map/diffuse_first/pallas_call | solution.py:240
  50.5 7.4 %all-to-all-start.3 = ((f32[32,4,2,8,128]{4,3,2,1,0:T(8,128)}), f32[32,4,2,8,128]{4,3,2,1,0:T(8,128)S(1)}, u32[]{:S(2)}, u32[]{:S(2)}) async-start(f32[32,4,2,8,128]{4,3,2,1,0:T(8,128)} %bitcast.19), calls=%async_computation.3 | async-start | bytes 2097152 | tf_op jit(solution)/shard_map/all_to_all | solution.py:625
  59.2 1.6 collective-permute-start
  60.8 1.7 collective-permute-start.1
  62.9 3.0 %collective-permute-start.5 = (f32[8,2,8,128]{3,2,1,0:T(8,128)S(1)}, f32[8,2,8,128]{3,2,1,0:T(8,128)S(1)}, u32[]{:S(2)}, u32[]{:S(2)}) collective-permute-start(f32[8,2,8,128]{3,2,1,0:T(8,128)S(1)} %get-tuple-element.71), channel_id=1, source_target_pairs={{0,12},{4,0},{8,4},{12,8},{1,13},{5,1},{9,5},{13,9},{2,14},{6,2},{... | collective-permute-start | bytes 196616 | tf_op jit(solution)/shard_map/ppermute | solution.py:644
  65.8 1.5 collective-permute-done.low
  68.2 4.6 %diffuse_second.1 = f32[2048,128]{1,0:T(8,128)} custom-call(f32[2048,128]{1,0:T(8,128)} %bitcast.1.main, f32[320,128]{1,0:T(8,128)S(1)} %collective-permute-done.low, f32[320,128]{1,0:T(8,128)S(1)} %collective-permute-done.1.high, f32[32,2,8,128]{3,2,1,0:T(8,128)S(1)} %get-tuple-element.41.start, f32[8,2,8,128]{3,2,1,0:T(8,128)S(1)} %collective-permute-done.4.start_low, ...), custom_call_target="tpu_custom_call" | custom-call | tf_op jit(solution)/shard_map/diffuse_second/pallas_call | solution.py:257
  73.3 6.8 %all-to-all-start.2 = ((f32[32,4,2,8,128]{4,3,2,1,0:T(8,128)}), f32[32,4,2,8,128]{4,3,2,1,0:T(8,128)S(1)}, u32[]{:S(2)}, u32[]{:S(2)}) async-start(f32[32,4,2,8,128]{4,3,2,1,0:T(8,128)} %bitcast.5), calls=%async_computation.2 | async-start | bytes 2097152 | tf_op jit(solution)/shard_map/all_to_all | solution.py:625
  85.1 1.7 collective-permute-done.7
  86.8 3.2 %collective-permute-start.8 = (f32[64,128]{1,0:T(8,128)S(1)}, f32[64,128]{1,0:T(8,128)S(1)}, u32[]{:S(2)}, u32[]{:S(2)}) collective-permute-start(f32[64,128]{1,0:T(8,128)S(1)} %add.31), channel_id=1, source_target_pairs={{0,12},{4,8},{8,4},{12,0},{1,13},{5,9},{9,5},{13,1},{2,14},{6,10},... | collective-permute-start | bytes 98312 | tf_op jit(solution)/shard_map/ppermute | solution.py:612
  90.0 6.3 %pack_slots.5.refs_0_ = f32[16,256,256]{2,1,0:T(8,128)} custom-call(s32[16,128]{1,0:T(8,128)S(1)} %bitcast.21, bf16[256,2048]{1,0:T(8,128)(2,1)S(1)} %slot_ranks.1.hot, bf16[128,2048]{1,0:T(8,128)(2,1)S(1)} %get-tuple-element.45.high, bf16[128,2048]{1,0:T(8,128)(2,1)S(1)} %get-tuple-element.46.low), custom_call_target="tpu_custom_call" | custom-call | flops 4294967296 | bytes 2097152 | tf_op jit(solution)/shard_map/pack_slots/pallas_call | solution.py:456
  96.3 2.2 %gram_blocks.3 = (f32[128,2048]{1,0:T(8,128)S(1)}, f32[64,256]{1,0:T(8,128)S(1)}, f32[64,256]{1,0:T(8,128)S(1)}) custom-call(s32[1]{0:T(128)} %bitcast.7.core, f32[2048,128]{1,0:T(8,128)S(1)} %bitcast.17, f32[128,2048]{1,0:T(8,128)S(1)} %get-tuple-element.44.whole.refs_1_), custom_call_target="tpu_custom_call" | custom-call | tf_op jit(solution)/shard_map/gram_blocks/pallas_call | solution.py:364
  100.3 2.1 %pack_slots.6.refs_0_ = f32[16,256,256]{2,1,0:T(8,128)} custom-call(s32[16,128]{1,0:T(8,128)S(1)} %bitcast.22, bf16[256,2048]{1,0:T(8,128)(2,1)S(1)} %slot_ranks.1.hot, bf16[128,2048]{1,0:T(8,128)(2,1)S(1)} %get-tuple-element.51.high, bf16[128,2048]{1,0:T(8,128)(2,1)S(1)} %get-tuple-element.52.low, ...), custom_call_target="tpu_custom_call", output_to_operand_aliasing={{}: (4, {})} | custom-call | flops 1073741824 | bytes 524288 | tf_op jit(solution)/shard_map/pack_slots/pallas_call | solution.py:456
  102.4 1.7 collective-permute-done.10
  105.4 2.1 %pack_slots.7.refs_0_ = f32[16,256,256]{2,1,0:T(8,128)} custom-call(s32[16,128]{1,0:T(8,128)S(1)} %bitcast.23, bf16[256,2048]{1,0:T(8,128)(2,1)S(1)} %slot_ranks.1.hot, bf16[128,2048]{1,0:T(8,128)(2,1)S(1)} %get-tuple-element.51.high, bf16[128,2048]{1,0:T(8,128)(2,1)S(1)} %get-tuple-element.52.low, ...), custom_call_target="tpu_custom_call", output_to_operand_aliasing={{}: (4, {})} | custom-call | flops 1073741824 | bytes 524288 | tf_op jit(solution)/shard_map/pack_slots/pallas_call | solution.py:456
  108.9 2.4 %collective-permute-start.12 = (f32[64,256]{1,0:T(8,128)S(1)}, f32[64,256]{1,0:T(8,128)S(1)}, u32[]{:S(2)}, u32[]{:S(2)}) collective-permute-start(f32[64,256]{1,0:T(8,128)S(1)} %slice.35), channel_id=1, source_target_pairs={{0,12},{4,8},{8,4},{12,0},{1,13},{5,9},{9,5},{13,1},{2,14},{6,10},... | collective-permute-start | bytes 196616 | tf_op jit(solution)/shard_map/ppermute | solution.py:612
  111.3 2.1 %pack_slots.8.refs_0_ = f32[16,256,256]{2,1,0:T(8,128)} custom-call(s32[16,128]{1,0:T(8,128)S(1)} %bitcast.24, bf16[256,2048]{1,0:T(8,128)(2,1)S(1)} %slot_ranks.1.hot, bf16[128,2048]{1,0:T(8,128)(2,1)S(1)} %get-tuple-element.51.high, bf16[128,2048]{1,0:T(8,128)(2,1)S(1)} %get-tuple-element.52.low, ...), custom_call_target="tpu_custom_call", output_to_operand_aliasing={{}: (4, {})} | custom-call | flops 1073741824 | bytes 524288 | tf_op jit(solution)/shard_map/pack_slots/pallas_call | solution.py:456
  115.2 2.1 %pack_slots.9 = f32[16,256,256]{2,1,0:T(8,128)} custom-call(s32[16,128]{1,0:T(8,128)S(1)} %bitcast.25, bf16[256,2048]{1,0:T(8,128)(2,1)S(1)} %slot_ranks.1.hot, bf16[128,2048]{1,0:T(8,128)(2,1)S(1)} %get-tuple-element.51.high, bf16[128,2048]{1,0:T(8,128)(2,1)S(1)} %get-tuple-element.52.low, ...), custom_call_target="tpu_custom_call", output_to_operand_aliasing={{}: (4, {})} | custom-call | flops 1073741824 | bytes 524288 | tf_op jit(solution)/shard_map/pack_slots/pallas_call | solution.py:456
  117.3 1.9 %collective-permute-done.13 = f32[64,384]{1,0:T(8,128)S(1)} collective-permute-done((f32[64,384]{1,0:T(8,128)S(1)}, f32[64,384]{1,0:T(8,128)S(1)}, u32[]{:S(2)}, u32[]{:S(2)}) %collective-permute-start.13) | collective-permute-done | bytes 98336 | tf_op jit(solution)/shard_map/ppermute | solution.py:612
  119.2 7.6 %all-to-all-start.4 = ((f32[16,256,256]{2,1,0:T(8,128)}), f32[16,256,256]{2,1,0:T(8,128)}, u32[]{:S(2)}, u32[]{:S(2)}) async-start(f32[16,256,256]{2,1,0:T(8,128)} %pack_slots.9), calls=%async_computation.4 | async-start | bytes 8388608 | tf_op jit(solution)/shard_map/all_to_all | solution.py:676
  127.4 4.1 %collective-permute-done.14 = f32[64,384]{1,0:T(8,128)S(1)} collective-permute-done((f32[64,384]{1,0:T(8,128)S(1)}, f32[64,384]{1,0:T(8,128)S(1)}, u32[]{:S(2)}, u32[]{:S(2)}) %collective-permute-start.14) | collective-permute-done | bytes 98336 | tf_op jit(solution)/shard_map/ppermute | solution.py:612
  132.7 4.6 %collective-permute-done.15 = f32[64,384]{1,0:T(8,128)S(1)} collective-permute-done((f32[64,384]{1,0:T(8,128)S(1)}, f32[64,384]{1,0:T(8,128)S(1)}, u32[]{:S(2)}, u32[]{:S(2)}) %collective-permute-start.15) | collective-permute-done | bytes 98336 | tf_op jit(solution)/shard_map/ppermute | solution.py:612
  139.0 12.4 %factor_lead.1 = (f32[128,128]{1,0:T(8,128)S(1)}, f32[128,128]{1,0:T(8,128)S(1)}) custom-call(s32[1]{0:T(128)} %bitcast.7.core, f32[64,128]{1,0:T(8,128)S(1)} %slice.42.own, f32[64,128]{1,0:T(8,128)S(1)} %slice.43.other), custom_call_target="tpu_custom_call" | custom-call | tf_op jit(solution)/shard_map/factor_lead/pallas_call | solution.py:548
  151.4 14.0 %factor_trail.1 = (f32[256,256]{1,0:T(8,128)}, f32[256,256]{1,0:T(8,128)S(1)}) custom-call(s32[1]{0:T(128)} %bitcast.7.core, f32[64,256]{1,0:T(8,128)S(1)} %slice.40.own_half, f32[64,256]{1,0:T(8,128)S(1)} %slice.41.other_half, f32[128,128]{1,0:T(8,128)S(1)} %get-tuple-element.66.lead, f32[128,128]{1,0:T(8,128)S(1)} %get-tuple-element.67.lead_inv), custom_call_target="tpu_custom_call" | custom-call | tf_op jit(solution)/shard_map/factor_trail/pallas_call | solution.py:561
  165.4 11.8 %all-to-all-done.4.panel = f32[16,256,256]{2,1,0:T(8,128)} async-done(((f32[16,256,256]{2,1,0:T(8,128)}), f32[16,256,256]{2,1,0:T(8,128)}, u32[]{:S(2)}, u32[]{:S(2)}) %all-to-all-start.4) | async-done | bytes 4194336 | tf_op jit(solution)/shard_map/all_to_all | solution.py:676
  177.2 5.0 %basis_rows.1 = f32[4096,256]{1,0:T(8,128)} custom-call(f32[256,256]{1,0:T(8,128)S(1)} %get-tuple-element.69.inverse, f32[16,256,256]{2,1,0:T(8,128)} %all-to-all-done.4.panel), custom_call_target="tpu_custom_call" | custom-call | tf_op jit(solution)/shard_map/basis_rows/pallas_call | solution.py:587
  (65 shorter events, 23.9 us)
Async XLA Ops:
  0.6 10.0 %copy-start.4 = (bf16[8,32,2,8,128]{4,3,2,1,0:T(8,128)(2,1)S(1)}, bf16[8,32,2,8,128]{4,3,2,1,0:T(8,128)(2,1)}, u32[]{:S(2)}) copy-start(bf16[8,32,2,8,128]{4,3,2,1,0:T(8,128)(2,1)} %forcing_from.1) | copy-start | bytes 3145732
  2.8 25.9 %all-to-all-start.1 = ((f32[32,5,2,8,128]{4,3,2,1,0:T(8,128)}), f32[32,5,2,8,128]{4,3,2,1,0:T(8,128)S(1)}, u32[]{:S(2)}, u32[]{:S(2)}) async-start(f32[32,5,2,8,128]{4,3,2,1,0:T(8,128)} %opening_blocks.1), calls=%async_computation.1 | async-start | bytes 2621440 | tf_op jit(solution)/shard_map/all_to_all | solution.py:625
  28.7 21.8 %all-to-all-start = ((f32[32,4,2,8,128]{4,3,2,1,0:T(8,128)}), f32[32,4,2,8,128]{4,3,2,1,0:T(8,128)}, u32[]{:S(2)}, u32[]{:S(2)}) async-start(f32[32,4,2,8,128]{4,3,2,1,0:T(8,128)} %convert_bitcast_fusion), calls=%async_computation | async-start | bytes 2097152 | tf_op jit(solution)/shard_map/all_to_all | solution.py:625
  35.8 9.1 %collective-permute-start.2 = (f32[448,128]{1,0:T(8,128)}, f32[448,128]{1,0:T(8,128)S(1)}, u32[]{:S(2)}, u32[]{:S(2)}) collective-permute-start(f32[448,128]{1,0:T(8,128)} %get-tuple-element.39), channel_id=1, source_target_pairs={{0,4},{4,8},{8,12},{12,0},{1,5},{5,9},{9,13},{13,1},{2,6},{6,10},{... | collective-permute-start | bytes 688136 | tf_op jit(solution)/shard_map/ppermute | solution.py:633
  37.3 7.6 %collective-permute-start.3 = (f32[448,128]{1,0:T(8,128)}, f32[448,128]{1,0:T(8,128)S(1)}, u32[]{:S(2)}, u32[]{:S(2)}) collective-permute-start(f32[448,128]{1,0:T(8,128)} %get-tuple-element.40), channel_id=1, source_target_pairs={{0,12},{4,0},{8,4},{12,8},{1,13},{5,1},{9,5},{13,9},{2,14},{6,2},{... | collective-permute-start | bytes 688136 | tf_op jit(solution)/shard_map/ppermute | solution.py:633
  44.9 0.7 copy-start.1
  45.6 0.9 copy-start.2
  49.5 1.0 copy-start
  50.5 22.8 %all-to-all-start.3 = ((f32[32,4,2,8,128]{4,3,2,1,0:T(8,128)}), f32[32,4,2,8,128]{4,3,2,1,0:T(8,128)S(1)}, u32[]{:S(2)}, u32[]{:S(2)}) async-start(f32[32,4,2,8,128]{4,3,2,1,0:T(8,128)} %bitcast.19), calls=%async_computation.3 | async-start | bytes 2097152 | tf_op jit(solution)/shard_map/all_to_all | solution.py:625
  59.2 24.9 %copy-start.3 = (s32[1,1,2048,1]{2,3,1,0:T(1,128)S(1)}, s32[1,1,2048,1]{2,3,1,0:T(1,128)}, u32[]{:S(2)}) copy-start(s32[1,1,2048,1]{2,3,1,0:T(1,128)} %param.7) | copy-start | bytes 24580
  59.2 8.1 %collective-permute-start = (f32[320,128]{1,0:T(8,128)S(1)}, f32[320,128]{1,0:T(8,128)S(1)}, u32[]{:S(2)}, u32[]{:S(2)}) collective-permute-start(f32[320,128]{1,0:T(8,128)S(1)} %get-tuple-element.37), channel_id=1, source_target_pairs={{0,4},{4,8},{8,12},{12,0},{1,5},{5,9},{9,13},{13,1},{2,6},{6,10},{... | collective-permute-start | bytes 491528 | tf_op jit(solution)/shard_map/ppermute | solution.py:633
  60.8 6.7 %collective-permute-start.1 = (f32[320,128]{1,0:T(8,128)S(1)}, f32[320,128]{1,0:T(8,128)S(1)}, u32[]{:S(2)}, u32[]{:S(2)}) collective-permute-start(f32[320,128]{1,0:T(8,128)S(1)} %get-tuple-element.38), channel_id=1, source_target_pairs={{0,12},{4,0},{8,4},{12,8},{1,13},{5,1},{9,5},{13,9},{2,14},{6,2},{... | collective-permute-start | bytes 491528 | tf_op jit(solution)/shard_map/ppermute | solution.py:633
  62.5 5.6 %collective-permute-start.4 = (f32[8,2,8,128]{3,2,1,0:T(8,128)S(1)}, f32[8,2,8,128]{3,2,1,0:T(8,128)S(1)}, u32[]{:S(2)}, u32[]{:S(2)}) collective-permute-start(f32[8,2,8,128]{3,2,1,0:T(8,128)S(1)} %get-tuple-element.72), channel_id=1, source_target_pairs={{0,4},{4,8},{8,12},{12,0},{1,5},{5,9},{9,13},{13,1},{2,6},{6,10},{... | collective-permute-start | bytes 196616 | tf_op jit(solution)/shard_map/ppermute | solution.py:643
  62.9 5.3 %collective-permute-start.5 = (f32[8,2,8,128]{3,2,1,0:T(8,128)S(1)}, f32[8,2,8,128]{3,2,1,0:T(8,128)S(1)}, u32[]{:S(2)}, u32[]{:S(2)}) collective-permute-start(f32[8,2,8,128]{3,2,1,0:T(8,128)S(1)} %get-tuple-element.71), channel_id=1, source_target_pairs={{0,12},{4,0},{8,4},{12,8},{1,13},{5,1},{9,5},{13,9},{2,14},{6,2},{... | collective-permute-start | bytes 196616 | tf_op jit(solution)/shard_map/ppermute | solution.py:644
  73.3 23.0 %all-to-all-start.2 = ((f32[32,4,2,8,128]{4,3,2,1,0:T(8,128)}), f32[32,4,2,8,128]{4,3,2,1,0:T(8,128)S(1)}, u32[]{:S(2)}, u32[]{:S(2)}) async-start(f32[32,4,2,8,128]{4,3,2,1,0:T(8,128)} %bitcast.5), calls=%async_computation.2 | async-start | bytes 2097152 | tf_op jit(solution)/shard_map/all_to_all | solution.py:625
  81.6 1.3 collective-permute-start.6
  82.9 3.9 %collective-permute-start.7 = (f32[64,128]{1,0:T(8,128)S(1)}, f32[64,128]{1,0:T(8,128)S(1)}, u32[]{:S(2)}, u32[]{:S(2)}) collective-permute-start(f32[64,128]{1,0:T(8,128)S(1)} %add.30), channel_id=1, source_target_pairs={{0,4},{4,0},{8,12},{12,8},{1,5},{5,1},{9,13},{13,9},{2,6},{6,2},{1... | collective-permute-start | bytes 98312 | tf_op jit(solution)/shard_map/ppermute | solution.py:612
  86.8 9.4 %collective-permute-start.8 = (f32[64,128]{1,0:T(8,128)S(1)}, f32[64,128]{1,0:T(8,128)S(1)}, u32[]{:S(2)}, u32[]{:S(2)}) collective-permute-start(f32[64,128]{1,0:T(8,128)S(1)} %add.31), channel_id=1, source_target_pairs={{0,12},{4,8},{8,4},{12,0},{1,13},{5,9},{9,5},{13,1},{2,14},{6,10},... | collective-permute-start | bytes 98312 | tf_op jit(solution)/shard_map/ppermute | solution.py:612
  98.4 1.3 collective-permute-start.9
  99.8 4.3 %collective-permute-start.10 = (f32[64,256]{1,0:T(8,128)S(1)}, f32[64,256]{1,0:T(8,128)S(1)}, u32[]{:S(2)}, u32[]{:S(2)}) collective-permute-start(f32[64,256]{1,0:T(8,128)S(1)} %add.33), channel_id=1, source_target_pairs={{0,4},{4,0},{8,12},{12,8},{1,5},{5,1},{9,13},{13,9},{2,6},{6,2},{1... | collective-permute-start | bytes 196616 | tf_op jit(solution)/shard_map/ppermute | solution.py:612
  104.2 4.7 %collective-permute-start.11 = (f32[64,384]{1,0:T(8,128)S(1)}, f32[64,384]{1,0:T(8,128)S(1)}, u32[]{:S(2)}, u32[]{:S(2)}) collective-permute-start(f32[64,384]{1,0:T(8,128)S(1)} %constant_dynamic-update-slice_fusion), channel_id=1, source_target_pairs={{0,1},{1,0},{2,3},{3,2},{4,5},{5,4},{6,7},{7,6},{8,9},{9,8},{10,11... | collective-permute-start | bytes 294920 | tf_op jit(solution)/shard_map/ppermute | solution.py:612
  108.9 5.6 %collective-permute-start.12 = (f32[64,256]{1,0:T(8,128)S(1)}, f32[64,256]{1,0:T(8,128)S(1)}, u32[]{:S(2)}, u32[]{:S(2)}) collective-permute-start(f32[64,256]{1,0:T(8,128)S(1)} %slice.35), channel_id=1, source_target_pairs={{0,12},{4,8},{8,4},{12,0},{1,13},{5,9},{9,5},{13,1},{2,14},{6,10},... | collective-permute-start | bytes 196616 | tf_op jit(solution)/shard_map/ppermute | solution.py:612
  114.5 4.7 %collective-permute-start.13 = (f32[64,384]{1,0:T(8,128)S(1)}, f32[64,384]{1,0:T(8,128)S(1)}, u32[]{:S(2)}, u32[]{:S(2)}) collective-permute-start(f32[64,384]{1,0:T(8,128)S(1)} %constant_dynamic-update-slice_fusion.2), channel_id=1, source_target_pairs={{0,3},{1,2},{2,1},{3,0},{4,7},{5,6},{6,5},{7,4},{8,11},{9,10},{10,... | collective-permute-start | bytes 294920 | tf_op jit(solution)/shard_map/ppermute | solution.py:612
  119.2 58.0 %all-to-all-start.4 = ((f32[16,256,256]{2,1,0:T(8,128)}), f32[16,256,256]{2,1,0:T(8,128)}, u32[]{:S(2)}, u32[]{:S(2)}) async-start(f32[16,256,256]{2,1,0:T(8,128)} %pack_slots.9), calls=%async_computation.4 | async-start | bytes 8388608 | tf_op jit(solution)/shard_map/all_to_all | solution.py:676
  126.8 4.6 %collective-permute-start.14 = (f32[64,384]{1,0:T(8,128)S(1)}, f32[64,384]{1,0:T(8,128)S(1)}, u32[]{:S(2)}, u32[]{:S(2)}) collective-permute-start(f32[64,384]{1,0:T(8,128)S(1)} %add.37), channel_id=1, source_target_pairs={{0,32},{32,0},{64,96},{96,64},{1,33},{33,1},{65,97},{97,65},{2,34}... | collective-permute-start | bytes 294920 | tf_op jit(solution)/shard_map/ppermute | solution.py:612
  131.4 5.9 %collective-permute-start.15 = (f32[64,384]{1,0:T(8,128)S(1)}, f32[64,384]{1,0:T(8,128)S(1)}, u32[]{:S(2)}, u32[]{:S(2)}) collective-permute-start(f32[64,384]{1,0:T(8,128)S(1)} %add.38), channel_id=1, source_target_pairs={{0,96},{32,64},{64,32},{96,0},{1,97},{33,65},{65,33},{97,1},{2,98}... | collective-permute-start | bytes 294920 | tf_op jit(solution)/shard_map/ppermute | solution.py:612
  137.4 1.6 collective-permute-start.16

commit v8 on v6

--- a/solution.py
+++ b/solution.py
@@ -338,9 +338,10 @@
     )(visc, start, forcing)
 
 
-def prep_kernel(fields, snaps, core, *refs):
+def gram_kernel(fields, snaps, core, *refs):
     rec, before = refs[0], refs[1:-6]
-    whole, high_out, low_out, keep, send, gram = refs[-6:]
+    mine = refs[-6:-3]
+    keep, send, gram = refs[-3:]
     for cell_row in range(16):
         for s in range(snaps):
             for f in range(0, fields, 16):
@@ -348,35 +349,38 @@
                     rec[pl.ds(((f + g) * snaps + s) * 16 + cell_row, 8, stride=snaps * 16), :]
                     for g in (0, 8)
                 ]
-                value = jnp.concatenate(parts, 0)
-                high, low = split(value)
+                rest = jnp.concatenate(parts, 0)
                 at = (slice(s * fields + f, s * fields + f + 16), slice(cell_row * 128, cell_row * 128 + 128))
-                whole[at] = value
-                high_out[at] = high
-                low_out[at] = low
+                for term in mine:
+                    piece = rest.astype(BF16)
+                    term[at] = piece
+                    rest = rest - piece.astype(F32)
     width = fields * snaps
-    mine = whole[...]
-    for c, other in enumerate(before + (whole,)):
-        gram[:, c * width : (c + 1) * width] = exact_dot(mine, other[...], NT)
+    high, middle, low = (ref[...] for ref in mine)
+    others = (before, mine) if before else (mine,)
+    high_of, middle_of, low_of = (jnp.concatenate([group[t][...] for group in others], 0) for t in range(3))
+    by_high = bf_dot(jnp.concatenate([high, middle, low], 0), high_of, NT)
+    by_middle = bf_dot(jnp.concatenate([high, middle], 0), middle_of, NT)
+    small = by_high[2 * width :] + by_middle[width:] + bf_dot(high, low_of, NT)
+    gram[...] = by_high[:width] + (by_high[width : 2 * width] + by_middle[:width] + small)
     half = width // 2
     kept = core[0]
     keep[...] = gram[pl.ds(kept * half, half), :]
     send[...] = gram[pl.ds((1 - kept) * half, half), :]
 
 
-def prep(core, rec, before, fields, snaps):
+def gram_of(core, rec, before, fields, snaps):
     width = fields * snaps
     cells = 2048
-    columns = width * (len(before) + 1)
-    return pl.pallas_call(
-        functools.partial(prep_kernel, fields, snaps),
-        out_shape=(jax.ShapeDtypeStruct((width, cells), F32),)
-        + (jax.ShapeDtypeStruct((width, cells), BF16),) * 2
+    columns = width * (2 if before else 1)
+    return pl.pallas_call(
+        functools.partial(gram_kernel, fields, snaps),
+        out_shape=(jax.ShapeDtypeStruct((width, cells), BF16),) * 3
         + (jax.ShapeDtypeStruct((width // 2, columns), F32),) * 2,
         in_specs=[SMEM] + [VMEM] * (1 + len(before)),
         out_specs=(VMEM,) * 5,
         scratch_shapes=[pltpu.VMEM((width, columns), F32)],
-        compiler_params=params(12),
+        compiler_params=params(16),
         name="gram_blocks",
     )(core, rec, *before)
 
@@ -642,11 +646,12 @@
     hot = rank_hot(owners, owner_count, capacity)
     core = lax.axis_index("core").astype(jnp.int32).reshape(1)
     both = (1, 3)
-    whole_a, high_a, low_a, keep_a, send_a = prep(core, home_one.reshape(-1, lanes), (), fields, HALF)
+    *terms_a, keep_a, send_a = gram_of(core, home_one.reshape(-1, lanes), (), fields, HALF)
+    high_a, low_a = terms_a[:2]
     part_a = summed(keep_a + swapped(send_a), "x", both)
     slots = pack(owners, hot, high_a, low_a, owner_count, 0)
     home_two, slots, part_a = lax.optimization_barrier((home_two, slots, part_a))
-    _, high_b, low_b, keep_b, send_b = prep(core, home_two.reshape(-1, lanes), (whole_a,), fields, HALF)
+    high_b, low_b, _, keep_b, send_b = gram_of(core, home_two.reshape(-1, lanes), terms_a, fields, HALF)
     quarters = 4
 
     def packed(slots, part, *values):
@@ -654,17 +659,17 @@
         return lax.optimization_barrier((slots,) + values)
 
     part_b = summed(keep_b + swapped(send_b), "x", (1,))
-    slots, part_b = packed(slots, 0, part_b)
-    part_b = summed(part_b, "x", (3,))
-    slots, part_b, part_a = packed(slots, 1, part_b, part_a)
+    slots, part_a, part_b = packed(slots, 0, part_a, part_b)
     part = summed(jnp.concatenate([part_a, part_b], 1), "z", (1,))
-    slots, part = packed(slots, 2, part)
-    part = summed(part, "z", (3,))
+    slots, part = packed(slots, 1, part)
+    width = fields * HALF
+    part_a, part_b = part[:, :width], summed(part[:, width:], "x", (3,))
+    slots, part_a, part_b = packed(slots, 2, part_a, part_b)
+    part = summed(jnp.concatenate([part_a, part_b], 1), "z", (3,))
     slots, part = packed(slots, 3, part)
     panel = lax.all_to_all(slots, ("x", "z"), split_axis=0, concat_axis=0, tiled=True)
     part = summed(part, "y", both)
     other = swapped(part)
-    width = fields * HALF
     lead, lead_inv = factor_lead(core, part[:, :width], other[:, :width])
     r_factor, inverse = factor_trail(core, part[:, width:], other[:, width:], lead, lead_inv)
     basis = basis_of(inverse, panel)

time: 184 us -> 184 us (level)
  waiting for transfers between devices: 62.2 us -> 56.9 us
  starting transfers between devices: 52.2 us -> 56.2 us
    ppermute x8, starting transfers between devices: 6.74 us -> 10.6 us  [summed(): lax.ppermute(value, axis, [(i, i ^ mask) for i in range(size)])]
    ppermute x8, waiting for transfers between devices: 18.9 us -> 16.9 us  [summed(): lax.ppermute(value, axis, [(i, i ^ mask) for i in range(size)])]
    unnamed x11 -> x16, local copies, waits for them, and re-layouts: 2.61 us -> 4.42 us
  transfers between devices with their start and end apart: 22 -> 22, of which waited for: 19 -> 18; matrix products, arithmetic and copies ran while one was open for 1% -> 1% of each run, Pallas kernels for 29% -> 29%
where the time goes in v8:
time: 184 us; the launch traced here: 183 us
  Pallas kernels  62.7 us (34%)
  waiting for transfers between devices  56.9 us (31%)
  starting transfers between devices  56.2 us (31%)
  local copies, waits for them, and re-layouts  5.19 us (3%)
    all_to_all x4, starting transfers between devices, swap(): return lax.all_to_all(value, plane, split_axis=0, concat_axis=0, tiled=True)  28.3 us
    all_to_all x4, waiting for transfers between devices, swap(): return lax.all_to_all(value, plane, split_axis=0, concat_axis=0, tiled=True)  17.7 us
    ppermute x8, waiting for transfers between devices, summed(): lax.ppermute(value, axis, [(i, i ^ mask) for i in range(size)])  16.9 us
    pallas_call x5, Pallas kernels, pack(): pl.pallas_call(functools.partial(pack_kernel, first), grid=(groups,), out...  14.8 us
    pallas_call x1, Pallas kernels, factor_trail(): pl.pallas_call(trail_kernel, out_shape=(jax.ShapeDtypeStruct((2 * order,...  14 us
    pallas_call x1, Pallas kernels, factor_lead(): pl.pallas_call(lead_kernel, out_shape=(jax.ShapeDtypeStruct((order, order...  12.4 us
    all_to_all x1, waiting for transfers between devices, on_device(): lax.all_to_all(slots, ('x', 'z'), split_axis=0, concat_axis=0, tiled=True)  11.8 us
    ppermute x8, starting transfers between devices, summed(): lax.ppermute(value, axis, [(i, i ^ mask) for i in range(size)])  10.6 us
  transfers between devices with their start and end apart: 22, of which 18 were waited for; matrix products, arithmetic and copies ran while one was open for 1% of the time, Pallas kernels for 29%

profile of v8, /device:TPU:64, one launch (start us, length us, event | category | flops | bytes accessed | tf_op | source)
XLA Modules:
  0.0 183.1 jit_solution(12143187101532068851)
XLA Ops:
  0.6 2.2 %opening_blocks.1 = f32[32,5,2,8,128]{4,3,2,1,0:T(8,128)} custom-call(f32[2,8,128]{2,1,0:T(8,128)} %visc_from.1, f32[32,2,8,128]{3,2,1,0:T(8,128)} %start_from.1, bf16[8,32,2,8,128]{4,3,2,1,0:T(8,128)(2,1)} %forcing_from.1), custom_call_target="tpu_custom_call" | custom-call | tf_op jit(solution)/shard_map/opening_blocks/pallas_call | solution.py:323
  2.8 7.8 %all-to-all-start.1 = ((f32[32,5,2,8,128]{4,3,2,1,0:T(8,128)}), f32[32,5,2,8,128]{4,3,2,1,0:T(8,128)S(1)}, u32[]{:S(2)}, u32[]{:S(2)}) async-start(f32[32,5,2,8,128]{4,3,2,1,0:T(8,128)} %opening_blocks.1), calls=%async_computation.1 | async-start | bytes 2621440 | tf_op jit(solution)/shard_map/all_to_all | solution.py:620
  11.7 17.1 %all-to-all-done.1 = f32[32,5,2,8,128]{4,3,2,1,0:T(8,128)S(1)} async-done(((f32[32,5,2,8,128]{4,3,2,1,0:T(8,128)}), f32[32,5,2,8,128]{4,3,2,1,0:T(8,128)S(1)}, u32[]{:S(2)}, u32[]{:S(2)}) %all-to-all-start.1) | async-done | bytes 1310752 | tf_op jit(solution)/shard_map/all_to_all | solution.py:620
  28.7 6.2 %all-to-all-start = ((f32[32,4,2,8,128]{4,3,2,1,0:T(8,128)}), f32[32,4,2,8,128]{4,3,2,1,0:T(8,128)}, u32[]{:S(2)}, u32[]{:S(2)}) async-start(f32[32,4,2,8,128]{4,3,2,1,0:T(8,128)} %convert_bitcast_fusion), calls=%async_computation | async-start | bytes 2097152 | tf_op jit(solution)/shard_map/all_to_all | solution.py:620
  37.3 1.7 collective-permute-start.3
  39.5 5.4 %collective-permute-done.2.low = f32[448,128]{1,0:T(8,128)S(1)} collective-permute-done((f32[448,128]{1,0:T(8,128)}, f32[448,128]{1,0:T(8,128)S(1)}, u32[]{:S(2)}, u32[]{:S(2)}) %collective-permute-start.2) | collective-permute-done | bytes 229408 | tf_op jit(solution)/shard_map/ppermute | solution.py:628
  46.5 2.9 %diffuse_first.1 = (f32[2048,128]{1,0:T(8,128)S(1)}, f32[32,2,8,128]{3,2,1,0:T(8,128)S(1)}, f32[20,2,8,128]{3,2,1,0:T(8,128)S(1)}) custom-call(s32[2]{0:T(128)S(1)} %add_convert_fusion.around, f32[2560,128]{1,0:T(8,128)S(1)} %bitcast.16, f32[448,128]{1,0:T(8,128)S(1)} %collective-permute-done.2.low, f32[448,128]{1,0:T(8,128)S(1)} %copy-done.4, ...), custom_call_target="tpu_custom_call" | custom-call | tf_op jit(solution)/shard_map/diffuse_first/pallas_call | solution.py:240
  50.5 7.4 %all-to-all-start.3 = ((f32[32,4,2,8,128]{4,3,2,1,0:T(8,128)}), f32[32,4,2,8,128]{4,3,2,1,0:T(8,128)S(1)}, u32[]{:S(2)}, u32[]{:S(2)}) async-start(f32[32,4,2,8,128]{4,3,2,1,0:T(8,128)} %bitcast.19), calls=%async_computation.3 | async-start | bytes 2097152 | tf_op jit(solution)/shard_map/all_to_all | solution.py:620
  59.2 1.6 collective-permute-start
  60.8 1.7 collective-permute-start.1
  62.9 3.0 %collective-permute-start.5 = (f32[8,2,8,128]{3,2,1,0:T(8,128)S(1)}, f32[8,2,8,128]{3,2,1,0:T(8,128)S(1)}, u32[]{:S(2)}, u32[]{:S(2)}) collective-permute-start(f32[8,2,8,128]{3,2,1,0:T(8,128)S(1)} %get-tuple-element.69), channel_id=1, source_target_pairs={{0,12},{4,0},{8,4},{12,8},{1,13},{5,1},{9,5},{13,9},{2,14},{6,2},{... | collective-permute-start | bytes 196616 | tf_op jit(solution)/shard_map/ppermute | solution.py:639
  68.2 4.6 %diffuse_second.1 = f32[2048,128]{1,0:T(8,128)} custom-call(f32[2048,128]{1,0:T(8,128)} %bitcast.1.main, f32[320,128]{1,0:T(8,128)S(1)} %collective-permute-done.low, f32[320,128]{1,0:T(8,128)S(1)} %collective-permute-done.1.high, f32[32,2,8,128]{3,2,1,0:T(8,128)S(1)} %get-tuple-element.40.start, f32[8,2,8,128]{3,2,1,0:T(8,128)S(1)} %collective-permute-done.4.start_low, ...), custom_call_target="tpu_custom_call" | custom-call | tf_op jit(solution)/shard_map/diffuse_second/pallas_call | solution.py:257
  73.3 6.8 %all-to-all-start.2 = ((f32[32,4,2,8,128]{4,3,2,1,0:T(8,128)}), f32[32,4,2,8,128]{4,3,2,1,0:T(8,128)S(1)}, u32[]{:S(2)}, u32[]{:S(2)}) async-start(f32[32,4,2,8,128]{4,3,2,1,0:T(8,128)} %bitcast.5), calls=%async_computation.2 | async-start | bytes 2097152 | tf_op jit(solution)/shard_map/all_to_all | solution.py:620
  85.5 1.9 %collective-permute-done.7 = f32[64,128]{1,0:T(8,128)S(1)} collective-permute-done((f32[64,128]{1,0:T(8,128)S(1)}, f32[64,128]{1,0:T(8,128)S(1)}, u32[]{:S(2)}, u32[]{:S(2)}) %collective-permute-start.7) | collective-permute-done | bytes 32800 | tf_op jit(solution)/shard_map/ppermute | solution.py:607
  87.4 3.2 %collective-permute-start.8 = (f32[64,128]{1,0:T(8,128)S(1)}, f32[64,128]{1,0:T(8,128)S(1)}, u32[]{:S(2)}, u32[]{:S(2)}) collective-permute-start(f32[64,128]{1,0:T(8,128)S(1)} %add.31), channel_id=1, source_target_pairs={{0,12},{4,8},{8,4},{12,0},{1,13},{5,9},{9,5},{13,1},{2,14},{6,10},... | collective-permute-start | bytes 98312 | tf_op jit(solution)/shard_map/ppermute | solution.py:607
  90.6 6.2 %pack_slots.5.refs_0_ = f32[16,256,256]{2,1,0:T(8,128)} custom-call(s32[16,128]{1,0:T(8,128)S(1)} %bitcast.21, bf16[256,2048]{1,0:T(8,128)(2,1)S(1)} %slot_ranks.1.hot, bf16[128,2048]{1,0:T(8,128)(2,1)S(1)} %get-tuple-element.43.high.refs_1_, bf16[128,2048]{1,0:T(8,128)(2,1)S(1)} %get-tuple-element.44.low.refs_2_), custom_call_target="tpu_custom_call" | custom-call | flops 4294967296 | bytes 2097152 | tf_op jit(solution)/shard_map/pack_slots/pallas_call | solution.py:451
  97.9 2.2 %gram_blocks.3 = (bf16[128,2048]{1,0:T(8,128)(2,1)S(1)}, bf16[128,2048]{1,0:T(8,128)(2,1)S(1)}, bf16[128,2048]{1,0:T(8,128)(2,1)}, f32[64,256]{1,0:T(8,128)S(1)}, f32[64,256]{1,0:T(8,128)S(1)}) custom-call(s32[1]{0:T(128)} %bitcast.7.core, f32[2048,128]{1,0:T(8,128)S(1)} %bitcast.17, bf16[128,2048]{1,0:T(8,128)(2,1)S(1)} %get-tuple-element.43.high.refs_1_, ...), custom_call_target="tpu_custom_call" | custom-call | tf_op jit(solution)/shard_map/gram_blocks/pallas_call | solution.py:376
  101.4 2.2 %pack_slots.6.refs_0_ = f32[16,256,256]{2,1,0:T(8,128)} custom-call(s32[16,128]{1,0:T(8,128)S(1)} %bitcast.22, bf16[256,2048]{1,0:T(8,128)(2,1)S(1)} %slot_ranks.1.hot, bf16[128,2048]{1,0:T(8,128)(2,1)S(1)} %get-tuple-element.49.high, bf16[128,2048]{1,0:T(8,128)(2,1)S(1)} %get-tuple-element.50.low, ...), custom_call_target="tpu_custom_call", output_to_operand_aliasing={{}: (4, {})} | custom-call | flops 1073741824 | bytes 524288 | tf_op jit(solution)/shard_map/pack_slots/pallas_call | solution.py:451
  103.6 2.1 %collective-permute-done.10 = f32[64,256]{1,0:T(8,128)S(1)} collective-permute-done((f32[64,256]{1,0:T(8,128)S(1)}, f32[64,256]{1,0:T(8,128)S(1)}, u32[]{:S(2)}, u32[]{:S(2)}) %collective-permute-start.10) | collective-permute-done | bytes 65568 | tf_op jit(solution)/shard_map/ppermute | solution.py:607
  107.0 2.1 %pack_slots.7.refs_0_ = f32[16,256,256]{2,1,0:T(8,128)} custom-call(s32[16,128]{1,0:T(8,128)S(1)} %bitcast.23, bf16[256,2048]{1,0:T(8,128)(2,1)S(1)} %slot_ranks.1.hot, bf16[128,2048]{1,0:T(8,128)(2,1)S(1)} %get-tuple-element.49.high, bf16[128,2048]{1,0:T(8,128)(2,1)S(1)} %get-tuple-element.50.low, ...), custom_call_target="tpu_custom_call", output_to_operand_aliasing={{}: (4, {})} | custom-call | flops 1073741824 | bytes 524288 | tf_op jit(solution)/shard_map/pack_slots/pallas_call | solution.py:451
  110.5 1.9 %collective-permute-start.12 = (f32[64,256]{1,0:T(8,128)S(1)}, f32[64,256]{1,0:T(8,128)S(1)}, u32[]{:S(2)}, u32[]{:S(2)}) collective-permute-start(f32[64,256]{1,0:T(8,128)S(1)} %slice.35), channel_id=1, source_target_pairs={{0,12},{4,8},{8,4},{12,0},{1,13},{5,9},{9,5},{13,1},{2,14},{6,10},... | collective-permute-start | bytes 196616 | tf_op jit(solution)/shard_map/ppermute | solution.py:607
  112.3 2.1 %pack_slots.8.refs_0_ = f32[16,256,256]{2,1,0:T(8,128)} custom-call(s32[16,128]{1,0:T(8,128)S(1)} %bitcast.24, bf16[256,2048]{1,0:T(8,128)(2,1)S(1)} %slot_ranks.1.hot, bf16[128,2048]{1,0:T(8,128)(2,1)S(1)} %get-tuple-element.49.high, bf16[128,2048]{1,0:T(8,128)(2,1)S(1)} %get-tuple-element.50.low, ...), custom_call_target="tpu_custom_call", output_to_operand_aliasing={{}: (4, {})} | custom-call | flops 1073741824 | bytes 524288 | tf_op jit(solution)/shard_map/pack_slots/pallas_call | solution.py:451
  116.7 2.1 %pack_slots.9 = f32[16,256,256]{2,1,0:T(8,128)} custom-call(s32[16,128]{1,0:T(8,128)S(1)} %bitcast.25, bf16[256,2048]{1,0:T(8,128)(2,1)S(1)} %slot_ranks.1.hot, bf16[128,2048]{1,0:T(8,128)(2,1)S(1)} %get-tuple-element.49.high, bf16[128,2048]{1,0:T(8,128)(2,1)S(1)} %get-tuple-element.50.low, ...), custom_call_target="tpu_custom_call", output_to_operand_aliasing={{}: (4, {})} | custom-call | flops 1073741824 | bytes 524288 | tf_op jit(solution)/shard_map/pack_slots/pallas_call | solution.py:451
  118.8 1.9 %collective-permute-done.13 = f32[64,384]{1,0:T(8,128)S(1)} collective-permute-done((f32[64,384]{1,0:T(8,128)S(1)}, f32[64,384]{1,0:T(8,128)S(1)}, u32[]{:S(2)}, u32[]{:S(2)}) %collective-permute-start.13) | collective-permute-done | bytes 98336 | tf_op jit(solution)/shard_map/ppermute | solution.py:607
  120.8 7.0 %all-to-all-start.4 = ((f32[16,256,256]{2,1,0:T(8,128)}), f32[16,256,256]{2,1,0:T(8,128)}, u32[]{:S(2)}, u32[]{:S(2)}) async-start(f32[16,256,256]{2,1,0:T(8,128)} %pack_slots.9), calls=%async_computation.4 | async-start | bytes 8388608 | tf_op jit(solution)/shard_map/all_to_all | solution.py:670
  128.3 4.1 %collective-permute-done.14 = f32[64,384]{1,0:T(8,128)S(1)} collective-permute-done((f32[64,384]{1,0:T(8,128)S(1)}, f32[64,384]{1,0:T(8,128)S(1)}, u32[]{:S(2)}, u32[]{:S(2)}) %collective-permute-start.14) | collective-permute-done | bytes 98336 | tf_op jit(solution)/shard_map/ppermute | solution.py:607
  132.4 1.8 %collective-permute-start.15 = (f32[64,384]{1,0:T(8,128)S(1)}, f32[64,384]{1,0:T(8,128)S(1)}, u32[]{:S(2)}, u32[]{:S(2)}) collective-permute-start(f32[64,384]{1,0:T(8,128)S(1)} %add.38), channel_id=1, source_target_pairs={{0,96},{32,64},{64,32},{96,0},{1,97},{33,65},{65,33},{97,1},{2,98}... | collective-permute-start | bytes 294920 | tf_op jit(solution)/shard_map/ppermute | solution.py:607
  134.3 4.1 %collective-permute-done.15 = f32[64,384]{1,0:T(8,128)S(1)} collective-permute-done((f32[64,384]{1,0:T(8,128)S(1)}, f32[64,384]{1,0:T(8,128)S(1)}, u32[]{:S(2)}, u32[]{:S(2)}) %collective-permute-start.15) | collective-permute-done | bytes 98336 | tf_op jit(solution)/shard_map/ppermute | solution.py:607
  139.9 12.4 %factor_lead.1 = (f32[128,128]{1,0:T(8,128)S(1)}, f32[128,128]{1,0:T(8,128)S(1)}) custom-call(s32[1]{0:T(128)} %bitcast.7.core, f32[64,128]{1,0:T(8,128)S(1)} %slice.42.own, f32[64,128]{1,0:T(8,128)S(1)} %slice.43.other), custom_call_target="tpu_custom_call" | custom-call | tf_op jit(solution)/shard_map/factor_lead/pallas_call | solution.py:543
  152.4 14.0 %factor_trail.1 = (f32[256,256]{1,0:T(8,128)}, f32[256,256]{1,0:T(8,128)S(1)}) custom-call(s32[1]{0:T(128)} %bitcast.7.core, f32[64,256]{1,0:T(8,128)S(1)} %slice.40.own_half, f32[64,256]{1,0:T(8,128)S(1)} %slice.41.other_half, f32[128,128]{1,0:T(8,128)S(1)} %get-tuple-element.64.lead, f32[128,128]{1,0:T(8,128)S(1)} %get-tuple-element.65.lead_inv), custom_call_target="tpu_custom_call" | custom-call | tf_op jit(solution)/shard_map/factor_trail/pallas_call | solution.py:556
  166.4 11.8 %all-to-all-done.4.panel = f32[16,256,256]{2,1,0:T(8,128)} async-done(((f32[16,256,256]{2,1,0:T(8,128)}), f32[16,256,256]{2,1,0:T(8,128)}, u32[]{:S(2)}, u32[]{:S(2)}) %all-to-all-start.4) | async-done | bytes 4194336 | tf_op jit(solution)/shard_map/all_to_all | solution.py:670
  178.2 5.0 %basis_rows.1 = f32[4096,256]{1,0:T(8,128)} custom-call(f32[256,256]{1,0:T(8,128)S(1)} %get-tuple-element.67.inverse, f32[16,256,256]{2,1,0:T(8,128)} %all-to-all-done.4.panel), custom_call_target="tpu_custom_call" | custom-call | tf_op jit(solution)/shard_map/basis_rows/pallas_call | solution.py:582
  (67 shorter events, 25.8 us)
Async XLA Ops:
  0.6 10.0 %copy-start.6 = (bf16[8,32,2,8,128]{4,3,2,1,0:T(8,128)(2,1)S(1)}, bf16[8,32,2,8,128]{4,3,2,1,0:T(8,128)(2,1)}, u32[]{:S(2)}) copy-start(bf16[8,32,2,8,128]{4,3,2,1,0:T(8,128)(2,1)} %forcing_from.1) | copy-start | bytes 3145732
  2.8 25.9 %all-to-all-start.1 = ((f32[32,5,2,8,128]{4,3,2,1,0:T(8,128)}), f32[32,5,2,8,128]{4,3,2,1,0:T(8,128)S(1)}, u32[]{:S(2)}, u32[]{:S(2)}) async-start(f32[32,5,2,8,128]{4,3,2,1,0:T(8,128)} %opening_blocks.1), calls=%async_computation.1 | async-start | bytes 2621440 | tf_op jit(solution)/shard_map/all_to_all | solution.py:620
  28.7 21.8 %all-to-all-start = ((f32[32,4,2,8,128]{4,3,2,1,0:T(8,128)}), f32[32,4,2,8,128]{4,3,2,1,0:T(8,128)}, u32[]{:S(2)}, u32[]{:S(2)}) async-start(f32[32,4,2,8,128]{4,3,2,1,0:T(8,128)} %convert_bitcast_fusion), calls=%async_computation | async-start | bytes 2097152 | tf_op jit(solution)/shard_map/all_to_all | solution.py:620
  35.8 9.1 %collective-permute-start.2 = (f32[448,128]{1,0:T(8,128)}, f32[448,128]{1,0:T(8,128)S(1)}, u32[]{:S(2)}, u32[]{:S(2)}) collective-permute-start(f32[448,128]{1,0:T(8,128)} %get-tuple-element.38), channel_id=1, source_target_pairs={{0,4},{4,8},{8,12},{12,0},{1,5},{5,9},{9,13},{13,1},{2,6},{6,10},{... | collective-permute-start | bytes 688136 | tf_op jit(solution)/shard_map/ppermute | solution.py:628
  37.3 7.6 %collective-permute-start.3 = (f32[448,128]{1,0:T(8,128)}, f32[448,128]{1,0:T(8,128)S(1)}, u32[]{:S(2)}, u32[]{:S(2)}) collective-permute-start(f32[448,128]{1,0:T(8,128)} %get-tuple-element.39), channel_id=1, source_target_pairs={{0,12},{4,0},{8,4},{12,8},{1,13},{5,1},{9,5},{13,9},{2,14},{6,2},{... | collective-permute-start | bytes 688136 | tf_op jit(solution)/shard_map/ppermute | solution.py:628
  44.9 0.7 copy-start.3
  45.6 0.9 copy-start.4
  49.5 1.0 copy-start
  50.5 22.8 %all-to-all-start.3 = ((f32[32,4,2,8,128]{4,3,2,1,0:T(8,128)}), f32[32,4,2,8,128]{4,3,2,1,0:T(8,128)S(1)}, u32[]{:S(2)}, u32[]{:S(2)}) async-start(f32[32,4,2,8,128]{4,3,2,1,0:T(8,128)} %bitcast.19), calls=%async_computation.3 | async-start | bytes 2097152 | tf_op jit(solution)/shard_map/all_to_all | solution.py:620
  59.2 25.5 %copy-start.5 = (s32[1,1,2048,1]{2,3,1,0:T(1,128)S(1)}, s32[1,1,2048,1]{2,3,1,0:T(1,128)}, u32[]{:S(2)}) copy-start(s32[1,1,2048,1]{2,3,1,0:T(1,128)} %param.7) | copy-start | bytes 24580
  59.2 8.1 %collective-permute-start = (f32[320,128]{1,0:T(8,128)S(1)}, f32[320,128]{1,0:T(8,128)S(1)}, u32[]{:S(2)}, u32[]{:S(2)}) collective-permute-start(f32[320,128]{1,0:T(8,128)S(1)} %get-tuple-element.36), channel_id=1, source_target_pairs={{0,4},{4,8},{8,12},{12,0},{1,5},{5,9},{9,13},{13,1},{2,6},{6,10},{... | collective-permute-start | bytes 491528 | tf_op jit(solution)/shard_map/ppermute | solution.py:628
  60.8 6.7 %collective-permute-start.1 = (f32[320,128]{1,0:T(8,128)S(1)}, f32[320,128]{1,0:T(8,128)S(1)}, u32[]{:S(2)}, u32[]{:S(2)}) collective-permute-start(f32[320,128]{1,0:T(8,128)S(1)} %get-tuple-element.37), channel_id=1, source_target_pairs={{0,12},{4,0},{8,4},{12,8},{1,13},{5,1},{9,5},{13,9},{2,14},{6,2},{... | collective-permute-start | bytes 491528 | tf_op jit(solution)/shard_map/ppermute | solution.py:628
  62.5 5.6 %collective-permute-start.4 = (f32[8,2,8,128]{3,2,1,0:T(8,128)S(1)}, f32[8,2,8,128]{3,2,1,0:T(8,128)S(1)}, u32[]{:S(2)}, u32[]{:S(2)}) collective-permute-start(f32[8,2,8,128]{3,2,1,0:T(8,128)S(1)} %get-tuple-element.70), channel_id=1, source_target_pairs={{0,4},{4,8},{8,12},{12,0},{1,5},{5,9},{9,13},{13,1},{2,6},{6,10},{... | collective-permute-start | bytes 196616 | tf_op jit(solution)/shard_map/ppermute | solution.py:638
  62.9 5.3 %collective-permute-start.5 = (f32[8,2,8,128]{3,2,1,0:T(8,128)S(1)}, f32[8,2,8,128]{3,2,1,0:T(8,128)S(1)}, u32[]{:S(2)}, u32[]{:S(2)}) collective-permute-start(f32[8,2,8,128]{3,2,1,0:T(8,128)S(1)} %get-tuple-element.69), channel_id=1, source_target_pairs={{0,12},{4,0},{8,4},{12,8},{1,13},{5,1},{9,5},{13,9},{2,14},{6,2},{... | collective-permute-start | bytes 196616 | tf_op jit(solution)/shard_map/ppermute | solution.py:639
  73.3 23.6 %all-to-all-start.2 = ((f32[32,4,2,8,128]{4,3,2,1,0:T(8,128)}), f32[32,4,2,8,128]{4,3,2,1,0:T(8,128)S(1)}, u32[]{:S(2)}, u32[]{:S(2)}) async-start(f32[32,4,2,8,128]{4,3,2,1,0:T(8,128)} %bitcast.5), calls=%async_computation.2 | async-start | bytes 2097152 | tf_op jit(solution)/shard_map/all_to_all | solution.py:620
  81.5 0.8 copy-start.1
  82.3 1.2 collective-permute-start.6
  83.5 3.9 %collective-permute-start.7 = (f32[64,128]{1,0:T(8,128)S(1)}, f32[64,128]{1,0:T(8,128)S(1)}, u32[]{:S(2)}, u32[]{:S(2)}) collective-permute-start(f32[64,128]{1,0:T(8,128)S(1)} %add.30), channel_id=1, source_target_pairs={{0,4},{4,0},{8,12},{12,8},{1,5},{5,1},{9,13},{13,9},{2,6},{6,2},{1... | collective-permute-start | bytes 98312 | tf_op jit(solution)/shard_map/ppermute | solution.py:607
  87.4 9.4 %collective-permute-start.8 = (f32[64,128]{1,0:T(8,128)S(1)}, f32[64,128]{1,0:T(8,128)S(1)}, u32[]{:S(2)}, u32[]{:S(2)}) collective-permute-start(f32[64,128]{1,0:T(8,128)S(1)} %add.31), channel_id=1, source_target_pairs={{0,12},{4,8},{8,4},{12,0},{1,13},{5,9},{9,5},{13,1},{2,14},{6,10},... | collective-permute-start | bytes 98312 | tf_op jit(solution)/shard_map/ppermute | solution.py:607
  96.8 1.0 copy-start.2
  100.1 1.3 collective-permute-start.9
  101.3 4.3 %collective-permute-start.10 = (f32[64,256]{1,0:T(8,128)S(1)}, f32[64,256]{1,0:T(8,128)S(1)}, u32[]{:S(2)}, u32[]{:S(2)}) collective-permute-start(f32[64,256]{1,0:T(8,128)S(1)} %add.33), channel_id=1, source_target_pairs={{0,4},{4,0},{8,12},{12,8},{1,5},{5,1},{9,13},{13,9},{2,6},{6,2},{1... | collective-permute-start | bytes 196616 | tf_op jit(solution)/shard_map/ppermute | solution.py:607
  105.7 4.7 %collective-permute-start.11 = (f32[64,384]{1,0:T(8,128)S(1)}, f32[64,384]{1,0:T(8,128)S(1)}, u32[]{:S(2)}, u32[]{:S(2)}) collective-permute-start(f32[64,384]{1,0:T(8,128)S(1)} %constant_dynamic-update-slice_fusion), channel_id=1, source_target_pairs={{0,1},{1,0},{2,3},{3,2},{4,5},{5,4},{6,7},{7,6},{8,9},{9,8},{10,11... | collective-permute-start | bytes 294920 | tf_op jit(solution)/shard_map/ppermute | solution.py:607
  110.5 5.6 %collective-permute-start.12 = (f32[64,256]{1,0:T(8,128)S(1)}, f32[64,256]{1,0:T(8,128)S(1)}, u32[]{:S(2)}, u32[]{:S(2)}) collective-permute-start(f32[64,256]{1,0:T(8,128)S(1)} %slice.35), channel_id=1, source_target_pairs={{0,12},{4,8},{8,4},{12,0},{1,13},{5,9},{9,5},{13,1},{2,14},{6,10},... | collective-permute-start | bytes 196616 | tf_op jit(solution)/shard_map/ppermute | solution.py:607
  116.1 4.7 %collective-permute-start.13 = (f32[64,384]{1,0:T(8,128)S(1)}, f32[64,384]{1,0:T(8,128)S(1)}, u32[]{:S(2)}, u32[]{:S(2)}) collective-permute-start(f32[64,384]{1,0:T(8,128)S(1)} %constant_dynamic-update-slice_fusion.2), channel_id=1, source_target_pairs={{0,3},{1,2},{2,1},{3,0},{4,7},{5,6},{6,5},{7,4},{8,11},{9,10},{10,... | collective-permute-start | bytes 294920 | tf_op jit(solution)/shard_map/ppermute | solution.py:607
  120.8 57.4 %all-to-all-start.4 = ((f32[16,256,256]{2,1,0:T(8,128)}), f32[16,256,256]{2,1,0:T(8,128)}, u32[]{:S(2)}, u32[]{:S(2)}) async-start(f32[16,256,256]{2,1,0:T(8,128)} %pack_slots.9), calls=%async_computation.4 | async-start | bytes 8388608 | tf_op jit(solution)/shard_map/all_to_all | solution.py:670
  127.8 4.6 %collective-permute-start.14 = (f32[64,384]{1,0:T(8,128)S(1)}, f32[64,384]{1,0:T(8,128)S(1)}, u32[]{:S(2)}, u32[]{:S(2)}) collective-permute-start(f32[64,384]{1,0:T(8,128)S(1)} %add.37), channel_id=1, source_target_pairs={{0,32},{32,0},{64,96},{96,64},{1,33},{33,1},{65,97},{97,65},{2,34}... | collective-permute-start | bytes 294920 | tf_op jit(solution)/shard_map/ppermute | solution.py:607
  132.4 5.9 %collective-permute-start.15 = (f32[64,384]{1,0:T(8,128)S(1)}, f32[64,384]{1,0:T(8,128)S(1)}, u32[]{:S(2)}, u32[]{:S(2)}) collective-permute-start(f32[64,384]{1,0:T(8,128)S(1)} %add.38), channel_id=1, source_target_pairs={{0,96},{32,64},{64,32},{96,0},{1,97},{33,65},{65,33},{97,1},{2,98}... | collective-permute-start | bytes 294920 | tf_op jit(solution)/shard_map/ppermute | solution.py:607
  138.3 1.6 collective-permute-start.16
